TPU v7x, 32 devices: a whole 2x2x4 slice. The times are simulated.
32 devices in a mesh: members: 2 (over x), lat: 16 (over z, y, core).
Axes of the slice: x: 2, y: 2, z: 4, core: 2. Of those that a mesh axis runs over, the one named last changes fastest.
Arguments:
- tracer: float32 [16, 128, 1440], P(None, ('members', 'lat')), parts along dimension 1, may hold values from -6 to 6
- diffusivity: float32 [64, 1440], P('lat'), may hold values from 0.02 to 0.18
- direction: float32 [128, 1440], P(('members', 'lat')), parts along dimension 0, may hold values from -0.015625 to 0.015625
- column_depth: int32 [64, 1440], P('lat'), may hold values from 0 to 16
- density_class: int32 [16, 128, 1440], P(None, ('members', 'lat')), parts along dimension 1, may hold values from 0 to 71
- band_of_row: int32 [64], P('lat'), may hold values from 0 to 31, as said below
- weights: float32 [32, 72], replicated, may hold values from 0.02 to 0.2
Outputs:
- binned: float32 [64, 72], P(('members', 'lat')), parts along dimension 0
- gradient: float32 [128, 1440], P(('members', 'lat')), parts along dimension 0
There are 2 independent parts, one for each index of `members`. A program takes and returns all parts, laid end to end along the dimension named above; an argument that names none is the same for every part. Nothing has to cross between parts.
Inputs may be any that keep to these rules, and one draw needn't show every extreme that they name: `band_of_row`: rows come in runs of 2 consecutive latitudes that share one band number, and each band number belongs to exactly one run.
All inputs are finite; a program needn't handle non-finite values.
Results may differ from a plain program's by a relative error of at most 0.00013.
Values sent between devices are 32-bit elements; how exact they have to be, the bound alone decides.
No kernel may reach another device: no remote copies, remote signals or barrier semaphores. Data moves between devices by JAX's collectives and lax.ppermute only.
A program may use at most 64 MiB of HBM per device.

v0:
```python
import jax
import jax.numpy as jnp
from jax import lax
from jax.sharding import PartitionSpec as P

STEPS = 3


vertical_mix = 0.05
level_block = 10


def with_halo(block, sides, width):
    for axis, dim in sides:
        count = lax.axis_size(axis)
        forward = [(i, i + 1) for i in range(count - 1)]
        backward = [(target, source) for source, target in forward]
        low = lax.ppermute(
            lax.slice_in_dim(block, block.shape[dim] - width, None, axis=dim), axis, forward
        )
        high = lax.ppermute(lax.slice_in_dim(block, 0, width, axis=dim), axis, backward)
        block = jnp.concatenate([low, block, high], axis=dim)
    return block


def lateral(tracer_field, mixing, wetness):
    east_mix = 0.5 * (mixing + jnp.roll(mixing, -1, axis=-1))
    east_flux = (
        east_mix
        * wetness
        * jnp.roll(wetness, -1, axis=-1)
        * (jnp.roll(tracer_field, -1, axis=-1) - tracer_field)
    )
    east_part = east_flux - jnp.roll(east_flux, 1, axis=-1)
    north_mix = 0.5 * (mixing[:-1] + mixing[1:])
    north_flux = (
        north_mix * wetness[:, :-1] * wetness[:, 1:] * (tracer_field[:, 1:] - tracer_field[:, :-1])
    )
    return east_part[:, 1:-1] + north_flux[:, 1:] - north_flux[:, :-1]


def columns(tracer_field, wetness):
    level_flux = vertical_mix * wetness[1:] * (tracer_field[1:] - tracer_field[:-1])
    zeros_top = jnp.zeros_like(level_flux[:1])
    flux_below = jnp.concatenate([level_flux, zeros_top], axis=0)
    flux_above = jnp.concatenate([zeros_top, level_flux], axis=0)
    return (flux_below - flux_above)[:, 1:-1]


def advance(tracer_field, mixing, wetness):
    return (
        tracer_field[:, 1:-1]
        + lateral(tracer_field, mixing, wetness)
        + columns(tracer_field, wetness)
    )


def sensitivity(base_field, adjoint_field, wetness):
    east_term = (
        wetness
        * jnp.roll(wetness, -1, axis=-1)
        * (jnp.roll(base_field, -1, axis=-1) - base_field)
        * (jnp.roll(adjoint_field, -1, axis=-1) - adjoint_field)
    )
    east_sum = jnp.sum(east_term[:, 1:-1], axis=0)
    north_term = (
        wetness[:, :-1]
        * wetness[:, 1:]
        * (base_field[:, 1:] - base_field[:, :-1])
        * (adjoint_field[:, 1:] - adjoint_field[:, :-1])
    )
    north_sum = jnp.sum(north_term, axis=0)
    return -0.5 * (east_sum + jnp.roll(east_sum, 1, axis=-1) + north_sum[1:] + north_sum[:-1])


def class_totals(values, classes, class_count):
    totals = jnp.zeros((values.shape[1], class_count), jnp.float32)
    labels = jnp.arange(class_count, dtype=jnp.int32)[:, None, None, None]
    for first_level in range(0, values.shape[0], level_block):
        last_level = min(first_level + level_block, values.shape[0])
        chosen = classes[first_level:last_level][None] == labels
        block_sum = jnp.sum(
            jnp.where(chosen, values[first_level:last_level][None], 0.0), axis=(1, 3)
        )
        totals = totals + block_sum.T
    return totals


def class_lookup(row_table, classes):
    labels = jnp.arange(row_table.shape[1], dtype=jnp.int32)[:, None, None, None]
    pieces = []
    for first_level in range(0, classes.shape[0], level_block):
        last_level = min(first_level + level_block, classes.shape[0])
        chosen = classes[first_level:last_level][None] == labels
        pieces.append(jnp.sum(jnp.where(chosen, row_table.T[:, None, :, None], 0.0), axis=0))
    return jnp.concatenate(pieces, axis=0)


def body(tracer, diffusivity, direction, column_depth, density_class, band_of_row, weights):
    row_count = tracer.shape[1]
    band_total = weights.shape[0]
    class_count = weights.shape[1]
    band_own = band_total // lax.axis_size("lat")
    static = jnp.stack([diffusivity, direction, column_depth.astype(jnp.float32)])
    static_ext = with_halo(static, (("lat", 1),), STEPS)
    level_values = jnp.arange(tracer.shape[0], dtype=jnp.float32)[:, None, None]
    lower_row = STEPS - 1
    slab = static_ext[:, lower_row : lower_row + row_count + 2 * 1]
    wetness = (level_values < slab[2][None]).astype(jnp.float32)
    mix_one = slab[0]
    dir_one = slab[1]
    stored = []
    tangent = None
    base_field = tracer
    for step_index in range(STEPS):
        if step_index == 0:
            base_ext = with_halo(base_field, (("lat", 1),), 1)
            tangent = lateral(base_ext, dir_one, wetness)
        else:
            paired = with_halo(jnp.stack([base_field, tangent]), (("lat", 2),), 1)
            base_ext = paired[0]
            tangent = advance(paired[1], mix_one, wetness) + lateral(base_ext, dir_one, wetness)
        stored.append(base_ext)
        if step_index + 1 < STEPS:
            base_field = advance(base_ext, mix_one, wetness)
    wet_own = wetness[:, 1:-1]
    row_sums = class_totals(wet_own * tangent, density_class, class_count)
    band_hot = (band_of_row[:, None] == jnp.arange(band_total, dtype=jnp.int32)[None]).astype(
        jnp.float32
    )
    partial_value = jnp.dot(
        band_hot.T, row_sums, precision=lax.Precision.HIGHEST, preferred_element_type=jnp.float32
    )
    totals = lax.psum(partial_value, "lat")
    weighted = weights * totals
    own_bins = lax.dynamic_slice_in_dim(totals, lax.axis_index("lat") * band_own, band_own, 0)
    row_table = jnp.dot(
        band_hot, weighted, precision=lax.Precision.HIGHEST, preferred_element_type=jnp.float32
    )
    adjoint = wet_own * class_lookup(row_table, density_class)
    gradient = jnp.zeros((row_count, tracer.shape[2]), jnp.float32)
    for step_index in reversed(range(STEPS)):
        adjoint_ext = with_halo(adjoint, (("lat", 1),), 1)
        gradient = gradient + sensitivity(stored[step_index], adjoint_ext, wetness)
        if step_index > 0:
            adjoint = advance(adjoint_ext, mix_one, wetness)
    return (own_bins, gradient)


def solution(mesh):
    placed = (
        P(None, ("members", "lat"), None),
        P("lat", None),
        P(("members", "lat"), None),
        P("lat", None),
        P(None, ("members", "lat"), None),
        P("lat"),
        P(),
    )
    return jax.shard_map(
        body,
        mesh=mesh,
        in_specs=placed,
        out_specs=(P(("members", "lat"), None), P(("members", "lat"), None)),
        check_vma=False,
    )
```

profile of v0, /device:TPU:1, one launch (start us, length us, event | category | flops | bytes accessed | tf_op | source)
XLA Modules:
  0.0 160.4 jit_solution(2321920101342643986)
XLA Ops:
  2.2 4.5 %collective-permute-start = (f32[3,3,1440]{2,1,0:T(4,128)S(1)}, f32[3,3,1440]{2,1,0:T(4,128)S(1)}, u32[]{:S(2)}, u32[]{:S(2)}) collective-permute-start(f32[3,3,1440]{2,1,0:T(4,128)S(1)} %get-tuple-element.53), channel_id=1, source_target_pairs={{0,1},{1,2},{2,3},{3,4},{4,5},{5,6},{6,7},{7,8},{8,9},{9,10},{10,1... | collective-permute-start | bytes 155528 | tf_op jit(solution)/shard_map/ppermute | solution.py:18
  6.8 1.9 %collective-permute-start.1 = (f32[3,3,1440]{2,1,0:T(4,128)S(1)}, f32[3,3,1440]{2,1,0:T(4,128)S(1)}, u32[]{:S(2)}, u32[]{:S(2)}) collective-permute-start(f32[3,3,1440]{2,1,0:T(4,128)S(1)} %get-tuple-element.54), channel_id=1, source_target_pairs={{1,0},{2,1},{3,2},{4,3},{5,4},{6,5},{7,6},{8,7},{9,8},{10,9},{11,1... | collective-permute-start | bytes 155528 | tf_op jit(solution)/shard_map/ppermute | solution.py:21
  8.7 1.3 fusion.75
  10.0 3.6 %collective-permute-start.2 = (f32[16,1,1440]{2,1,0:T(1,128)S(1)}, f32[16,1,1440]{2,1,0:T(1,128)S(1)}, u32[]{:S(2)}, u32[]{:S(2)}) collective-permute-start(f32[16,1,1440]{2,1,0:T(1,128)S(1)} %get-tuple-element.47), channel_id=1, source_target_pairs={{0,1},{1,2},{2,3},{3,4},{4,5},{5,6},{6,7},{7,8},{8,9},{9,10},{10,1... | collective-permute-start | bytes 276488 | tf_op jit(solution)/shard_map/ppermute | solution.py:18
  13.7 1.9 %collective-permute-start.3 = (f32[16,1,1440]{2,1,0:T(1,128)S(1)}, f32[16,1,1440]{2,1,0:T(1,128)S(1)}, u32[]{:S(2)}, u32[]{:S(2)}) collective-permute-start(f32[16,1,1440]{2,1,0:T(1,128)S(1)} %get-tuple-element.46), channel_id=1, source_target_pairs={{1,0},{2,1},{3,2},{4,3},{5,4},{6,5},{7,6},{8,7},{9,8},{10,9},{11,1... | collective-permute-start | bytes 276488 | tf_op jit(solution)/shard_map/ppermute | solution.py:21
  17.2 2.4 %collective-permute-done.3 = f32[16,1,1440]{2,1,0:T(1,128)S(1)} collective-permute-done((f32[16,1,1440]{2,1,0:T(1,128)S(1)}, f32[16,1,1440]{2,1,0:T(1,128)S(1)}, u32[]{:S(2)}, u32[]{:S(2)}) %collective-permute-start.3) | collective-permute-done | bytes 92192 | tf_op jit(solution)/shard_map/ppermute | solution.py:21
  23.4 1.9 %collective-permute-start.4 = (f32[2,16,1,1440]{3,2,1,0:T(1,128)S(1)}, f32[2,16,1,1440]{3,2,1,0:T(1,128)S(1)}, u32[]{:S(2)}, u32[]{:S(2)}) collective-permute-start(f32[2,16,1,1440]{3,2,1,0:T(1,128)S(1)} %get-tuple-element.37), channel_id=1, source_target_pairs={{0,1},{1,2},{2,3},{3,4},{4,5},{5,6},{6,7},{7,8},{8,9},{9,10},{10,1... | collective-permute-start | bytes 552968 | tf_op jit(solution)/shard_map/ppermute | solution.py:18
  25.3 2.4 %collective-permute-start.5 = (f32[2,16,1,1440]{3,2,1,0:T(1,128)S(1)}, f32[2,16,1,1440]{3,2,1,0:T(1,128)S(1)}, u32[]{:S(2)}, u32[]{:S(2)}) collective-permute-start(f32[2,16,1,1440]{3,2,1,0:T(1,128)S(1)} %get-tuple-element.38), channel_id=1, source_target_pairs={{1,0},{2,1},{3,2},{4,3},{5,4},{6,5},{7,6},{8,7},{9,8},{10,9},{11,1... | collective-permute-start | bytes 552968 | tf_op jit(solution)/shard_map/ppermute | solution.py:21
  27.9 6.1 %collective-permute-done.5 = f32[2,16,1,1440]{3,2,1,0:T(1,128)S(1)} collective-permute-done((f32[2,16,1,1440]{3,2,1,0:T(1,128)S(1)}, f32[2,16,1,1440]{3,2,1,0:T(1,128)S(1)}, u32[]{:S(2)}, u32[]{:S(2)}) %collective-permute-start.5) | collective-permute-done | bytes 184352 | tf_op jit(solution)/shard_map/ppermute | solution.py:21
  35.5 1.4 fusion.70
  39.5 1.9 %collective-permute-start.6 = (f32[2,16,1,1440]{3,2,1,0:T(1,128)S(1)}, f32[2,16,1,1440]{3,2,1,0:T(1,128)S(1)}, u32[]{:S(2)}, u32[]{:S(2)}) collective-permute-start(f32[2,16,1,1440]{3,2,1,0:T(1,128)S(1)} %get-tuple-element.32), channel_id=1, source_target_pairs={{0,1},{1,2},{2,3},{3,4},{4,5},{5,6},{6,7},{7,8},{8,9},{9,10},{10,1... | collective-permute-start | bytes 552968 | tf_op jit(solution)/shard_map/ppermute | solution.py:18
  41.5 2.6 %collective-permute-start.7 = (f32[2,16,1,1440]{3,2,1,0:T(1,128)S(1)}, f32[2,16,1,1440]{3,2,1,0:T(1,128)S(1)}, u32[]{:S(2)}, u32[]{:S(2)}) collective-permute-start(f32[2,16,1,1440]{3,2,1,0:T(1,128)S(1)} %get-tuple-element.33), channel_id=1, source_target_pairs={{1,0},{2,1},{3,2},{4,3},{5,4},{6,5},{7,6},{8,7},{9,8},{10,9},{11,1... | collective-permute-start | bytes 552968 | tf_op jit(solution)/shard_map/ppermute | solution.py:21
  44.1 5.2 %collective-permute-done.7 = f32[2,16,1,1440]{3,2,1,0:T(1,128)S(1)} collective-permute-done((f32[2,16,1,1440]{3,2,1,0:T(1,128)S(1)}, f32[2,16,1,1440]{3,2,1,0:T(1,128)S(1)}, u32[]{:S(2)}, u32[]{:S(2)}) %collective-permute-start.7) | collective-permute-done | bytes 184352 | tf_op jit(solution)/shard_map/ppermute | solution.py:21
  51.0 1.4 fusion.19
  53.7 2.7 %select_reduce_fusion.1 = f32[72,4]{0,1:T(4,128)S(1)} fusion(f32[10,4,1440]{2,1,0:T(4,128)S(1)} %slice.815, s32[10,4,1440]{2,1,0:T(4,128)S(1)} %slice.591), kind=kLoop, calls=%fused_computation.1 | loop fusion | flops 12441312 | bytes 461952 | tf_op jit(solution)/shard_map/reduce_sum | solution.py:82
  56.3 1.8 %select_reduce_fusion.3 = f32[72,4]{0,1:T(4,128)S(1)} fusion(f32[6,4,1440]{2,1,0:T(4,128)S(1)} %slice.816, s32[6,4,1440]{2,1,0:T(4,128)S(1)} %slice.690), kind=kLoop, calls=%fused_computation.4 | loop fusion | flops 7464672 | bytes 277632 | tf_op jit(solution)/shard_map/reduce_sum | solution.py:82
  59.0 53.0 %psum.7 = f32[32,72]{1,0:T(8,128)S(1)} all-reduce(f32[32,72]{1,0:T(8,128)} %fusion.62), channel_id=1, replica_groups=mesh['members'=2,'lat'=16] {'lat'}, use_global_device_ids=true, to_apply=%region_2.3 | all-reduce | flops 2304 | bytes 18432 | tf_op jit(solution)/shard_map/psum | solution.py:134
  112.9 4.2 %select_reduce_fusion = f32[10,4,1440]{2,1,0:T(4,128)S(1)} fusion(f32[72,4]{0,1:T(4,128)S(1)} %fusion.60, s32[10,4,1440]{2,1,0:T(4,128)S(1)} %slice.591), kind=kLoop, calls=%fused_computation | loop fusion | flops 12384000 | bytes 461952 | tf_op jit(solution)/shard_map/reduce_sum | solution.py:95
  117.0 1.9 %select_reduce_fusion.2 = f32[6,4,1440]{2,1,0:T(4,128)S(1)} fusion(f32[72,4]{0,1:T(4,128)S(1)} %fusion.60, s32[6,4,1440]{2,1,0:T(4,128)S(1)} %slice.690), kind=kLoop, calls=%fused_computation.3 | loop fusion | flops 7430400 | bytes 277632 | tf_op jit(solution)/shard_map/reduce_sum | solution.py:95
  119.3 3.6 %collective-permute-start.8 = (f32[16,1,1440]{2,1,0:T(1,128)S(1)}, f32[16,1,1440]{2,1,0:T(1,128)S(1)}, u32[]{:S(2)}, u32[]{:S(2)}) collective-permute-start(f32[16,1,1440]{2,1,0:T(1,128)S(1)} %get-tuple-element.44), channel_id=1, source_target_pairs={{0,1},{1,2},{2,3},{3,4},{4,5},{5,6},{6,7},{7,8},{8,9},{9,10},{10,1... | collective-permute-start | bytes 276488 | tf_op jit(solution)/shard_map/ppermute | solution.py:18
  122.9 4.6 %collective-permute-start.9 = (f32[16,1,1440]{2,1,0:T(1,128)S(1)}, f32[16,1,1440]{2,1,0:T(1,128)S(1)}, u32[]{:S(2)}, u32[]{:S(2)}) collective-permute-start(f32[16,1,1440]{2,1,0:T(1,128)S(1)} %get-tuple-element.45), channel_id=1, source_target_pairs={{1,0},{2,1},{3,2},{4,3},{5,4},{6,5},{7,6},{8,7},{9,8},{10,9},{11,1... | collective-permute-start | bytes 276488 | tf_op jit(solution)/shard_map/ppermute | solution.py:21
  127.6 1.3 collective-permute-done.9
  130.3 1.4 fusion.69
  134.2 1.9 %collective-permute-start.10 = (f32[16,1,1440]{2,1,0:T(1,128)}, f32[16,1,1440]{2,1,0:T(1,128)}, u32[]{:S(2)}, u32[]{:S(2)}) collective-permute-start(f32[16,1,1440]{2,1,0:T(1,128)} %get-tuple-element.42), channel_id=1, source_target_pairs={{0,1},{1,2},{2,3},{3,4},{4,5},{5,6},{6,7},{7,8},{8,9},{9,10},{10,1... | collective-permute-start | bytes 276488 | tf_op jit(solution)/shard_map/ppermute | solution.py:18
  136.1 3.3 %collective-permute-start.11 = (f32[16,1,1440]{2,1,0:T(1,128)}, f32[16,1,1440]{2,1,0:T(1,128)}, u32[]{:S(2)}, u32[]{:S(2)}) collective-permute-start(f32[16,1,1440]{2,1,0:T(1,128)} %get-tuple-element.43), channel_id=1, source_target_pairs={{1,0},{2,1},{3,2},{4,3},{5,4},{6,5},{7,6},{8,7},{9,8},{10,9},{11,1... | collective-permute-start | bytes 276488 | tf_op jit(solution)/shard_map/ppermute | solution.py:21
  139.4 2.9 %collective-permute-done.11 = f32[16,1,1440]{2,1,0:T(1,128)} collective-permute-done((f32[16,1,1440]{2,1,0:T(1,128)}, f32[16,1,1440]{2,1,0:T(1,128)}, u32[]{:S(2)}, u32[]{:S(2)}) %collective-permute-start.11) | collective-permute-done | bytes 92192 | tf_op jit(solution)/shard_map/ppermute | solution.py:21
  142.3 1.3 pad_maximum_fusion.5
  145.0 1.5 fusion.68
  146.6 2.0 %multiply_reduce_fusion.1 = (f32[5,1440]{1,0:T(8,128)S(1)}, f32[5,1440]{1,0:T(8,128)S(1)}, f32[16,5,1440]{2,1,0:T(8,128)S(1)}) fusion(f32[16,4,1440]{2,1,0:T(4,128)S(1)} %maximum_multiply_fusion, f32[16,1,1440]{2,1,0:T(1,128)S(1)} %copy-done.28, f32[16,1,1440]{2,1,0:T(1,128)S(1)} %copy-done.30, f32[16,6,1440]{2,1,0:T(8,128)S(1)} %get-tuple-element.26, ...), kind=kLoop, calls=%fused_computation.39 | loop fusion | flops 1828800 | bytes 4849920 | tf_op jit(solution)/shard_map/reduce_sum | solution.py:72
  149.3 2.1 %collective-permute-start.12 = (f32[16,1,1440]{2,1,0:T(1,128)S(1)}, f32[16,1,1440]{2,1,0:T(1,128)S(1)}, u32[]{:S(2)}, u32[]{:S(2)}) collective-permute-start(f32[16,1,1440]{2,1,0:T(1,128)S(1)} %get-tuple-element.40), channel_id=1, source_target_pairs={{0,1},{1,2},{2,3},{3,4},{4,5},{5,6},{6,7},{7,8},{8,9},{9,10},{10,1... | collective-permute-start | bytes 276488 | tf_op jit(solution)/shard_map/ppermute | solution.py:18
  151.3 2.4 %collective-permute-start.13 = (f32[16,1,1440]{2,1,0:T(1,128)S(1)}, f32[16,1,1440]{2,1,0:T(1,128)S(1)}, u32[]{:S(2)}, u32[]{:S(2)}) collective-permute-start(f32[16,1,1440]{2,1,0:T(1,128)S(1)} %get-tuple-element.41), channel_id=1, source_target_pairs={{1,0},{2,1},{3,2},{4,3},{5,4},{6,5},{7,6},{8,7},{9,8},{10,9},{11,1... | collective-permute-start | bytes 276488 | tf_op jit(solution)/shard_map/ppermute | solution.py:21
  154.3 2.9 %collective-permute-done.13 = f32[16,1,1440]{2,1,0:T(1,128)S(1)} collective-permute-done((f32[16,1,1440]{2,1,0:T(1,128)S(1)}, f32[16,1,1440]{2,1,0:T(1,128)S(1)}, u32[]{:S(2)}, u32[]{:S(2)}) %collective-permute-start.13) | collective-permute-done | bytes 92192 | tf_op jit(solution)/shard_map/ppermute | solution.py:21
  (162 shorter events, 25.5 us)
Async XLA Ops:
  0.6 16.2 %copy-start.33 = (f32[4,1440]{1,0:T(4,128)S(1)}, f32[4,1440]{1,0:T(4,128)}, u32[]{:S(2)}) copy-start(f32[4,1440]{1,0:T(4,128)} %param.8) | copy-start | bytes 69124
  0.6 16.2 %copy-start.32 = (f32[4,1440]{1,0:T(4,128)S(1)}, f32[4,1440]{1,0:T(4,128)}, u32[]{:S(2)}) copy-start(f32[4,1440]{1,0:T(4,128)} %param.9) | copy-start | bytes 69124
  2.2 13.4 %collective-permute-start = (f32[3,3,1440]{2,1,0:T(4,128)S(1)}, f32[3,3,1440]{2,1,0:T(4,128)S(1)}, u32[]{:S(2)}, u32[]{:S(2)}) collective-permute-start(f32[3,3,1440]{2,1,0:T(4,128)S(1)} %get-tuple-element.53), channel_id=1, source_target_pairs={{0,1},{1,2},{2,3},{3,4},{4,5},{5,6},{6,7},{7,8},{8,9},{9,10},{10,1... | collective-permute-start | bytes 155528 | tf_op jit(solution)/shard_map/ppermute | solution.py:18
  6.8 8.8 %collective-permute-start.1 = (f32[3,3,1440]{2,1,0:T(4,128)S(1)}, f32[3,3,1440]{2,1,0:T(4,128)S(1)}, u32[]{:S(2)}, u32[]{:S(2)}) collective-permute-start(f32[3,3,1440]{2,1,0:T(4,128)S(1)} %get-tuple-element.54), channel_id=1, source_target_pairs={{1,0},{2,1},{3,2},{4,3},{5,4},{6,5},{7,6},{8,7},{9,8},{10,9},{11,1... | collective-permute-start | bytes 155528 | tf_op jit(solution)/shard_map/ppermute | solution.py:21
  10.0 7.1 %collective-permute-start.2 = (f32[16,1,1440]{2,1,0:T(1,128)S(1)}, f32[16,1,1440]{2,1,0:T(1,128)S(1)}, u32[]{:S(2)}, u32[]{:S(2)}) collective-permute-start(f32[16,1,1440]{2,1,0:T(1,128)S(1)} %get-tuple-element.47), channel_id=1, source_target_pairs={{0,1},{1,2},{2,3},{3,4},{4,5},{5,6},{6,7},{7,8},{8,9},{9,10},{10,1... | collective-permute-start | bytes 276488 | tf_op jit(solution)/shard_map/ppermute | solution.py:18
  13.7 5.9 %collective-permute-start.3 = (f32[16,1,1440]{2,1,0:T(1,128)S(1)}, f32[16,1,1440]{2,1,0:T(1,128)S(1)}, u32[]{:S(2)}, u32[]{:S(2)}) collective-permute-start(f32[16,1,1440]{2,1,0:T(1,128)S(1)} %get-tuple-element.46), channel_id=1, source_target_pairs={{1,0},{2,1},{3,2},{4,3},{5,4},{6,5},{7,6},{8,7},{9,8},{10,9},{11,1... | collective-permute-start | bytes 276488 | tf_op jit(solution)/shard_map/ppermute | solution.py:21
  16.4 34.6 %copy-start.14 = (f32[6,1440]{1,0:T(8,128)}, f32[6,1440]{1,0:T(8,128)S(1)}, u32[]{:S(2)}) copy-start(f32[6,1440]{1,0:T(8,128)S(1)} %get-tuple-element.52) | copy-start | bytes 103684
  16.6 3.0 %copy-start.5 = (f32[16,4,1440]{2,1,0:T(4,128)S(1)}, f32[16,4,1440]{2,1,0:T(4,128)}, u32[]{:S(2)}) copy-start(f32[16,4,1440]{2,1,0:T(4,128)} %param.7) | copy-start | bytes 1105924
  16.8 34.2 %copy-start.17 = (f32[6,1440]{1,0:T(8,128)}, f32[6,1440]{1,0:T(8,128)S(1)}, u32[]{:S(2)}) copy-start(f32[6,1440]{1,0:T(8,128)S(1)} %get-tuple-element.55) | copy-start | bytes 103684
  17.1 33.9 %copy-start.11 = (f32[16,6,1]{2,1,0:T(8,128)}, f32[16,6,1]{2,1,0:T(8,128)S(1)}, u32[]{:S(2)}) copy-start(f32[16,6,1]{2,1,0:T(8,128)S(1)} %slice.741) | copy-start | bytes 1156
  17.2 4.5 %copy-start.23 = (f32[16,1,1440]{2,1,0:T(1,128)}, f32[16,1,1440]{2,1,0:T(1,128)S(1)}, u32[]{:S(2)}) copy-start(f32[16,1,1440]{2,1,0:T(1,128)S(1)} %collective-permute-done.2) | copy-start | bytes 276484
  19.6 2.1 %copy-start.25 = (f32[16,1,1440]{2,1,0:T(1,128)}, f32[16,1,1440]{2,1,0:T(1,128)S(1)}, u32[]{:S(2)}) copy-start(f32[16,1,1440]{2,1,0:T(1,128)S(1)} %collective-permute-done.3) | copy-start | bytes 276484
  22.2 27.8 %copy-start = (f32[16,5,1440]{2,1,0:T(8,128)}, f32[16,5,1440]{2,1,0:T(8,128)S(1)}, u32[]{:S(2)}) copy-start(f32[16,5,1440]{2,1,0:T(8,128)S(1)} %get-tuple-element.18) | copy-start | bytes 1382404
  23.4 4.5 %collective-permute-start.4 = (f32[2,16,1,1440]{3,2,1,0:T(1,128)S(1)}, f32[2,16,1,1440]{3,2,1,0:T(1,128)S(1)}, u32[]{:S(2)}, u32[]{:S(2)}) collective-permute-start(f32[2,16,1,1440]{3,2,1,0:T(1,128)S(1)} %get-tuple-element.37), channel_id=1, source_target_pairs={{0,1},{1,2},{2,3},{3,4},{4,5},{5,6},{6,7},{7,8},{8,9},{9,10},{10,1... | collective-permute-start | bytes 552968 | tf_op jit(solution)/shard_map/ppermute | solution.py:18
  25.3 8.7 %collective-permute-start.5 = (f32[2,16,1,1440]{3,2,1,0:T(1,128)S(1)}, f32[2,16,1,1440]{3,2,1,0:T(1,128)S(1)}, u32[]{:S(2)}, u32[]{:S(2)}) collective-permute-start(f32[2,16,1,1440]{3,2,1,0:T(1,128)S(1)} %get-tuple-element.38), channel_id=1, source_target_pairs={{1,0},{2,1},{3,2},{4,3},{5,4},{6,5},{7,6},{8,7},{9,8},{10,9},{11,1... | collective-permute-start | bytes 552968 | tf_op jit(solution)/shard_map/ppermute | solution.py:21
  38.3 5.8 %copy-start.31 = (s32[16,4,1440]{2,1,0:T(4,128)S(1)}, s32[16,4,1440]{2,1,0:T(4,128)}, u32[]{:S(2)}) copy-start(s32[16,4,1440]{2,1,0:T(4,128)} %param.11) | copy-start | bytes 1105924
  39.5 4.6 %collective-permute-start.6 = (f32[2,16,1,1440]{3,2,1,0:T(1,128)S(1)}, f32[2,16,1,1440]{3,2,1,0:T(1,128)S(1)}, u32[]{:S(2)}, u32[]{:S(2)}) collective-permute-start(f32[2,16,1,1440]{3,2,1,0:T(1,128)S(1)} %get-tuple-element.32), channel_id=1, source_target_pairs={{0,1},{1,2},{2,3},{3,4},{4,5},{5,6},{6,7},{7,8},{8,9},{9,10},{10,1... | collective-permute-start | bytes 552968 | tf_op jit(solution)/shard_map/ppermute | solution.py:18
  41.5 7.9 %collective-permute-start.7 = (f32[2,16,1,1440]{3,2,1,0:T(1,128)S(1)}, f32[2,16,1,1440]{3,2,1,0:T(1,128)S(1)}, u32[]{:S(2)}, u32[]{:S(2)}) collective-permute-start(f32[2,16,1,1440]{3,2,1,0:T(1,128)S(1)} %get-tuple-element.33), channel_id=1, source_target_pairs={{1,0},{2,1},{3,2},{4,3},{5,4},{6,5},{7,6},{8,7},{9,8},{10,9},{11,1... | collective-permute-start | bytes 552968 | tf_op jit(solution)/shard_map/ppermute | solution.py:21
  53.6 4.5 %copy-start.34 = (s32[4]{0:T(128)S(1)}, s32[4]{0:T(128)}, u32[]{:S(2)}) copy-start(s32[4]{0:T(128)} %param.12) | copy-start | bytes 52
  119.3 8.3 %collective-permute-start.8 = (f32[16,1,1440]{2,1,0:T(1,128)S(1)}, f32[16,1,1440]{2,1,0:T(1,128)S(1)}, u32[]{:S(2)}, u32[]{:S(2)}) collective-permute-start(f32[16,1,1440]{2,1,0:T(1,128)S(1)} %get-tuple-element.44), channel_id=1, source_target_pairs={{0,1},{1,2},{2,3},{3,4},{4,5},{5,6},{6,7},{7,8},{8,9},{9,10},{10,1... | collective-permute-start | bytes 276488 | tf_op jit(solution)/shard_map/ppermute | solution.py:18
  122.9 5.9 %collective-permute-start.9 = (f32[16,1,1440]{2,1,0:T(1,128)S(1)}, f32[16,1,1440]{2,1,0:T(1,128)S(1)}, u32[]{:S(2)}, u32[]{:S(2)}) collective-permute-start(f32[16,1,1440]{2,1,0:T(1,128)S(1)} %get-tuple-element.45), channel_id=1, source_target_pairs={{1,0},{2,1},{3,2},{4,3},{5,4},{6,5},{7,6},{8,7},{9,8},{10,9},{11,1... | collective-permute-start | bytes 276488 | tf_op jit(solution)/shard_map/ppermute | solution.py:21
  127.6 4.1 %copy-start.27 = (f32[16,1,1440]{2,1,0:T(1,128)}, f32[16,1,1440]{2,1,0:T(1,128)S(1)}, u32[]{:S(2)}) copy-start(f32[16,1,1440]{2,1,0:T(1,128)S(1)} %collective-permute-done.8) | copy-start | bytes 276484
  128.9 2.8 %copy-start.29 = (f32[16,1,1440]{2,1,0:T(1,128)}, f32[16,1,1440]{2,1,0:T(1,128)S(1)}, u32[]{:S(2)}) copy-start(f32[16,1,1440]{2,1,0:T(1,128)S(1)} %collective-permute-done.9) | copy-start | bytes 276484
  134.2 5.2 %collective-permute-start.10 = (f32[16,1,1440]{2,1,0:T(1,128)}, f32[16,1,1440]{2,1,0:T(1,128)}, u32[]{:S(2)}, u32[]{:S(2)}) collective-permute-start(f32[16,1,1440]{2,1,0:T(1,128)} %get-tuple-element.42), channel_id=1, source_target_pairs={{0,1},{1,2},{2,3},{3,4},{4,5},{5,6},{6,7},{7,8},{8,9},{9,10},{10,1... | collective-permute-start | bytes 276488 | tf_op jit(solution)/shard_map/ppermute | solution.py:18
  136.1 6.3 %collective-permute-start.11 = (f32[16,1,1440]{2,1,0:T(1,128)}, f32[16,1,1440]{2,1,0:T(1,128)}, u32[]{:S(2)}, u32[]{:S(2)}) collective-permute-start(f32[16,1,1440]{2,1,0:T(1,128)} %get-tuple-element.43), channel_id=1, source_target_pairs={{1,0},{2,1},{3,2},{4,3},{5,4},{6,5},{7,6},{8,7},{9,8},{10,9},{11,1... | collective-permute-start | bytes 276488 | tf_op jit(solution)/shard_map/ppermute | solution.py:21
  148.6 9.2 %copy-start.22 = (f32[16,6,1440]{2,1,0:T(8,128)S(1)}, f32[16,6,1440]{2,1,0:T(8,128)}, u32[]{:S(2)}) copy-start(f32[16,6,1440]{2,1,0:T(8,128)} %get-tuple-element.10) | copy-start | bytes 1658884
  149.1 8.8 %copy-start.21 = (f32[16,6,1440]{2,1,0:T(8,128)S(1)}, f32[16,6,1440]{2,1,0:T(8,128)}, u32[]{:S(2)}) copy-start(f32[16,6,1440]{2,1,0:T(8,128)} %get-tuple-element.12) | copy-start | bytes 1658884
  149.2 8.6 %copy-start.8 = (f32[16,6,1440]{2,1,0:T(8,128)S(1)}, f32[16,6,1440]{2,1,0:T(8,128)}, u32[]{:S(2)}) copy-start(f32[16,6,1440]{2,1,0:T(8,128)} %copy-done.7) | copy-start | bytes 1658884
  149.2 8.6 %copy-start.10 = (f32[16,6,1440]{2,1,0:T(8,128)S(1)}, f32[16,6,1440]{2,1,0:T(8,128)}, u32[]{:S(2)}) copy-start(f32[16,6,1440]{2,1,0:T(8,128)} %copy-done.9) | copy-start | bytes 1658884
  149.2 8.6 %copy-start.20 = (f32[16,6,1440]{2,1,0:T(8,128)S(1)}, f32[16,6,1440]{2,1,0:T(8,128)}, u32[]{:S(2)}) copy-start(f32[16,6,1440]{2,1,0:T(8,128)} %get-tuple-element.31) | copy-start | bytes 1658884
  149.3 5.1 %collective-permute-start.12 = (f32[16,1,1440]{2,1,0:T(1,128)S(1)}, f32[16,1,1440]{2,1,0:T(1,128)S(1)}, u32[]{:S(2)}, u32[]{:S(2)}) collective-permute-start(f32[16,1,1440]{2,1,0:T(1,128)S(1)} %get-tuple-element.40), channel_id=1, source_target_pairs={{0,1},{1,2},{2,3},{3,4},{4,5},{5,6},{6,7},{7,8},{8,9},{9,10},{10,1... | collective-permute-start | bytes 276488 | tf_op jit(solution)/shard_map/ppermute | solution.py:18
  151.3 5.9 %collective-permute-start.13 = (f32[16,1,1440]{2,1,0:T(1,128)S(1)}, f32[16,1,1440]{2,1,0:T(1,128)S(1)}, u32[]{:S(2)}, u32[]{:S(2)}) collective-permute-start(f32[16,1,1440]{2,1,0:T(1,128)S(1)} %get-tuple-element.41), channel_id=1, source_target_pairs={{1,0},{2,1},{3,2},{4,3},{5,4},{6,5},{7,6},{8,7},{9,8},{10,9},{11,1... | collective-permute-start | bytes 276488 | tf_op jit(solution)/shard_map/ppermute | solution.py:21
  (17 other events, 18.5 us)
where the time goes:
time: 161 us; the launch traced here: 160 us
  blocking collectives  53 us (33%)
  starting transfers between devices  38.8 us (24%)
  other arithmetic  34.4 us (21%)
  waiting for transfers between devices  21.1 us (13%)
  local copies, waits for them, and re-layouts  9.92 us (6%)
  matrix products  1.78 us (1%)
    psum x1, blocking collectives, body(): totals = lax.psum(partial_value, 'lat')  53 us
    ppermute x7, waiting for transfers between devices, with_halo(): lax.ppermute(lax.slice_in_dim(block, 0, width, axis=dim), axis, backward)  20.9 us
    ppermute x7, starting transfers between devices, with_halo(): lax.ppermute(lax.slice_in_dim(block, block.shape[dim] - width, None, axis...  19.6 us
    ppermute x7, starting transfers between devices, with_halo(): lax.ppermute(lax.slice_in_dim(block, 0, width, axis=dim), axis, backward)  19.2 us
    mul x8, other arithmetic, lateral(): east_mix * wetness * jnp.roll(wetness, -1, axis=-1)  6.55 us
    reduce_sum x2, other arithmetic, class_lookup(): jnp.sum(jnp.where(chosen, row_table.T[:, None, :, None], 0.0), axis=0)  6.09 us
    reduce_sum x2, other arithmetic, class_totals(): jnp.sum(jnp.where(chosen, values[first_level:last_level][None], 0.0), axi...  4.45 us
    concatenate x7, other arithmetic, with_halo(): block = jnp.concatenate([low, block, high], axis=dim)  3.99 us
  transfers between devices with their start and end apart: 14, of which 7 were waited for; matrix products, arithmetic and copies ran while one was open for 2% of the time, Pallas kernels for 0%

commit v1 on v0

v1 whole, which is shorter than its diff:
```python
import functools

import jax
import jax.numpy as jnp
from jax import lax
from jax.experimental import pallas as pl
from jax.experimental.pallas import tpu as pltpu
from jax.sharding import PartitionSpec as P

STEPS = 3
vertical_mix = 0.05

LANES = 128
GHOST = 4
OWN = LANES - 2 * GHOST
HIGH_COUNT = 5
LOW_COUNT = 16
LOW_SHIFT = 4
VMEM_LIMIT = 50 * 1024 * 1024


def strip_of(row, j, lon_count):
    first = OWN * j - GHOST
    last = first + LANES
    if first < 0:
        return jnp.concatenate([row[:, first + lon_count :], row[:, :last]], axis=1)
    if last > lon_count:
        return jnp.concatenate([row[:, first:], row[:, : last - lon_count]], axis=1)
    return row[:, first:last]


def is_odd():
    return lax.rem(lax.axis_index("lat"), 2) == 1


def oriented(ref, t, odd):
    last = ref.shape[1] - 1
    return jnp.where(odd, ref[:, last - t, :], ref[:, t, :])


def pack_fields(tracer, mix, heading, depth, own, own_maps, near, far):
    levels, rows, lon_count = tracer.shape
    strips = lon_count // OWN
    odd = is_odd()
    for t in range(rows):
        field = oriented(tracer, t, odd)
        for j in range(strips):
            strip = strip_of(field, j, lon_count)
            own[j, t * levels : (t + 1) * levels, :] = strip
            if t < STEPS:
                at = (j * STEPS + STEPS - 1 - t) * levels
                far[at : at + levels, :] = strip
            if t > 0:
                at = (j * STEPS + rows - 1 - t) * levels
                near[at : at + levels, :] = strip
    base = strips * STEPS * levels
    for a, ref in enumerate((mix, heading, depth)):
        field = ref[...].astype(jnp.float32)
        flipped = jnp.concatenate([field[r : r + 1] for r in reversed(range(rows))], axis=0)
        up = jnp.where(odd, flipped, field)
        down = jnp.where(odd, field, flipped)
        for j in range(strips):
            own_maps[j, a * 4 : a * 4 + 4, :] = strip_of(up, j, lon_count)
            strip = strip_of(down, j, lon_count)
            at = base + (3 * j + a) * STEPS
            near[at : at + STEPS, :] = strip[:STEPS]
            far[at : at + STEPS, :] = strip[1:]
    own_maps[:, 12:, :] = jnp.zeros_like(own_maps[:, 12:, :])


def pack_classes(classes, own, near, far):
    levels, rows, lon_count = classes.shape
    strips = lon_count // OWN
    odd = is_odd()
    for t in range(rows):
        field = oriented(classes, t, odd)
        for j in range(strips):
            strip = strip_of(field, j, lon_count)
            own[j, t * levels : (t + 1) * levels, :] = strip
            if t < STEPS:
                at = (j * STEPS + STEPS - 1 - t) * levels
                far[at : at + levels, :] = strip
            if t > 0:
                at = (j * STEPS + rows - 1 - t) * levels
                near[at : at + levels, :] = strip


def east(x):
    return pltpu.roll(x, LANES - 1, 1)


def west(x):
    return pltpu.roll(x, 1, 1)


class Coefficients:
    def __init__(self, maps, work, levels, with_direction):
        self.level = lax.broadcasted_iota(jnp.int32, (levels, LANES), 0).astype(jnp.float32)
        self.levels = levels
        mix, heading, depth = maps[0:16, :], maps[16:32, :], maps[32:48, :]

        def north(x):
            return pltpu.roll(x, 15, 0)

        work[0:16, :] = jnp.minimum(depth, east(depth))
        work[16:32, :] = jnp.minimum(depth, north(depth))
        work[32:48, :] = 0.5 * (mix + east(mix))
        work[48:64, :] = 0.5 * (mix + north(mix))
        if with_direction:
            work[64:80, :] = 0.5 * (heading + east(heading))
            work[80:96, :] = 0.5 * (heading + north(heading))
        self.maps = maps
        self.work = work
        self.cache = {}

    def row(self, ref, block, t):
        at = 16 * block + t + STEPS
        return jnp.broadcast_to(ref[at : at + 1, :], (self.levels, LANES))

    def get(self, kind, t):
        if (kind, t) not in self.cache:
            zero = jnp.zeros((self.levels, LANES), jnp.float32)
            if kind == "wet":
                value = self.level < self.row(self.maps, 2, t)
            elif kind == "column":
                inside = self.level + 1.0 < self.row(self.maps, 2, t)
                value = jnp.where(inside, vertical_mix, zero)
            elif kind == "east_open":
                value = self.level < self.row(self.work, 0, t)
            elif kind == "north_open":
                value = self.level < self.row(self.work, 1, t)
            else:
                block, side = {
                    "east_mix": (2, "east_open"),
                    "north_mix": (3, "north_open"),
                    "east_dir": (4, "east_open"),
                    "north_dir": (5, "north_open"),
                }[kind]
                value = jnp.where(self.get(side, t), self.row(self.work, block, t), zero)
            self.cache[kind, t] = value
        return self.cache[kind, t]


def column(field, coefficient):
    levels = field.shape[0]
    flux = coefficient * (pltpu.roll(field, levels - 1, 0) - field)
    return flux - pltpu.roll(flux, 1, 0)


def gaps(field, rows):
    across = {t: east(field[t]) - field[t] for t in rows}
    along = {t: field[t + 1] - field[t] for t in range(rows[0] - 1, rows[-1] + 1)}
    return across, along


def spread(across, along, t):
    return (across[t] - west(across[t])) + (along[t] - along[t - 1])


def forward(
    weights, band_of_row, own, own_maps, near, far, classes,
    sums, maps, later, work, grams,
):
    strips, _, _ = own.shape
    levels = own.shape[1] // 4
    odd = is_odd()
    base = strips * STEPS * levels
    has_far = jnp.logical_and(lax.axis_index("lat") != 0, lax.axis_index("lat") != lax.axis_size("lat") - 1)
    keep = jnp.where(has_far, 1.0, 0.0)
    for j in range(strips):
        for a in range(3):
            at = base + (3 * j + a) * STEPS
            low = far[at : at + STEPS, :]
            if a == 2:
                low = low * keep
            high = near[at : at + STEPS, :]
            maps[j, 16 * a : 16 * a + 16, :] = jnp.concatenate(
                [low, own_maps[j, 4 * a : 4 * a + 4, :], high, high, high], axis=0
            )
    grams[...] = jnp.zeros_like(grams)
    lane = lax.broadcasted_iota(jnp.int32, (levels, LANES), 1)
    inner = jnp.logical_and(lane >= GHOST, lane < LANES - GHOST)

    def strip(j, carry):
        coef = Coefficients(maps.at[j], work, levels, True)
        field = {}
        for s in range(STEPS):
            at = pl.multiple_of((j * STEPS + s) * levels, levels)
            field[s - STEPS] = far[pl.ds(at, levels), :]
            field[4 + s] = near[pl.ds(at, levels), :]
        for t in range(4):
            field[t] = own[j, t * levels : (t + 1) * levels, :]
        tangent = None
        for n in range(STEPS):
            rows = list(range(n + 1 - STEPS, 4 + STEPS - n - 1))
            faces = [rows[0] - 1] + rows
            across, along = gaps(field, rows)
            push_e = {t: coef.get("east_dir", t) * across[t] for t in rows}
            push_n = {t: coef.get("north_dir", t) * along[t] for t in faces}
            if n > 0:
                t_across, t_along = gaps(tangent, rows)
                push_e = {t: push_e[t] + coef.get("east_mix", t) * t_across[t] for t in rows}
                push_n = {t: push_n[t] + coef.get("north_mix", t) * t_along[t] for t in faces}
            following = {}
            for t in rows:
                value = spread(push_e, push_n, t)
                if n > 0:
                    value = value + tangent[t] + column(tangent[t], coef.get("column", t))
                following[t] = value
            tangent = following
            if n + 1 < STEPS:
                flux_e = {t: coef.get("east_mix", t) * across[t] for t in rows}
                flux_n = {t: coef.get("north_mix", t) * along[t] for t in faces}
                field = {
                    t: field[t] + spread(flux_e, flux_n, t) + column(field[t], coef.get("column", t))
                    for t in rows
                }
                for t in range(-1, 5):
                    at = (n * 6 + t + 1) * levels
                    later[j, at : at + levels, :] = field[t]
        for pair in range(2):
            tops, bottoms, ones = [], [], []
            for t in (2 * pair, 2 * pair + 1):
                chosen = jnp.logical_and(inner, coef.get("wet", t))
                value = jnp.where(chosen, tangent[t], 0.0)
                top = value.astype(jnp.bfloat16)
                bottom = (value - top.astype(jnp.float32)).astype(jnp.bfloat16)
                label = classes[j, t * levels : (t + 1) * levels, :]
                high = (label >> LOW_SHIFT).astype(jnp.float32).astype(jnp.bfloat16)
                low = (label & (LOW_COUNT - 1)).astype(jnp.float32).astype(jnp.bfloat16)
                none = jnp.zeros((levels, LANES), jnp.bfloat16)
                one = jnp.ones((levels, LANES), jnp.bfloat16)
                picks = [high == jnp.bfloat16(h) for h in range(HIGH_COUNT)]
                tops.append(
                    jnp.concatenate(
                        [jnp.where(p, top, none) for p in picks] + [jnp.where(p, bottom, none) for p in picks],
                        axis=0,
                    )
                )
                ones.append(
                    jnp.concatenate(
                        [jnp.where(low == jnp.bfloat16(l), one, none) for l in range(LOW_COUNT)], axis=0
                    )
                )
            grams[pair] += lax.dot_general(
                jnp.concatenate(tops, axis=1),
                jnp.concatenate(ones, axis=1),
                (((1,), (1,)), ((), ())),
                preferred_element_type=jnp.float32,
            )
        return carry

    lax.fori_loop(0, strips, strip, 0)

    width = LOW_COUNT * levels
    own_level = lax.broadcasted_iota(jnp.int32, (levels, width), 0)
    other_level = lax.broadcasted_iota(jnp.int32, (levels, width), 1) % levels
    diagonal = own_level == other_level
    label = lax.broadcasted_iota(jnp.int32, (8, LANES), 1)
    here = lax.broadcasted_iota(jnp.int32, (8, LANES), 0)
    table_rows = []
    for pair in range(2):
        sheets = []
        for h in range(HIGH_COUNT):
            both = (
                grams[pair, h * levels : (h + 1) * levels, :]
                + grams[pair, (HIGH_COUNT + h) * levels : (HIGH_COUNT + h + 1) * levels, :]
            )
            sheets.append(jnp.sum(jnp.where(diagonal, both, 0.0), axis=0, keepdims=True))
        sheets.append(jnp.zeros((8 - HIGH_COUNT, width), jnp.float32))
        sheet = jnp.concatenate(sheets, axis=0)
        shift = 1
        while shift < levels:
            sheet = sheet + pltpu.roll(sheet, width - shift, 1)
            shift *= 2
        low = label % LOW_COUNT
        half = LANES // levels
        spot = (low % half) * levels
        left = jnp.take_along_axis(sheet[:, :LANES], spot, axis=1)
        right = jnp.take_along_axis(sheet[:, LANES:], spot, axis=1)
        picked = jnp.where(low < half, left, right)
        picked = jnp.where(here == label // LOW_COUNT, picked, 0.0)
        table_rows.append(jnp.sum(picked, axis=0, keepdims=True))
    band_count, class_count = weights.shape
    label = lax.broadcasted_iota(jnp.int32, (1, LANES), 1)
    weighted_rows, total_rows = [], []
    for pair in range(2):
        row = jnp.where(odd, 3 - 2 * pair, 2 * pair)
        band = band_of_row[row]
        scale = weights[pl.ds(band, 1), :]
        scale = jnp.concatenate([scale, jnp.zeros((1, LANES - class_count), jnp.float32)], axis=1)
        weighted_rows.append(scale * table_rows[pair])
        total_rows.append(jnp.where(label == LANES - 1, band.astype(jnp.float32), table_rows[pair]))
    sums[...] = jnp.concatenate(
        total_rows + weighted_rows + [jnp.zeros((4, LANES), jnp.float32)], axis=0
    )


def adjoint_part(
    own, near, far, maps, later, own_classes, near_classes, far_classes,
    own_sums, near_sums, far_sums, gradient, work, strips_out,
):
    strips = own.shape[0]
    levels = own.shape[1] // 4
    rows, lon_count = gradient.shape
    odd = is_odd()

    def strip(j, carry):
        coef = Coefficients(maps.at[j], work, levels, False)
        fields = [{t: own[j, t * levels : (t + 1) * levels, :] for t in range(4)}]
        at = pl.multiple_of((j * STEPS + STEPS - 1) * levels, levels)
        fields[0][-1] = far[pl.ds(at, levels), :]
        at = pl.multiple_of(j * STEPS * levels, levels)
        fields[0][4] = near[pl.ds(at, levels), :]
        for n in range(STEPS - 1):
            fields.append(
                {t: later[j, (n * 6 + t + 1) * levels : (n * 6 + t + 2) * levels, :] for t in range(-1, 5)}
            )
        adjoint = {}
        for t in range(-STEPS, 4 + STEPS):
            if t < 0:
                at = pl.multiple_of((j * STEPS + t + STEPS) * levels, levels)
                label = far_classes[pl.ds(at, levels), :]
                source, row = far_sums, 2 + (-1 - t) // 2
            elif t < 4:
                label = own_classes[j, t * levels : (t + 1) * levels, :]
                source, row = own_sums, 2 + t // 2
            else:
                at = pl.multiple_of((j * STEPS + t - 4) * levels, levels)
                label = near_classes[pl.ds(at, levels), :]
                source, row = near_sums, 2 + (7 - t) // 2
            table = jnp.broadcast_to(source[row : row + 1, :], (8, LANES))
            value = jnp.concatenate(
                [jnp.take_along_axis(table, label[k : k + 8, :], axis=1) for k in range(0, levels, 8)], axis=0
            )
            adjoint[t] = jnp.where(coef.get("wet", t), value, 0.0)
        east_total = {t: jnp.zeros((levels, LANES), jnp.float32) for t in range(4)}
        north_total = {t: jnp.zeros((levels, LANES), jnp.float32) for t in range(-1, 4)}
        for n in reversed(range(STEPS)):
            margin = n
            rows_out = list(range(-margin, 4 + margin))
            across, along = gaps(adjoint, rows_out)
            f_across, f_along = gaps(fields[n], list(range(4)))
            for t in range(4):
                east_total[t] = east_total[t] + f_across[t] * across[t]
            for t in range(-1, 4):
                north_total[t] = north_total[t] + f_along[t] * along[t]
            if n > 0:
                faces = [rows_out[0] - 1] + rows_out
                flux_e = {t: coef.get("east_mix", t) * across[t] for t in rows_out}
                flux_n = {t: coef.get("north_mix", t) * along[t] for t in faces}
                adjoint = {
                    t: adjoint[t] + spread(flux_e, flux_n, t) + column(adjoint[t], coef.get("column", t))
                    for t in rows_out
                }
        north_total = {t: jnp.where(coef.get("north_open", t), north_total[t], 0.0) for t in north_total}
        out = []
        for t in range(4):
            part = jnp.where(coef.get("east_open", t), east_total[t], 0.0)
            part = part + west(part) + north_total[t] + north_total[t - 1]
            out.append(-0.5 * jnp.sum(part, axis=0, keepdims=True))
        up = jnp.concatenate(out, axis=0)
        down = jnp.concatenate(out[::-1], axis=0)
        strips_out[j, 0:4, :] = jnp.where(odd, down, up)
        return carry

    lax.fori_loop(0, strips, strip, 0)
    gradient[...] = jnp.concatenate(
        [strips_out[j, 0:4, GHOST : LANES - GHOST] for j in range(strips)], axis=1
    )


def near_pairs(count):
    return [(i, i ^ 1) for i in range(count)]


def far_pairs(members, count):
    pairs = []
    for m in range(members):
        for i in range(1, count - 1, 2):
            pairs += [(m * count + i, m * count + i + 1), (m * count + i + 1, m * count + i)]
        for i in (0, count - 1):
            pairs.append((m * count + i, (m ^ 1) * count + i))
    return pairs


def vmem(count):
    return [pl.BlockSpec(memory_space=pltpu.VMEM)] * count


def body(tracer, diffusivity, direction, column_depth, density_class, band_of_row, weights):
    levels, rows, lon_count = tracer.shape
    strips = lon_count // OWN
    count = lax.axis_size("lat")
    members = lax.axis_size("members")
    params = pltpu.CompilerParams(vmem_limit_bytes=VMEM_LIMIT)
    f32, i32 = jnp.float32, jnp.int32
    halo = strips * STEPS * levels
    payload = halo + strips * 9

    def to_near(x):
        return lax.ppermute(x, "lat", near_pairs(count))

    def to_far(x):
        return lax.ppermute(x, ("members", "lat"), far_pairs(members, count))

    own, own_maps, near_out, far_out = pl.pallas_call(
        pack_fields,
        name="pack_fields",
        out_shape=(
            jax.ShapeDtypeStruct((strips, rows * levels, LANES), f32),
            jax.ShapeDtypeStruct((strips, 16, LANES), f32),
            jax.ShapeDtypeStruct((payload, LANES), f32),
            jax.ShapeDtypeStruct((payload, LANES), f32),
        ),
        in_specs=vmem(4),
        out_specs=tuple(vmem(4)),
        compiler_params=params,
    )(tracer, diffusivity, direction, column_depth)
    far = to_far(far_out)
    near = to_near(near_out)

    own_classes, near_classes_out, far_classes_out = pl.pallas_call(
        pack_classes,
        name="pack_classes",
        out_shape=(
            jax.ShapeDtypeStruct((strips, rows * levels, LANES), i32),
            jax.ShapeDtypeStruct((halo, LANES), i32),
            jax.ShapeDtypeStruct((halo, LANES), i32),
        ),
        in_specs=vmem(1),
        out_specs=tuple(vmem(3)),
        compiler_params=params,
    )(density_class)
    near_classes_out, far_classes_out, near, far = lax.optimization_barrier(
        (near_classes_out, far_classes_out, near, far)
    )
    far_classes = to_far(far_classes_out)
    near_classes = to_near(near_classes_out)

    sums, maps, later = pl.pallas_call(
        forward,
        name="forward",
        out_shape=(
            jax.ShapeDtypeStruct((8, LANES), f32),
            jax.ShapeDtypeStruct((strips, 48, LANES), f32),
            jax.ShapeDtypeStruct((strips, 12 * levels, LANES), f32),
        ),
        in_specs=vmem(1) + [pl.BlockSpec(memory_space=pltpu.SMEM)] + vmem(5),
        out_specs=tuple(vmem(3)),
        scratch_shapes=[
            pltpu.VMEM((96, LANES), f32),
            pltpu.VMEM((2, 2 * HIGH_COUNT * levels, LOW_COUNT * levels), f32),
        ],
        compiler_params=params,
    )(weights, band_of_row, own, own_maps, near, far, own_classes)

    near_sums = to_near(sums)
    far_sums = to_far(sums)
    gathered = jnp.concatenate([sums, near_sums], axis=0)

    gradient = pl.pallas_call(
        adjoint_part,
        name="adjoint_part",
        out_shape=jax.ShapeDtypeStruct((rows, lon_count), f32),
        in_specs=vmem(11),
        out_specs=pl.BlockSpec(memory_space=pltpu.VMEM),
        scratch_shapes=[
            pltpu.VMEM((96, LANES), f32),
            pltpu.VMEM((strips, 8, LANES), f32),
        ],
        compiler_params=params,
    )(own, near, far, maps, later, own_classes, near_classes, far_classes, sums, near_sums, far_sums)

    step = 2
    while step < count:
        other = lax.ppermute(gathered, "lat", [(i, i ^ step) for i in range(count)])
        gathered = jnp.concatenate([gathered, other], axis=0)
        step *= 2
    band_own = weights.shape[0] // count
    finished = gathered.reshape(count, 8, LANES)[:, :2]
    wanted = lax.axis_index("lat") * band_own + jnp.arange(band_own)
    hits = finished[None, :, :, LANES - 1] == wanted[:, None, None].astype(f32)
    binned = jnp.sum(
        jnp.where(hits[..., None], finished[None, :, :, : weights.shape[1]], 0.0), axis=(1, 2)
    )
    return binned, gradient


def solution(mesh):
    placed = (
        P(None, ("members", "lat"), None),
        P("lat", None),
        P(("members", "lat"), None),
        P("lat", None),
        P(None, ("members", "lat"), None),
        P("lat"),
        P(),
    )
    return jax.shard_map(
        body,
        mesh=mesh,
        in_specs=placed,
        out_specs=(P(("members", "lat"), None), P(("members", "lat"), None)),
        check_vma=False,
    )
```

time: 161 us -> 64.4 us (0.40)
  the two profiles are of different devices: /device:TPU:1 before, /device:TPU:0 now
where the time goes in v1:
time: 64.4 us; the launch traced here: 63.6 us
  Pallas kernels  20.1 us (31%)
  starting transfers between devices  18.5 us (29%)
  local copies, waits for them, and re-layouts  10.3 us (16%)
  waiting for transfers between devices  10.1 us (16%)
  other arithmetic  3.98 us (6%)
  between operations  0.68 us (1%)
    pallas_call x1, Pallas kernels, body(): pl.pallas_call(forward, name='forward', out_shape=(jax.ShapeDtypeStruct((...  9.43 us
    ppermute x3, starting transfers between devices, body(): other = lax.ppermute(gathered, 'lat', [(i, i ^ step) for i in range(count)])  8.49 us
    unnamed x23, local copies, waits for them, and re-layouts  8.27 us
    ppermute x3, waiting for transfers between devices, body(): other = lax.ppermute(gathered, 'lat', [(i, i ^ step) for i in range(count)])  8 us
    pallas_call x1, Pallas kernels, body(): pl.pallas_call(adjoint_part, name='adjoint_part', out_shape=jax.ShapeDtyp...  7.95 us
    ppermute x3, starting transfers between devices, to_far(): return lax.ppermute(x, ('members', 'lat'), far_pairs(members, count))  6.07 us
    ppermute x3, starting transfers between devices, to_near(): return lax.ppermute(x, 'lat', near_pairs(count))  3.9 us
    ppermute x3, waiting for transfers between devices, to_far(): return lax.ppermute(x, ('members', 'lat'), far_pairs(members, count))  2.11 us
  transfers between devices with their start and end apart: 9, of which 4 were waited for; matrix products, arithmetic and copies ran while one was open for 13% of the time, Pallas kernels for 3%

profile of v1, /device:TPU:0, one launch (start us, length us, event | category | flops | bytes accessed | tf_op | source)
XLA Modules:
  0.0 63.6 jit_solution(8326824377707412138)
XLA Ops:
  0.6 1.0 %copy-done = f32[16,4,1440]{2,1,0:T(4,128)S(1)} copy-done((f32[16,4,1440]{2,1,0:T(4,128)S(1)}, f32[16,4,1440]{2,1,0:T(4,128)}, u32[]{:S(2)}) %copy-start) | copy-done | bytes 368664
  1.6 0.7 %copy-done.4 = f32[4,1440]{1,0:T(4,128)S(1)} copy-done((f32[4,1440]{1,0:T(4,128)S(1)}, f32[4,1440]{1,0:T(4,128)}, u32[]{:S(2)}) %copy-start.4) | copy-done | bytes 23064
  2.4 0.7 %copy-done.5 = f32[4,1440]{1,0:T(4,128)S(1)} copy-done((f32[4,1440]{1,0:T(4,128)S(1)}, f32[4,1440]{1,0:T(4,128)}, u32[]{:S(2)}) %copy-start.5) | copy-done | bytes 23064
  3.1 0.7 %copy-done.6 = s32[4,1440]{1,0:T(4,128)S(1)} copy-done((s32[4,1440]{1,0:T(4,128)S(1)}, s32[4,1440]{1,0:T(4,128)}, u32[]{:S(2)}) %copy-start.6) | copy-done | bytes 23064
  3.8 1.1 %pack_fields.1 = (f32[12,64,128]{2,1,0:T(8,128)S(1)}, f32[12,16,128]{2,1,0:T(8,128)S(1)}, f32[684,128]{1,0:T(8,128)S(1)}, f32[684,128]{1,0:T(8,128)S(1)}) custom-call(f32[16,4,1440]{2,1,0:T(4,128)S(1)} %copy-done, f32[4,1440]{1,0:T(4,128)S(1)} %copy-done.4, f32[4,1440]{1,0:T(4,128)S(1)} %copy-done.5, s32[4,1440]{1,0:T(4,128)S(1)} %copy-done.6), custom_call_target="tpu_custom_call" | custom-call | tf_op jit(solution)/shard_map/pack_fields/pallas_call | solution.py:407
  5.4 2.6 %collective-permute-start.1 = (f32[684,128]{1,0:T(8,128)S(1)}, f32[684,128]{1,0:T(8,128)S(1)}, u32[]{:S(2)}, u32[]{:S(2)}) collective-permute-start(f32[684,128]{1,0:T(8,128)S(1)} %get-tuple-element.21), channel_id=1, source_target_pairs={{1,2},{2,1},{3,4},{4,3},{5,6},{6,5},{7,8},{8,7},{9,10},{10,9},{11,... | collective-permute-start | bytes 1050632 | tf_op jit(solution)/shard_map/ppermute | solution.py:405
  8.0 1.0 %copy-done.1 = s32[16,4,1440]{2,1,0:T(4,128)S(1)} copy-done((s32[16,4,1440]{2,1,0:T(4,128)S(1)}, s32[16,4,1440]{2,1,0:T(4,128)}, u32[]{:S(2)}) %copy-start.1) | copy-done | bytes 368664
  9.0 1.7 %pack_classes.1 = (s32[12,64,128]{2,1,0:T(8,128)S(1)}, s32[576,128]{1,0:T(8,128)}, s32[576,128]{1,0:T(8,128)}) custom-call(s32[16,4,1440]{2,1,0:T(4,128)S(1)} %copy-done.1), custom_call_target="tpu_custom_call" | custom-call | tf_op jit(solution)/shard_map/pack_classes/pallas_call | solution.py:423
  11.2 2.1 %collective-permute-done.1.far = f32[684,128]{1,0:T(8,128)S(1)} collective-permute-done((f32[684,128]{1,0:T(8,128)S(1)}, f32[684,128]{1,0:T(8,128)S(1)}, u32[]{:S(2)}, u32[]{:S(2)}) %collective-permute-start.1) | collective-permute-done | bytes 350240 | tf_op jit(solution)/shard_map/ppermute | solution.py:405
  13.3 0.7 %copy-done.7 = f32[32,72]{1,0:T(8,128)S(1)} copy-done((f32[32,72]{1,0:T(8,128)S(1)}, f32[32,72]{1,0:T(8,128)}, u32[]{:S(2)}) %copy-start.7) | copy-done | bytes 9240
  14.0 0.7 %copy-done.8 = s32[4]{0:T(128)S(1)} copy-done((s32[4]{0:T(128)S(1)}, s32[4]{0:T(128)}, u32[]{:S(2)}) %copy-start.8) | copy-done | bytes 40
  14.7 9.4 %forward.1 = (f32[8,128]{1,0:T(8,128)}, f32[12,48,128]{2,1,0:T(8,128)S(1)}, f32[12,192,128]{2,1,0:T(8,128)S(1)}) custom-call(f32[32,72]{1,0:T(8,128)S(1)} %copy-done.7, s32[4]{0:T(128)S(1)} %copy-done.8, f32[12,64,128]{2,1,0:T(8,128)S(1)} %get-tuple-element.16.own, f32[12,16,128]{2,1,0:T(8,128)S(1)} %get-tuple-element.17.own_maps, ...), custom_call_target="tpu_custom_call" | custom-call | tf_op jit(solution)/shard_map/forward/pallas_call | solution.py:441
  24.1 2.0 %collective-permute-start.8 = (f32[8,128]{1,0:T(8,128)}, f32[8,128]{1,0:T(8,128)}, u32[]{:S(2)}, u32[]{:S(2)}) collective-permute-start(f32[8,128]{1,0:T(8,128)} %get-tuple-element.25.own_sums), channel_id=1, source_target_pairs={{1,2},{2,1},{3,4},{4,3},{5,6},{6,5},{7,8},{8,7},{9,10},{10,9},{11,... | collective-permute-start | bytes 12296 | tf_op jit(solution)/shard_map/ppermute | solution.py:405
  26.1 3.3 %collective-permute-start.2 = (f32[8,128]{1,0:T(8,128)}, f32[8,128]{1,0:T(8,128)S(1)}, u32[]{:S(2)}, u32[]{:S(2)}) collective-permute-start(f32[8,128]{1,0:T(8,128)} %get-tuple-element.25.own_sums), channel_id=1, source_target_pairs={{0,1},{1,0},{2,3},{3,2},{4,5},{5,4},{6,7},{7,6},{8,9},{9,8},{10,11... | collective-permute-start | bytes 12296 | tf_op jit(solution)/shard_map/ppermute | solution.py:402
  29.5 0.7 %constant_dynamic-update-slice_fusion.4 = f32[128,128]{1,0:T(8,128)S(1)} fusion(f32[8,128]{1,0:T(8,128)} %get-tuple-element.25.own_sums), kind=kLoop, calls=%fused_computation.7 | loop fusion | bytes 8192
  30.2 1.5 %collective-permute-start.7 = (s32[576,128]{1,0:T(8,128)}, s32[576,128]{1,0:T(8,128)S(1)}, u32[]{:S(2)}, u32[]{:S(2)}) collective-permute-start(s32[576,128]{1,0:T(8,128)} %get-tuple-element.29), channel_id=1, source_target_pairs={{1,2},{2,1},{3,4},{4,3},{5,6},{6,5},{7,8},{8,7},{9,10},{10,9},{11,... | collective-permute-start | bytes 884744 | tf_op jit(solution)/shard_map/ppermute | solution.py:405
  31.7 0.7 %pad_maximum_fusion.2 = f32[16,128]{1,0:T(8,128)S(1)} fusion(f32[8,128]{1,0:T(8,128)S(1)} %collective-permute-done.2.near_sums, f32[8,128]{1,0:T(8,128)} %get-tuple-element.25.own_sums), kind=kLoop, calls=%fused_computation.8 | loop fusion | flops 2048 | bytes 16384 | tf_op jit(solution)/shard_map/concatenate | solution.py:460
  32.4 0.6 collective-permute-start.3
  33.0 4.4 %collective-permute-done.3 = f32[16,128]{1,0:T(8,128)S(1)} collective-permute-done((f32[16,128]{1,0:T(8,128)S(1)}, f32[16,128]{1,0:T(8,128)S(1)}, u32[]{:S(2)}, u32[]{:S(2)}) %collective-permute-start.3) | collective-permute-done | bytes 8224 | tf_op jit(solution)/shard_map/ppermute | solution.py:477
  37.4 0.7 %pad_maximum_fusion.1 = f32[32,128]{1,0:T(8,128)S(1)} fusion(f32[16,128]{1,0:T(8,128)S(1)} %collective-permute-done.3, f32[8,128]{1,0:T(8,128)S(1)} %collective-permute-done.2.near_sums, f32[8,128]{1,0:T(8,128)} %get-tuple-element.25.own_sums), kind=kLoop, calls=%fused_computation.2 | loop fusion | flops 8192 | bytes 32768 | tf_op jit(solution)/shard_map/concatenate | solution.py:478
  38.0 4.7 %collective-permute-start.4 = (f32[32,128]{1,0:T(8,128)S(1)}, f32[32,128]{1,0:T(8,128)S(1)}, u32[]{:S(2)}, u32[]{:S(2)}) collective-permute-start(f32[32,128]{1,0:T(8,128)S(1)} %pad_maximum_fusion.1), channel_id=1, source_target_pairs={{0,4},{1,5},{2,6},{3,7},{4,0},{5,1},{6,2},{7,3},{8,12},{9,13},{10,... | collective-permute-start | bytes 49160 | tf_op jit(solution)/shard_map/ppermute | solution.py:477
  42.8 1.7 %collective-permute-done.4 = f32[32,128]{1,0:T(8,128)S(1)} collective-permute-done((f32[32,128]{1,0:T(8,128)S(1)}, f32[32,128]{1,0:T(8,128)S(1)}, u32[]{:S(2)}, u32[]{:S(2)}) %collective-permute-start.4) | collective-permute-done | bytes 16416 | tf_op jit(solution)/shard_map/ppermute | solution.py:477
  44.5 0.7 %pad_maximum_fusion = f32[64,128]{1,0:T(8,128)S(1)} fusion(f32[32,128]{1,0:T(8,128)S(1)} %collective-permute-done.4, f32[16,128]{1,0:T(8,128)S(1)} %collective-permute-done.3, f32[8,128]{1,0:T(8,128)S(1)} %collective-permute-done.2.near_sums, f32[8,128]{1,0:T(8,128)} %get-tuple-element.25.own_sums), kind=kLoop, calls=%fused_computation | loop fusion | flops 24576 | bytes 65536 | tf_op jit(solution)/shard_map/concatenate | solution.py:478
  45.2 3.1 %collective-permute-start.5 = (f32[64,128]{1,0:T(8,128)S(1)}, f32[64,128]{1,0:T(8,128)S(1)}, u32[]{:S(2)}, u32[]{:S(2)}) collective-permute-start(f32[64,128]{1,0:T(8,128)S(1)} %pad_maximum_fusion), channel_id=1, source_target_pairs={{0,8},{1,9},{2,10},{3,11},{4,12},{5,13},{6,14},{7,15},{8,0},{9,1},... | collective-permute-start | bytes 98312 | tf_op jit(solution)/shard_map/ppermute | solution.py:477
  48.3 1.9 %collective-permute-done.5 = f32[64,128]{1,0:T(8,128)S(1)} collective-permute-done((f32[64,128]{1,0:T(8,128)S(1)}, f32[64,128]{1,0:T(8,128)S(1)}, u32[]{:S(2)}, u32[]{:S(2)}) %collective-permute-start.5) | collective-permute-done | bytes 32800 | tf_op jit(solution)/shard_map/ppermute | solution.py:477
  50.8 0.7 %slice.11 = f32[16,2,1]{2,1,0:T(2,128)} slice(f32[16,8,128]{2,1,0:T(8,128)S(1)} %bitcast.3), slice={[0:16], [0:2], [127:128]} | slice | bytes 256 | tf_op jit(solution)/shard_map/slice | solution.py:483
  51.5 1.4 %copy.13 = f32[16,2,1]{0,1,2:T(2,128)} copy(f32[16,2,1]{2,1,0:T(2,128)} %slice.11) | data formatting | bytes 256
  52.9 0.7 %copy.12 = f32[16,2,72]{2,0,1:T(8,128)S(1)} copy(f32[16,2,72]{2,1,0:T(2,128)} %slice.12) | data formatting | bytes 18432 | tf_op jit(solution)/shard_map/slice | solution.py:485
  53.6 0.8 %broadcast_compare_fusion = pred[2,16,2]{1,2,0:T(4,128)(4,1)S(1)} fusion(f32[16,2]{0,1:T(2,128)} %bitcast.4, f32[2]{0:T(128)} %add_convert_fusion), kind=kLoop, calls=%fused_computation.9 | loop fusion | flops 64 | bytes 200 | tf_op jit(solution)/shard_map/eq | solution.py:483
  54.3 0.7 %select_reduce_fusion = f32[2,72]{1,0:T(2,128)} fusion(f32[16,2,72]{2,0,1:T(8,128)S(1)} %copy.12, pred[2,16,2]{1,2,0:T(4,128)(4,1)S(1)} %broadcast_compare_fusion), kind=kLoop, calls=%fused_computation.1 | loop fusion | flops 9072 | bytes 9856 | tf_op jit(solution)/shard_map/reduce_sum | solution.py:484
  55.0 0.7 %copy-done.3 = f32[8,128]{1,0:T(8,128)S(1)} copy-done((f32[8,128]{1,0:T(8,128)S(1)}, f32[8,128]{1,0:T(8,128)}, u32[]{:S(2)}) %copy-start.3) | copy-done | bytes 4120
  55.7 8.0 %adjoint_part.1 = f32[4,1440]{1,0:T(4,128)} custom-call(f32[12,64,128]{2,1,0:T(8,128)S(1)} %get-tuple-element.16.own, f32[684,128]{1,0:T(8,128)S(1)} %collective-permute-done.near, f32[684,128]{1,0:T(8,128)S(1)} %collective-permute-done.1.far, f32[12,48,128]{2,1,0:T(8,128)S(1)} %get-tuple-element.26.maps, f32[12,192,128]{2,1,0:T(8,128)S(1)} %get-tuple-element.27.later, ...), custom_call_target="tpu_custom_call" | custom-call | tf_op jit(solution)/shard_map/adjoint_part/pallas_call | solution.py:462
  (23 shorter events, 1.7 us)
Async XLA Ops:
  0.6 1.0 %copy-start = (f32[16,4,1440]{2,1,0:T(4,128)S(1)}, f32[16,4,1440]{2,1,0:T(4,128)}, u32[]{:S(2)}) copy-start(f32[16,4,1440]{2,1,0:T(4,128)} %tracer.1) | copy-start | bytes 1105924
  1.6 0.7 %copy-start.4 = (f32[4,1440]{1,0:T(4,128)S(1)}, f32[4,1440]{1,0:T(4,128)}, u32[]{:S(2)}) copy-start(f32[4,1440]{1,0:T(4,128)} %mix.1) | copy-start | bytes 69124
  2.4 0.7 %copy-start.5 = (f32[4,1440]{1,0:T(4,128)S(1)}, f32[4,1440]{1,0:T(4,128)}, u32[]{:S(2)}) copy-start(f32[4,1440]{1,0:T(4,128)} %heading.1) | copy-start | bytes 69124
  3.1 0.7 %copy-start.6 = (s32[4,1440]{1,0:T(4,128)S(1)}, s32[4,1440]{1,0:T(4,128)}, u32[]{:S(2)}) copy-start(s32[4,1440]{1,0:T(4,128)} %depth.1) | copy-start | bytes 69124
  4.9 6.3 %collective-permute-start = (f32[684,128]{1,0:T(8,128)S(1)}, f32[684,128]{1,0:T(8,128)S(1)}, u32[]{:S(2)}, u32[]{:S(2)}) collective-permute-start(f32[684,128]{1,0:T(8,128)S(1)} %get-tuple-element.20), channel_id=1, source_target_pairs={{0,1},{1,0},{2,3},{3,2},{4,5},{5,4},{6,7},{7,6},{8,9},{9,8},{10,11... | collective-permute-start | bytes 1050632 | tf_op jit(solution)/shard_map/ppermute | solution.py:402
  5.4 7.9 %collective-permute-start.1 = (f32[684,128]{1,0:T(8,128)S(1)}, f32[684,128]{1,0:T(8,128)S(1)}, u32[]{:S(2)}, u32[]{:S(2)}) collective-permute-start(f32[684,128]{1,0:T(8,128)S(1)} %get-tuple-element.21), channel_id=1, source_target_pairs={{1,2},{2,1},{3,4},{4,3},{5,6},{6,5},{7,8},{8,7},{9,10},{10,9},{11,... | collective-permute-start | bytes 1050632 | tf_op jit(solution)/shard_map/ppermute | solution.py:405
  8.0 1.0 %copy-start.1 = (s32[16,4,1440]{2,1,0:T(4,128)S(1)}, s32[16,4,1440]{2,1,0:T(4,128)}, u32[]{:S(2)}) copy-start(s32[16,4,1440]{2,1,0:T(4,128)} %classes.1) | copy-start | bytes 1105924
  13.3 0.7 %copy-start.7 = (f32[32,72]{1,0:T(8,128)S(1)}, f32[32,72]{1,0:T(8,128)}, u32[]{:S(2)}) copy-start(f32[32,72]{1,0:T(8,128)} %weights.1) | copy-start | bytes 27652
  14.0 0.7 %copy-start.8 = (s32[4]{0:T(128)S(1)}, s32[4]{0:T(128)}, u32[]{:S(2)}) copy-start(s32[4]{0:T(128)} %band_of_row.1) | copy-start | bytes 52
  24.1 30.9 %collective-permute-start.8 = (f32[8,128]{1,0:T(8,128)}, f32[8,128]{1,0:T(8,128)}, u32[]{:S(2)}, u32[]{:S(2)}) collective-permute-start(f32[8,128]{1,0:T(8,128)} %get-tuple-element.25.own_sums), channel_id=1, source_target_pairs={{1,2},{2,1},{3,4},{4,3},{5,6},{6,5},{7,8},{8,7},{9,10},{10,9},{11,... | collective-permute-start | bytes 12296 | tf_op jit(solution)/shard_map/ppermute | solution.py:405
  26.1 5.5 %collective-permute-start.2 = (f32[8,128]{1,0:T(8,128)}, f32[8,128]{1,0:T(8,128)S(1)}, u32[]{:S(2)}, u32[]{:S(2)}) collective-permute-start(f32[8,128]{1,0:T(8,128)} %get-tuple-element.25.own_sums), channel_id=1, source_target_pairs={{0,1},{1,0},{2,3},{3,2},{4,5},{5,4},{6,7},{7,6},{8,9},{9,8},{10,11... | collective-permute-start | bytes 12296 | tf_op jit(solution)/shard_map/ppermute | solution.py:402
  30.1 24.9 %collective-permute-start.6 = (s32[576,128]{1,0:T(8,128)}, s32[576,128]{1,0:T(8,128)S(1)}, u32[]{:S(2)}, u32[]{:S(2)}) collective-permute-start(s32[576,128]{1,0:T(8,128)} %get-tuple-element.28), channel_id=1, source_target_pairs={{0,1},{1,0},{2,3},{3,2},{4,5},{5,4},{6,7},{7,6},{8,9},{9,8},{10,11... | collective-permute-start | bytes 884744 | tf_op jit(solution)/shard_map/ppermute | solution.py:402
  30.2 24.8 %collective-permute-start.7 = (s32[576,128]{1,0:T(8,128)}, s32[576,128]{1,0:T(8,128)S(1)}, u32[]{:S(2)}, u32[]{:S(2)}) collective-permute-start(s32[576,128]{1,0:T(8,128)} %get-tuple-element.29), channel_id=1, source_target_pairs={{1,2},{2,1},{3,4},{4,3},{5,6},{6,5},{7,8},{8,7},{9,10},{10,9},{11,... | collective-permute-start | bytes 884744 | tf_op jit(solution)/shard_map/ppermute | solution.py:405
  31.7 12.8 %copy-start.2 = (f32[8,128]{1,0:T(8,128)}, f32[8,128]{1,0:T(8,128)S(1)}, u32[]{:S(2)}) copy-start(f32[8,128]{1,0:T(8,128)S(1)} %collective-permute-done.2.near_sums) | copy-start | bytes 12292
  32.4 5.0 %collective-permute-start.3 = (f32[16,128]{1,0:T(8,128)S(1)}, f32[16,128]{1,0:T(8,128)S(1)}, u32[]{:S(2)}, u32[]{:S(2)}) collective-permute-start(f32[16,128]{1,0:T(8,128)S(1)} %pad_maximum_fusion.2), channel_id=1, source_target_pairs={{0,2},{1,3},{2,0},{3,1},{4,6},{5,7},{6,4},{7,5},{8,10},{9,11},{10,... | collective-permute-start | bytes 24584 | tf_op jit(solution)/shard_map/ppermute | solution.py:477
  38.0 6.5 %collective-permute-start.4 = (f32[32,128]{1,0:T(8,128)S(1)}, f32[32,128]{1,0:T(8,128)S(1)}, u32[]{:S(2)}, u32[]{:S(2)}) collective-permute-start(f32[32,128]{1,0:T(8,128)S(1)} %pad_maximum_fusion.1), channel_id=1, source_target_pairs={{0,4},{1,5},{2,6},{3,7},{4,0},{5,1},{6,2},{7,3},{8,12},{9,13},{10,... | collective-permute-start | bytes 49160 | tf_op jit(solution)/shard_map/ppermute | solution.py:477
  45.2 5.0 %collective-permute-start.5 = (f32[64,128]{1,0:T(8,128)S(1)}, f32[64,128]{1,0:T(8,128)S(1)}, u32[]{:S(2)}, u32[]{:S(2)}) collective-permute-start(f32[64,128]{1,0:T(8,128)S(1)} %pad_maximum_fusion), channel_id=1, source_target_pairs={{0,8},{1,9},{2,10},{3,11},{4,12},{5,13},{6,14},{7,15},{8,0},{9,1},... | collective-permute-start | bytes 98312 | tf_op jit(solution)/shard_map/ppermute | solution.py:477
  55.0 0.7 %copy-start.3 = (f32[8,128]{1,0:T(8,128)S(1)}, f32[8,128]{1,0:T(8,128)}, u32[]{:S(2)}) copy-start(f32[8,128]{1,0:T(8,128)} %copy-done.2) | copy-start | bytes 12292

commit v2 on v1

v2 whole, which is shorter than its diff:
```python
import functools

import jax
import jax.numpy as jnp
from jax import lax
from jax.experimental import pallas as pl
from jax.experimental.pallas import tpu as pltpu
from jax.sharding import PartitionSpec as P

STEPS = 3
vertical_mix = 0.05

LANES = 128
GHOST = 4
OWN = LANES - 2 * GHOST
HIGH_COUNT = 5
LOW_COUNT = 16
LOW_SHIFT = 4
GROUP = 3
VMEM_LIMIT = 50 * 1024 * 1024


def strip_of(row, j, lon_count):
    first = OWN * j - GHOST
    last = first + LANES
    if first < 0:
        return jnp.concatenate([row[:, first + lon_count :], row[:, :last]], axis=1)
    if last > lon_count:
        return jnp.concatenate([row[:, first:], row[:, : last - lon_count]], axis=1)
    return row[:, first:last]


def is_odd():
    return lax.rem(lax.axis_index("lat"), 2) == 1


def oriented(ref, t, odd):
    last = ref.shape[1] - 1
    order = level_order(ref.shape[0])
    up = jnp.concatenate([ref[k, t : t + 1, :] for k in order], axis=0)
    down = jnp.concatenate([ref[k, last - t : last - t + 1, :] for k in order], axis=0)
    return jnp.where(odd, down, up)


def pack_fields(tracer, mix, heading, depth, own, own_maps, near, far):
    levels, rows, lon_count = tracer.shape
    strips = lon_count // OWN
    odd = is_odd()
    for t in range(rows):
        field = oriented(tracer, t, odd)
        for j in range(strips):
            strip = strip_of(field, j, lon_count)
            own[j, t * levels : (t + 1) * levels, :] = strip
            if t < STEPS:
                at = (j * STEPS + STEPS - 1 - t) * levels
                far[at : at + levels, :] = strip
            if t > 0:
                at = (j * STEPS + rows - 1 - t) * levels
                near[at : at + levels, :] = strip
    base = strips * STEPS * levels
    for a, ref in enumerate((mix, heading, depth)):
        field = ref[...].astype(jnp.float32)
        flipped = jnp.concatenate([field[r : r + 1] for r in reversed(range(rows))], axis=0)
        up = jnp.where(odd, flipped, field)
        down = jnp.where(odd, field, flipped)
        for j in range(strips):
            own_maps[j, a * 4 : a * 4 + 4, :] = strip_of(up, j, lon_count)
            strip = strip_of(down, j, lon_count)
            at = base + (3 * j + a) * STEPS
            near[at : at + STEPS, :] = strip[:STEPS]
            far[at : at + STEPS, :] = strip[1:]
    own_maps[:, 12:, :] = jnp.zeros_like(own_maps[:, 12:, :])


def pack_classes(classes, weights, band_of_row, own, near, far, scales):
    levels, rows, lon_count = classes.shape
    strips = lon_count // OWN
    odd = is_odd()
    for t in range(rows):
        field = oriented(classes, t, odd)
        for j in range(strips):
            strip = strip_of(field, j, lon_count)
            own[j, t * levels : (t + 1) * levels, :] = strip
            if t < STEPS:
                at = (j * STEPS + STEPS - 1 - t) * levels
                far[at : at + levels, :] = strip
            if t > 0:
                at = (j * STEPS + rows - 1 - t) * levels
                near[at : at + levels, :] = strip
    class_count = weights.shape[1]
    label = lax.broadcasted_iota(jnp.int32, (1, LANES), 1)
    scale_rows, band_rows = [], []
    for pair in range(2):
        band = band_of_row[jnp.where(odd, 3 - 2 * pair, 2 * pair)]
        scale = weights[pl.ds(band, 1), :]
        scale_rows.append(jnp.concatenate([scale, jnp.zeros((1, LANES - class_count), jnp.float32)], axis=1))
        band_rows.append(jnp.where(label == LANES - 1, band.astype(jnp.float32), 0.0))
    scales[...] = jnp.concatenate(
        scale_rows + band_rows + [jnp.zeros((4, LANES), jnp.float32)], axis=0
    )


def east(x):
    return pltpu.roll(x, LANES - 1, 1)


def west(x):
    return pltpu.roll(x, 1, 1)


MAP_FIELDS = 10


def level_order(levels):
    half = levels // 2
    return [2 * (i % half) + i // half for i in range(levels)]


class Coefficients:
    blocks = {
        "wet": 0, "east_open": 1, "west_open": 2, "north_open": 3,
        "east_mix": 4, "west_mix": 5, "north_mix": 6,
        "east_dir": 7, "west_dir": 8, "north_dir": 9,
    }

    def __init__(self, maps, j, levels):
        order = lax.broadcasted_iota(jnp.int32, (levels, LANES), 0)
        half = levels // 2
        self.level = (2 * (order & (half - 1)) + jnp.where(order < half, 0, 1)).astype(jnp.float32)
        self.levels = levels
        self.maps = maps
        self.j = j
        self.cache = {}

    def row(self, kind, t):
        at = 16 * self.blocks[kind] + t + STEPS
        return jnp.broadcast_to(self.maps[self.j, at : at + 1, :], (self.levels, LANES))

    def get(self, kind, t):
        if (kind, t) not in self.cache:
            side, _, what = kind.partition("_")
            if kind == "column":
                value = jnp.where(self.level + 1.0 < self.row("wet", t), vertical_mix, 0.0)
            elif kind == "wet" or what == "open":
                value = self.level < self.row(kind, t)
            else:
                value = jnp.where(self.get(side + "_open", t), self.row(kind, t), 0.0)
            self.cache[kind, t] = value
        return self.cache[kind, t]


def column(field, coefficient):
    half = field.shape[0] // 2
    even, odd = field[:half], field[half:]
    after_even = coefficient[:half] * (odd - even)
    after_odd = coefficient[half:] * (pltpu.roll(even, half - 1, 0) - odd)
    return jnp.concatenate([after_even - pltpu.roll(after_odd, 1, 0), after_odd - after_even], axis=0)


def gaps(field, rows):
    to_east = {t: east(field[t]) - field[t] for t in rows}
    to_west = {t: west(field[t]) - field[t] for t in rows}
    to_north = {t: field[t + 1] - field[t] for t in range(rows[0] - 1, rows[-1] + 1)}
    return to_east, to_west, to_north


def spread(coef, kind, steps, rows):
    to_east, to_west, to_north = steps
    flux = {t: coef.get("north_" + kind, t) * to_north[t] for t in range(rows[0] - 1, rows[-1] + 1)}
    return {
        t: coef.get("east_" + kind, t) * to_east[t]
        + coef.get("west_" + kind, t) * to_west[t]
        + (flux[t] - flux[t - 1])
        for t in rows
    }


def advance(coef, field, steps, rows):
    moved = spread(coef, "mix", steps, rows)
    return {t: field[t] + moved[t] + column(field[t], coef.get("column", t)) for t in rows}


def face_maps(own_maps, near, far, maps, base):
    strips = own_maps.shape[0]
    count, edge = lax.axis_size("lat"), lax.axis_index("lat")
    keep = jnp.where(jnp.logical_and(edge != 0, edge != count - 1), 1.0, 0.0)

    def north(x):
        return pltpu.roll(x, 15, 0)

    for j in range(strips):
        whole = []
        for a in range(3):
            at = base + (3 * j + a) * STEPS
            low = far[at : at + STEPS, :]
            if a == 2:
                low = low * keep
            high = near[at : at + STEPS, :]
            whole.append(jnp.concatenate([low, own_maps[j, 4 * a : 4 * a + 4, :], high, high, high], axis=0))
        mix, heading, depth = whole
        blocks = [depth] + [jnp.minimum(depth, f(depth)) for f in (east, west, north)]
        blocks += [0.5 * (x + f(x)) for x in (mix, heading) for f in (east, west, north)]
        for i, block in enumerate(blocks):
            maps[j, 16 * i : 16 * i + 16, :] = block


def class_hits(value, label, levels):
    top = value.astype(jnp.bfloat16)
    bottom = (value - top.astype(jnp.float32)).astype(jnp.bfloat16)
    high = (label >> LOW_SHIFT).astype(jnp.float32).astype(jnp.bfloat16)
    low = (label & (LOW_COUNT - 1)).astype(jnp.float32).astype(jnp.bfloat16)
    none = jnp.zeros((levels, LANES), jnp.bfloat16)
    one = jnp.ones((levels, LANES), jnp.bfloat16)
    picks = [high == jnp.bfloat16(h) for h in range(HIGH_COUNT)]
    left = [jnp.where(p, part, none) for part in (top, bottom) for p in picks]
    right = [jnp.where(low == jnp.bfloat16(l), one, none) for l in range(LOW_COUNT)]
    return jnp.concatenate(left, axis=0), jnp.concatenate(right, axis=0)


def forward(scales, own, own_maps, near, far, classes, sums, maps, later, grams):
    strips, _, _ = own.shape
    levels = own.shape[1] // 4
    face_maps(own_maps, near, far, maps, strips * STEPS * levels)
    grams[...] = jnp.zeros_like(grams)
    lane = lax.broadcasted_iota(jnp.int32, (levels, LANES), 1)
    inner = jnp.logical_and(lane >= GHOST, lane < LANES - GHOST)

    def some_strips(i, carry):
        group = [i * GROUP + u for u in range(GROUP)]
        coefs = [Coefficients(maps, j, levels) for j in group]
        fields, tangents = [], [None] * GROUP
        for j in group:
            field = {}
            for s in range(STEPS):
                at = pl.multiple_of((j * STEPS + s) * levels, levels)
                field[s - STEPS] = far[pl.ds(at, levels), :]
                field[4 + s] = near[pl.ds(at, levels), :]
            for t in range(4):
                field[t] = own[j, t * levels : (t + 1) * levels, :]
            fields.append(field)
        for n in range(STEPS):
            rows = list(range(n + 1 - STEPS, 4 + STEPS - n - 1))
            for u, j in enumerate(group):
                steps = gaps(fields[u], rows)
                pushed = spread(coefs[u], "dir", steps, rows)
                if n > 0:
                    carried = advance(coefs[u], tangents[u], gaps(tangents[u], rows), rows)
                    pushed = {t: pushed[t] + carried[t] for t in rows}
                tangents[u] = pushed
                if n + 1 < STEPS:
                    fields[u] = advance(coefs[u], fields[u], steps, rows)
                    for t in range(-1, 5):
                        at = (n * 6 + t + 1) * levels
                        later[j, at : at + levels, :] = fields[u][t]
        for pair in range(2):
            lefts, rights = [], []
            for u, j in enumerate(group):
                for t in (2 * pair, 2 * pair + 1):
                    chosen = jnp.logical_and(inner, coefs[u].get("wet", t))
                    value = jnp.where(chosen, tangents[u][t], 0.0)
                    left, right = class_hits(value, classes[j, t * levels : (t + 1) * levels, :], levels)
                    lefts.append(left)
                    rights.append(right)
            grams[pair] += lax.dot_general(
                jnp.concatenate(lefts, axis=1),
                jnp.concatenate(rights, axis=1),
                (((1,), (1,)), ((), ())),
                preferred_element_type=jnp.float32,
            )
        return carry

    lax.fori_loop(0, strips // GROUP, some_strips, 0)

    width = LOW_COUNT * levels
    own_level = lax.broadcasted_iota(jnp.int32, (levels, width), 0)
    other_level = lax.broadcasted_iota(jnp.int32, (levels, width), 1) & (levels - 1)
    diagonal = own_level == other_level
    sheets = []
    for pair in range(2):
        for h in range(HIGH_COUNT):
            both = (
                grams[pair, h * levels : (h + 1) * levels, :]
                + grams[pair, (HIGH_COUNT + h) * levels : (HIGH_COUNT + h + 1) * levels, :]
            )
            sheets.append(jnp.sum(jnp.where(diagonal, both, 0.0), axis=0, keepdims=True))
        sheets.append(jnp.zeros((8 - HIGH_COUNT, width), jnp.float32))
    rest = jnp.concatenate(sheets, axis=0)
    parts = []
    for _ in range(3):
        part = rest.astype(jnp.bfloat16)
        rest = rest - part.astype(jnp.float32)
        parts.append(part)
    at_low = lax.broadcasted_iota(jnp.int32, (width, LANES), 0) >> (levels.bit_length() - 1)
    of_low = lax.broadcasted_iota(jnp.int32, (width, LANES), 1) & (LOW_COUNT - 1)
    gather = jnp.where(at_low == of_low, 1.0, 0.0).astype(jnp.bfloat16)
    added = jnp.dot(jnp.concatenate(parts, axis=0), gather, preferred_element_type=jnp.float32)
    added = (added[32:48] + added[16:32]) + added[0:16]
    here = lax.broadcasted_iota(jnp.int32, (8, LANES), 0)
    label = lax.broadcasted_iota(jnp.int32, (8, LANES), 1)
    totals = [
        jnp.sum(
            jnp.where(here == (label >> LOW_SHIFT), added[8 * p : 8 * p + 8], 0.0), axis=0, keepdims=True
        )
        for p in range(2)
    ]
    finish_sums(scales, totals, sums)


def finish_sums(scales, totals, sums):
    weighted = [scales[p : p + 1, :] * totals[p] for p in range(2)]
    sums[...] = jnp.concatenate(
        [totals[p] + scales[2 + p : 3 + p, :] for p in range(2)]
        + weighted
        + [jnp.zeros((4, LANES), jnp.float32)],
        axis=0,
    )


def adjoint_part(
    own, near, far, maps, later, own_classes, near_classes, far_classes,
    own_sums, near_sums, far_sums, gradient, strips_out,
):
    strips = own.shape[0]
    levels = own.shape[1] // 4
    rows, lon_count = gradient.shape
    odd = is_odd()

    def some_strips(i, carry):
        group = [i * GROUP + u for u in range(GROUP)]
        coefs = [Coefficients(maps, j, levels) for j in group]
        fields, adjoints = [], []
        for u, j in enumerate(group):
            field = [{t: own[j, t * levels : (t + 1) * levels, :] for t in range(4)}]
            at = pl.multiple_of((j * STEPS + STEPS - 1) * levels, levels)
            field[0][-1] = far[pl.ds(at, levels), :]
            at = pl.multiple_of(j * STEPS * levels, levels)
            field[0][4] = near[pl.ds(at, levels), :]
            for n in range(STEPS - 1):
                field.append(
                    {t: later[j, (n * 6 + t + 1) * levels : (n * 6 + t + 2) * levels, :] for t in range(-1, 5)}
                )
            fields.append(field)
            adjoint = {}
            for t in range(-STEPS, 4 + STEPS):
                if t < 0:
                    at = pl.multiple_of((j * STEPS + t + STEPS) * levels, levels)
                    label = far_classes[pl.ds(at, levels), :]
                    source, row = far_sums, 2 + (-1 - t) // 2
                elif t < 4:
                    label = own_classes[j, t * levels : (t + 1) * levels, :]
                    source, row = own_sums, 2 + t // 2
                else:
                    at = pl.multiple_of((j * STEPS + t - 4) * levels, levels)
                    label = near_classes[pl.ds(at, levels), :]
                    source, row = near_sums, 2 + (7 - t) // 2
                table = jnp.broadcast_to(source[row : row + 1, :], (8, LANES))
                value = jnp.concatenate(
                    [jnp.take_along_axis(table, label[k : k + 8, :], axis=1) for k in range(0, levels, 8)],
                    axis=0,
                )
                adjoint[t] = jnp.where(coefs[u].get("wet", t), value, 0.0)
            adjoints.append(adjoint)
        east_total = [{t: 0.0 for t in range(4)} for _ in group]
        north_total = [{t: 0.0 for t in range(-1, 4)} for _ in group]
        for n in reversed(range(STEPS)):
            rows_out = list(range(-n, 4 + n))
            for u, j in enumerate(group):
                steps = gaps(adjoints[u], rows_out)
                field = fields[u][n]
                for t in range(4):
                    gap = east(field[t]) - field[t]
                    east_total[u][t] = east_total[u][t] + gap * steps[0][t]
                for t in range(-1, 4):
                    gap = field[t + 1] - field[t]
                    north_total[u][t] = north_total[u][t] + gap * steps[2][t]
                if n > 0:
                    adjoints[u] = advance(coefs[u], adjoints[u], steps, rows_out)
        for u, j in enumerate(group):
            north_part = {
                t: jnp.where(coefs[u].get("north_open", t), north_total[u][t], 0.0) for t in range(-1, 4)
            }
            out = []
            for t in range(4):
                part = jnp.where(coefs[u].get("east_open", t), east_total[u][t], 0.0)
                out.append(jnp.sum(part, axis=0, keepdims=True))
            part = jnp.concatenate(out, axis=0)
            part = part + west(part)
            north_part = [
                jnp.sum(north_part[t] + north_part[t - 1], axis=0, keepdims=True) for t in range(4)
            ]
            strips_out[j, 0:4, :] = -0.5 * (part + jnp.concatenate(north_part, axis=0))
        return carry

    lax.fori_loop(0, strips // GROUP, some_strips, 0)
    up = jnp.concatenate([strips_out[j, 0:4, GHOST : LANES - GHOST] for j in range(strips)], axis=1)
    down = jnp.concatenate([up[t : t + 1] for t in reversed(range(4))], axis=0)
    gradient[...] = jnp.where(odd, down, up)


def near_pairs(count):
    return [(i, i ^ 1) for i in range(count)]


def far_pairs(members, count):
    pairs = []
    for m in range(members):
        for i in range(1, count - 1, 2):
            pairs += [(m * count + i, m * count + i + 1), (m * count + i + 1, m * count + i)]
        for i in (0, count - 1):
            pairs.append((m * count + i, (m ^ 1) * count + i))
    return pairs


def vmem(count):
    return [pl.BlockSpec(memory_space=pltpu.VMEM)] * count


def body(tracer, diffusivity, direction, column_depth, density_class, band_of_row, weights):
    levels, rows, lon_count = tracer.shape
    strips = lon_count // OWN
    count = lax.axis_size("lat")
    members = lax.axis_size("members")
    params = pltpu.CompilerParams(vmem_limit_bytes=VMEM_LIMIT)
    f32, i32 = jnp.float32, jnp.int32
    halo = strips * STEPS * levels
    payload = halo + strips * 9

    def to_near(x):
        return lax.ppermute(x, "lat", near_pairs(count))

    def to_far(x):
        return lax.ppermute(x, ("members", "lat"), far_pairs(members, count))

    own, own_maps, near_out, far_out = pl.pallas_call(
        pack_fields,
        name="pack_fields",
        out_shape=(
            jax.ShapeDtypeStruct((strips, rows * levels, LANES), f32),
            jax.ShapeDtypeStruct((strips, 16, LANES), f32),
            jax.ShapeDtypeStruct((payload, LANES), f32),
            jax.ShapeDtypeStruct((payload, LANES), f32),
        ),
        in_specs=vmem(4),
        out_specs=tuple(vmem(4)),
        compiler_params=params,
    )(tracer, diffusivity, direction, column_depth)
    far = to_far(far_out)
    near = to_near(near_out)

    own_classes, near_classes_out, far_classes_out, scales = pl.pallas_call(
        pack_classes,
        name="pack_classes",
        out_shape=(
            jax.ShapeDtypeStruct((strips, rows * levels, LANES), i32),
            jax.ShapeDtypeStruct((halo, LANES), i32),
            jax.ShapeDtypeStruct((halo, LANES), i32),
            jax.ShapeDtypeStruct((8, LANES), f32),
        ),
        in_specs=vmem(2) + [pl.BlockSpec(memory_space=pltpu.SMEM)],
        out_specs=tuple(vmem(4)),
        compiler_params=params,
    )(density_class, weights, band_of_row)
    near_classes_out, far_classes_out, near, far = lax.optimization_barrier(
        (near_classes_out, far_classes_out, near, far)
    )
    far_classes = to_far(far_classes_out)
    near_classes = to_near(near_classes_out)

    sums, maps, later = pl.pallas_call(
        forward,
        name="forward",
        out_shape=(
            jax.ShapeDtypeStruct((8, LANES), f32),
            jax.ShapeDtypeStruct((strips, 16 * MAP_FIELDS, LANES), f32),
            jax.ShapeDtypeStruct((strips, 12 * levels, LANES), f32),
        ),
        in_specs=vmem(6),
        out_specs=tuple(vmem(3)),
        scratch_shapes=[
            pltpu.VMEM((2, 2 * HIGH_COUNT * levels, LOW_COUNT * levels), f32),
        ],
        compiler_params=params,
    )(scales, own, own_maps, near, far, own_classes)

    near_sums = to_near(sums)
    far_sums = to_far(sums)
    gathered = jnp.concatenate([sums, near_sums], axis=0)

    gradient = pl.pallas_call(
        adjoint_part,
        name="adjoint_part",
        out_shape=jax.ShapeDtypeStruct((rows, lon_count), f32),
        in_specs=vmem(11),
        out_specs=pl.BlockSpec(memory_space=pltpu.VMEM),
        scratch_shapes=[pltpu.VMEM((strips, 8, LANES), f32)],
        compiler_params=params,
    )(own, near, far, maps, later, own_classes, near_classes, far_classes, sums, near_sums, far_sums)

    step = 2
    while step < count:
        other = lax.ppermute(gathered, "lat", [(i, i ^ step) for i in range(count)])
        gathered = jnp.concatenate([gathered, other], axis=0)
        step *= 2
    band_own = weights.shape[0] // count
    finished = gathered.reshape(count, 8, LANES)[:, :2]
    wanted = lax.axis_index("lat") * band_own + jnp.arange(band_own)
    hits = finished[None, :, :, LANES - 1] == wanted[:, None, None].astype(f32)
    binned = jnp.sum(
        jnp.where(hits[..., None], finished[None, :, :, : weights.shape[1]], 0.0), axis=(1, 2)
    )
    return binned, gradient


def solution(mesh):
    placed = (
        P(None, ("members", "lat"), None),
        P("lat", None),
        P(("members", "lat"), None),
        P("lat", None),
        P(None, ("members", "lat"), None),
        P("lat"),
        P(),
    )
    return jax.shard_map(
        body,
        mesh=mesh,
        in_specs=placed,
        out_specs=(P(("members", "lat"), None), P(("members", "lat"), None)),
        check_vma=False,
    )
```

time: 64.4 us -> 47.4 us (0.74)
  Pallas kernels: 20.1 us -> 10.5 us
  local copies, waits for them, and re-layouts: 10.3 us -> 6.79 us
  other arithmetic: 3.98 us -> 0.76 us
    pallas_call x1, Pallas kernels: 9.43 us -> 3.75 us  [body(): pl.pallas_call(forward, name='forward', out_shape=(jax.ShapeDtypeStruct((...]
    pallas_call x1, Pallas kernels: 7.95 us -> 4.56 us  [body(): pl.pallas_call(adjoint_part, name='adjoint_part', out_shape=jax.ShapeDtyp...]
    unnamed x23 -> x21, local copies, waits for them, and re-layouts: 8.27 us -> 6.7 us
    concatenate x2, other arithmetic: 1.35 us -> 0.01 us  [body(): gathered = jnp.concatenate([gathered, other], axis=0)]
    slice x2, local copies, waits for them, and re-layouts: 1.33 us -> 0.01 us  [body(): finished[None, :, :, :weights.shape[1]]]
    ppermute x3, waiting for transfers between devices: 2.11 us -> 1.29 us  [to_far(): return lax.ppermute(x, ('members', 'lat'), far_pairs(members, count))]
    eq x1, other arithmetic: 0.75 us -> 0.07 us  [body(): hits = finished[None, :, :, LANES - 1] == wanted[:, None, None].astype(f32)]
    concatenate x1, other arithmetic: 0.68 us -> 0.01 us  [body(): gathered = jnp.concatenate([sums, near_sums], axis=0)]
  transfers between devices with their start and end apart: 9 -> 9, of which waited for: 4 -> 4; matrix products, arithmetic and copies ran while one was open for 13% -> 2% of each run, Pallas kernels for 3% -> 4%
where the time goes in v2:
time: 47.4 us; the launch traced here: 46.9 us
  starting transfers between devices  18.4 us (39%)
  Pallas kernels  10.5 us (22%)
  waiting for transfers between devices  9.77 us (21%)
  local copies, waits for them, and re-layouts  6.79 us (14%)
  other arithmetic  0.76 us (2%)
  between operations  0.69 us (1%)
    ppermute x3, waiting for transfers between devices, body(): other = lax.ppermute(gathered, 'lat', [(i, i ^ step) for i in range(count)])  8.47 us
    ppermute x3, starting transfers between devices, body(): other = lax.ppermute(gathered, 'lat', [(i, i ^ step) for i in range(count)])  8.42 us
    unnamed x21, local copies, waits for them, and re-layouts  6.7 us
    ppermute x3, starting transfers between devices, to_far(): return lax.ppermute(x, ('members', 'lat'), far_pairs(members, count))  6.07 us
    pallas_call x1, Pallas kernels, body(): pl.pallas_call(adjoint_part, name='adjoint_part', out_shape=jax.ShapeDtyp...  4.56 us
    ppermute x3, starting transfers between devices, to_near(): return lax.ppermute(x, 'lat', near_pairs(count))  3.87 us
    pallas_call x1, Pallas kernels, body(): pl.pallas_call(forward, name='forward', out_shape=(jax.ShapeDtypeStruct((...  3.75 us
    pallas_call x1, Pallas kernels, body(): pl.pallas_call(pack_classes, name='pack_classes', out_shape=(jax.ShapeDty...  1.65 us
  transfers between devices with their start and end apart: 9, of which 4 were waited for; matrix products, arithmetic and copies ran while one was open for 2% of the time, Pallas kernels for 4%

profile of v2, /device:TPU:0, one launch (start us, length us, event | category | flops | bytes accessed | tf_op | source)
XLA Modules:
  0.0 46.9 jit_solution(453259718922460102)
XLA Ops:
  0.6 1.0 %copy-done.1 = f32[16,4,1440]{2,1,0:T(4,128)S(1)} copy-done((f32[16,4,1440]{2,1,0:T(4,128)S(1)}, f32[16,4,1440]{2,1,0:T(4,128)}, u32[]{:S(2)}) %copy-start.1) | copy-done | bytes 368664
  1.6 0.7 %copy-done.3 = f32[4,1440]{1,0:T(4,128)S(1)} copy-done((f32[4,1440]{1,0:T(4,128)S(1)}, f32[4,1440]{1,0:T(4,128)}, u32[]{:S(2)}) %copy-start.3) | copy-done | bytes 23064
  2.4 0.7 %copy-done.4 = f32[4,1440]{1,0:T(4,128)S(1)} copy-done((f32[4,1440]{1,0:T(4,128)S(1)}, f32[4,1440]{1,0:T(4,128)}, u32[]{:S(2)}) %copy-start.4) | copy-done | bytes 23064
  3.1 0.7 %copy-done.5 = s32[4,1440]{1,0:T(4,128)S(1)} copy-done((s32[4,1440]{1,0:T(4,128)S(1)}, s32[4,1440]{1,0:T(4,128)}, u32[]{:S(2)}) %copy-start.5) | copy-done | bytes 23064
  3.8 0.6 %pack_fields.1 = (f32[12,64,128]{2,1,0:T(8,128)S(1)}, f32[12,16,128]{2,1,0:T(8,128)S(1)}, f32[684,128]{1,0:T(8,128)S(1)}, f32[684,128]{1,0:T(8,128)S(1)}) custom-call(f32[16,4,1440]{2,1,0:T(4,128)S(1)} %copy-done.1, f32[4,1440]{1,0:T(4,128)S(1)} %copy-done.3, f32[4,1440]{1,0:T(4,128)S(1)} %copy-done.4, s32[4,1440]{1,0:T(4,128)S(1)} %copy-done.5), custom_call_target="tpu_custom_call" | custom-call | tf_op jit(solution)/shard_map/pack_fields/pallas_call | solution.py:434
  4.4 0.5 %collective-permute-start = (f32[684,128]{1,0:T(8,128)S(1)}, f32[684,128]{1,0:T(8,128)S(1)}, u32[]{:S(2)}, u32[]{:S(2)}) collective-permute-start(f32[684,128]{1,0:T(8,128)S(1)} %get-tuple-element.22), channel_id=1, source_target_pairs={{0,1},{1,0},{2,3},{3,2},{4,5},{5,4},{6,7},{7,6},{8,9},{9,8},{10,11... | collective-permute-start | bytes 1050632 | tf_op jit(solution)/shard_map/ppermute | solution.py:429
  4.9 2.6 %collective-permute-start.1 = (f32[684,128]{1,0:T(8,128)S(1)}, f32[684,128]{1,0:T(8,128)S(1)}, u32[]{:S(2)}, u32[]{:S(2)}) collective-permute-start(f32[684,128]{1,0:T(8,128)S(1)} %get-tuple-element.23), channel_id=1, source_target_pairs={{1,2},{2,1},{3,4},{4,3},{5,6},{6,5},{7,8},{8,7},{9,10},{10,9},{11,... | collective-permute-start | bytes 1050632 | tf_op jit(solution)/shard_map/ppermute | solution.py:432
  7.5 1.0 %copy-done.2 = s32[16,4,1440]{2,1,0:T(4,128)S(1)} copy-done((s32[16,4,1440]{2,1,0:T(4,128)S(1)}, s32[16,4,1440]{2,1,0:T(4,128)}, u32[]{:S(2)}) %copy-start.2) | copy-done | bytes 368664
  8.5 0.7 %copy-done.6 = f32[32,72]{1,0:T(8,128)S(1)} copy-done((f32[32,72]{1,0:T(8,128)S(1)}, f32[32,72]{1,0:T(8,128)}, u32[]{:S(2)}) %copy-start.6) | copy-done | bytes 9240
  9.2 0.7 %copy-done.7 = s32[4]{0:T(128)S(1)} copy-done((s32[4]{0:T(128)S(1)}, s32[4]{0:T(128)}, u32[]{:S(2)}) %copy-start.7) | copy-done | bytes 40
  9.9 1.7 %pack_classes.1 = (s32[12,64,128]{2,1,0:T(8,128)S(1)}, s32[576,128]{1,0:T(8,128)}, s32[576,128]{1,0:T(8,128)S(1)}, f32[8,128]{1,0:T(8,128)S(1)}) custom-call(s32[16,4,1440]{2,1,0:T(4,128)S(1)} %copy-done.2, f32[32,72]{1,0:T(8,128)S(1)} %copy-done.6, s32[4]{0:T(128)S(1)} %copy-done.7), custom_call_target="tpu_custom_call" | custom-call | tf_op jit(solution)/shard_map/pack_classes/pallas_call | solution.py:450
  11.5 0.0 collective-permute-done.near
  11.5 1.3 %collective-permute-done.1.far = f32[684,128]{1,0:T(8,128)S(1)} collective-permute-done((f32[684,128]{1,0:T(8,128)S(1)}, f32[684,128]{1,0:T(8,128)S(1)}, u32[]{:S(2)}, u32[]{:S(2)}) %collective-permute-start.1) | collective-permute-done | bytes 350240 | tf_op jit(solution)/shard_map/ppermute | solution.py:432
  12.8 3.8 %forward.1 = (f32[8,128]{1,0:T(8,128)S(1)}, f32[12,160,128]{2,1,0:T(8,128)S(1)}, f32[12,192,128]{2,1,0:T(8,128)S(1)}) custom-call(f32[8,128]{1,0:T(8,128)S(1)} %get-tuple-element.17.scales, f32[12,64,128]{2,1,0:T(8,128)S(1)} %get-tuple-element.18.own, f32[12,16,128]{2,1,0:T(8,128)S(1)} %get-tuple-element.19.own_maps, ...), custom_call_target="tpu_custom_call" | custom-call | tf_op jit(solution)/shard_map/forward/pallas_call | solution.py:469
  16.6 1.0 %copy-done = f32[12,192,128]{2,1,0:T(8,128)} copy-done((f32[12,192,128]{2,1,0:T(8,128)}, f32[12,192,128]{2,1,0:T(8,128)S(1)}, u32[]{:S(2)}) %copy-start) | copy-done | bytes 1179672
  17.6 2.0 %collective-permute-start.8 = (f32[8,128]{1,0:T(8,128)S(1)}, f32[8,128]{1,0:T(8,128)S(1)}, u32[]{:S(2)}, u32[]{:S(2)}) collective-permute-start(f32[8,128]{1,0:T(8,128)S(1)} %get-tuple-element.27.own_sums), channel_id=1, source_target_pairs={{1,2},{2,1},{3,4},{4,3},{5,6},{6,5},{7,8},{8,7},{9,10},{10,9},{11,... | collective-permute-start | bytes 12296 | tf_op jit(solution)/shard_map/ppermute | solution.py:432
  19.6 3.3 %collective-permute-start.2 = (f32[8,128]{1,0:T(8,128)S(1)}, f32[8,128]{1,0:T(8,128)S(1)}, u32[]{:S(2)}, u32[]{:S(2)}) collective-permute-start(f32[8,128]{1,0:T(8,128)S(1)} %get-tuple-element.27.own_sums), channel_id=1, source_target_pairs={{0,1},{1,0},{2,3},{3,2},{4,5},{5,4},{6,7},{7,6},{8,9},{9,8},{10,11... | collective-permute-start | bytes 12296 | tf_op jit(solution)/shard_map/ppermute | solution.py:429
  23.0 0.0 collective-permute-start.6
  23.0 1.5 %collective-permute-start.7 = (s32[576,128]{1,0:T(8,128)S(1)}, s32[576,128]{1,0:T(8,128)S(1)}, u32[]{:S(2)}, u32[]{:S(2)}) collective-permute-start(s32[576,128]{1,0:T(8,128)S(1)} %get-tuple-element.31), channel_id=1, source_target_pairs={{1,2},{2,1},{3,4},{4,3},{5,6},{6,5},{7,8},{8,7},{9,10},{10,9},{11,... | collective-permute-start | bytes 884744 | tf_op jit(solution)/shard_map/ppermute | solution.py:432
  24.5 0.6 %collective-permute-start.3 = (f32[16,128]{1,0:T(8,128)S(1)}, f32[16,128]{1,0:T(8,128)S(1)}, u32[]{:S(2)}, u32[]{:S(2)}) collective-permute-start(f32[16,128]{1,0:T(8,128)S(1)} %pad_maximum_fusion.2), channel_id=1, source_target_pairs={{0,2},{1,3},{2,0},{3,1},{4,6},{5,7},{6,4},{7,5},{8,10},{9,11},{10,... | collective-permute-start | bytes 24584 | tf_op jit(solution)/shard_map/ppermute | solution.py:501
  25.1 4.9 %collective-permute-done.3 = f32[16,128]{1,0:T(8,128)S(1)} collective-permute-done((f32[16,128]{1,0:T(8,128)S(1)}, f32[16,128]{1,0:T(8,128)S(1)}, u32[]{:S(2)}, u32[]{:S(2)}) %collective-permute-start.3) | collective-permute-done | bytes 8224 | tf_op jit(solution)/shard_map/ppermute | solution.py:501
  30.0 4.7 %collective-permute-start.4 = (f32[32,128]{1,0:T(8,128)S(1)}, f32[32,128]{1,0:T(8,128)S(1)}, u32[]{:S(2)}, u32[]{:S(2)}) collective-permute-start(f32[32,128]{1,0:T(8,128)S(1)} %pad_maximum_fusion.1), channel_id=1, source_target_pairs={{0,4},{1,5},{2,6},{3,7},{4,0},{5,1},{6,2},{7,3},{8,12},{9,13},{10,... | collective-permute-start | bytes 49160 | tf_op jit(solution)/shard_map/ppermute | solution.py:501
  34.7 1.7 %collective-permute-done.4 = f32[32,128]{1,0:T(8,128)S(1)} collective-permute-done((f32[32,128]{1,0:T(8,128)S(1)}, f32[32,128]{1,0:T(8,128)S(1)}, u32[]{:S(2)}, u32[]{:S(2)}) %collective-permute-start.4) | collective-permute-done | bytes 16416 | tf_op jit(solution)/shard_map/ppermute | solution.py:501
  36.4 3.0 %collective-permute-start.5 = (f32[64,128]{1,0:T(8,128)S(1)}, f32[64,128]{1,0:T(8,128)S(1)}, u32[]{:S(2)}, u32[]{:S(2)}) collective-permute-start(f32[64,128]{1,0:T(8,128)S(1)} %pad_maximum_fusion), channel_id=1, source_target_pairs={{0,8},{1,9},{2,10},{3,11},{4,12},{5,13},{6,14},{7,15},{8,0},{9,1},... | collective-permute-start | bytes 98312 | tf_op jit(solution)/shard_map/ppermute | solution.py:501
  39.5 1.9 %collective-permute-done.5 = f32[64,128]{1,0:T(8,128)S(1)} collective-permute-done((f32[64,128]{1,0:T(8,128)S(1)}, f32[64,128]{1,0:T(8,128)S(1)}, u32[]{:S(2)}, u32[]{:S(2)}) %collective-permute-start.5) | collective-permute-done | bytes 32800 | tf_op jit(solution)/shard_map/ppermute | solution.py:501
  41.4 0.1 slice.11
  41.5 0.1 copy.13
  41.6 0.1 broadcast_compare_fusion
  41.6 0.7 %select_reduce_fusion = f32[2,72]{1,0:T(2,128)} fusion(f32[16,2,72]{2,0,1:T(8,128)S(1)} %copy.12, pred[2,16,2]{1,2,0:T(4,128)(4,1)S(1)} %broadcast_compare_fusion), kind=kLoop, calls=%fused_computation.1 | loop fusion | flops 9072 | bytes 9856 | tf_op jit(solution)/shard_map/reduce_sum | solution.py:508
  42.3 0.0 collective-permute-done.8.far_sums
  42.3 0.0 collective-permute-done.6.near_classes
  42.3 4.6 %adjoint_part.1 = f32[4,1440]{1,0:T(4,128)} custom-call(f32[12,64,128]{2,1,0:T(8,128)S(1)} %get-tuple-element.18.own, f32[684,128]{1,0:T(8,128)S(1)} %collective-permute-done.near, f32[684,128]{1,0:T(8,128)S(1)} %collective-permute-done.1.far, f32[12,160,128]{2,1,0:T(8,128)S(1)} %get-tuple-element.28.maps, f32[12,192,128]{2,1,0:T(8,128)} %copy-done, ...), custom_call_target="tpu_custom_call" | custom-call | tf_op jit(solution)/shard_map/adjoint_part/pallas_call | solution.py:489
  (21 shorter events, 0.0 us)
Async XLA Ops:
  0.6 1.0 %copy-start.1 = (f32[16,4,1440]{2,1,0:T(4,128)S(1)}, f32[16,4,1440]{2,1,0:T(4,128)}, u32[]{:S(2)}) copy-start(f32[16,4,1440]{2,1,0:T(4,128)} %tracer.1) | copy-start | bytes 1105924
  1.6 0.7 %copy-start.3 = (f32[4,1440]{1,0:T(4,128)S(1)}, f32[4,1440]{1,0:T(4,128)}, u32[]{:S(2)}) copy-start(f32[4,1440]{1,0:T(4,128)} %mix.1) | copy-start | bytes 69124
  2.4 0.7 %copy-start.4 = (f32[4,1440]{1,0:T(4,128)S(1)}, f32[4,1440]{1,0:T(4,128)}, u32[]{:S(2)}) copy-start(f32[4,1440]{1,0:T(4,128)} %heading.1) | copy-start | bytes 69124
  3.1 0.7 %copy-start.5 = (s32[4,1440]{1,0:T(4,128)S(1)}, s32[4,1440]{1,0:T(4,128)}, u32[]{:S(2)}) copy-start(s32[4,1440]{1,0:T(4,128)} %depth.1) | copy-start | bytes 69124
  4.4 7.1 %collective-permute-start = (f32[684,128]{1,0:T(8,128)S(1)}, f32[684,128]{1,0:T(8,128)S(1)}, u32[]{:S(2)}, u32[]{:S(2)}) collective-permute-start(f32[684,128]{1,0:T(8,128)S(1)} %get-tuple-element.22), channel_id=1, source_target_pairs={{0,1},{1,0},{2,3},{3,2},{4,5},{5,4},{6,7},{7,6},{8,9},{9,8},{10,11... | collective-permute-start | bytes 1050632 | tf_op jit(solution)/shard_map/ppermute | solution.py:429
  4.9 7.9 %collective-permute-start.1 = (f32[684,128]{1,0:T(8,128)S(1)}, f32[684,128]{1,0:T(8,128)S(1)}, u32[]{:S(2)}, u32[]{:S(2)}) collective-permute-start(f32[684,128]{1,0:T(8,128)S(1)} %get-tuple-element.23), channel_id=1, source_target_pairs={{1,2},{2,1},{3,4},{4,3},{5,6},{6,5},{7,8},{8,7},{9,10},{10,9},{11,... | collective-permute-start | bytes 1050632 | tf_op jit(solution)/shard_map/ppermute | solution.py:432
  7.5 1.0 %copy-start.2 = (s32[16,4,1440]{2,1,0:T(4,128)S(1)}, s32[16,4,1440]{2,1,0:T(4,128)}, u32[]{:S(2)}) copy-start(s32[16,4,1440]{2,1,0:T(4,128)} %classes.1) | copy-start | bytes 1105924
  8.5 0.7 %copy-start.6 = (f32[32,72]{1,0:T(8,128)S(1)}, f32[32,72]{1,0:T(8,128)}, u32[]{:S(2)}) copy-start(f32[32,72]{1,0:T(8,128)} %weights.1) | copy-start | bytes 27652
  9.2 0.7 %copy-start.7 = (s32[4]{0:T(128)S(1)}, s32[4]{0:T(128)}, u32[]{:S(2)}) copy-start(s32[4]{0:T(128)} %band_of_row.1) | copy-start | bytes 52
  16.6 1.0 %copy-start = (f32[12,192,128]{2,1,0:T(8,128)}, f32[12,192,128]{2,1,0:T(8,128)S(1)}, u32[]{:S(2)}) copy-start(f32[12,192,128]{2,1,0:T(8,128)S(1)} %get-tuple-element.29.later) | copy-start | bytes 3538948
  17.6 24.7 %collective-permute-start.8 = (f32[8,128]{1,0:T(8,128)S(1)}, f32[8,128]{1,0:T(8,128)S(1)}, u32[]{:S(2)}, u32[]{:S(2)}) collective-permute-start(f32[8,128]{1,0:T(8,128)S(1)} %get-tuple-element.27.own_sums), channel_id=1, source_target_pairs={{1,2},{2,1},{3,4},{4,3},{5,6},{6,5},{7,8},{8,7},{9,10},{10,9},{11,... | collective-permute-start | bytes 12296 | tf_op jit(solution)/shard_map/ppermute | solution.py:432
  19.6 4.8 %collective-permute-start.2 = (f32[8,128]{1,0:T(8,128)S(1)}, f32[8,128]{1,0:T(8,128)S(1)}, u32[]{:S(2)}, u32[]{:S(2)}) collective-permute-start(f32[8,128]{1,0:T(8,128)S(1)} %get-tuple-element.27.own_sums), channel_id=1, source_target_pairs={{0,1},{1,0},{2,3},{3,2},{4,5},{5,4},{6,7},{7,6},{8,9},{9,8},{10,11... | collective-permute-start | bytes 12296 | tf_op jit(solution)/shard_map/ppermute | solution.py:429
  23.0 19.3 %collective-permute-start.6 = (s32[576,128]{1,0:T(8,128)}, s32[576,128]{1,0:T(8,128)S(1)}, u32[]{:S(2)}, u32[]{:S(2)}) collective-permute-start(s32[576,128]{1,0:T(8,128)} %get-tuple-element.30), channel_id=1, source_target_pairs={{0,1},{1,0},{2,3},{3,2},{4,5},{5,4},{6,7},{7,6},{8,9},{9,8},{10,11... | collective-permute-start | bytes 884744 | tf_op jit(solution)/shard_map/ppermute | solution.py:429
  23.0 19.3 %collective-permute-start.7 = (s32[576,128]{1,0:T(8,128)S(1)}, s32[576,128]{1,0:T(8,128)S(1)}, u32[]{:S(2)}, u32[]{:S(2)}) collective-permute-start(s32[576,128]{1,0:T(8,128)S(1)} %get-tuple-element.31), channel_id=1, source_target_pairs={{1,2},{2,1},{3,4},{4,3},{5,6},{6,5},{7,8},{8,7},{9,10},{10,9},{11,... | collective-permute-start | bytes 884744 | tf_op jit(solution)/shard_map/ppermute | solution.py:432
  24.5 5.5 %collective-permute-start.3 = (f32[16,128]{1,0:T(8,128)S(1)}, f32[16,128]{1,0:T(8,128)S(1)}, u32[]{:S(2)}, u32[]{:S(2)}) collective-permute-start(f32[16,128]{1,0:T(8,128)S(1)} %pad_maximum_fusion.2), channel_id=1, source_target_pairs={{0,2},{1,3},{2,0},{3,1},{4,6},{5,7},{6,4},{7,5},{8,10},{9,11},{10,... | collective-permute-start | bytes 24584 | tf_op jit(solution)/shard_map/ppermute | solution.py:501
  30.0 6.5 %collective-permute-start.4 = (f32[32,128]{1,0:T(8,128)S(1)}, f32[32,128]{1,0:T(8,128)S(1)}, u32[]{:S(2)}, u32[]{:S(2)}) collective-permute-start(f32[32,128]{1,0:T(8,128)S(1)} %pad_maximum_fusion.1), channel_id=1, source_target_pairs={{0,4},{1,5},{2,6},{3,7},{4,0},{5,1},{6,2},{7,3},{8,12},{9,13},{10,... | collective-permute-start | bytes 49160 | tf_op jit(solution)/shard_map/ppermute | solution.py:501
  36.4 4.9 %collective-permute-start.5 = (f32[64,128]{1,0:T(8,128)S(1)}, f32[64,128]{1,0:T(8,128)S(1)}, u32[]{:S(2)}, u32[]{:S(2)}) collective-permute-start(f32[64,128]{1,0:T(8,128)S(1)} %pad_maximum_fusion), channel_id=1, source_target_pairs={{0,8},{1,9},{2,10},{3,11},{4,12},{5,13},{6,14},{7,15},{8,0},{9,1},... | collective-permute-start | bytes 98312 | tf_op jit(solution)/shard_map/ppermute | solution.py:501

commit v3 on v2

--- a/solution.py
+++ b/solution.py
@@ -17,7 +17,7 @@
 LOW_COUNT = 16
 LOW_SHIFT = 4
 GROUP = 3
-VMEM_LIMIT = 50 * 1024 * 1024
+VMEM_LIMIT = 16 * 1024 * 1024
 
 
 def strip_of(row, j, lon_count):
@@ -42,7 +42,14 @@
     return jnp.where(odd, down, up)
 
 
-def pack_fields(tracer, mix, heading, depth, own, own_maps, near, far):
+def pack_fields(*refs):
+    sources, (own, own_maps, near, far), held, arrived = refs[:4], refs[4:8], refs[8:12], refs[12]
+    copies = [pltpu.make_async_copy(a, b, arrived.at[i]) for i, (a, b) in enumerate(zip(sources, held))]
+    for copy in copies:
+        copy.start()
+    for copy in copies:
+        copy.wait()
+    tracer, mix, heading, depth = held
     levels, rows, lon_count = tracer.shape
     strips = lon_count // OWN
     odd = is_odd()
@@ -217,7 +224,7 @@
     return jnp.concatenate(left, axis=0), jnp.concatenate(right, axis=0)
 
 
-def forward(scales, own, own_maps, near, far, classes, sums, maps, later, grams):
+def forward(scales, own, own_maps, near, far, classes, sums, later, maps, grams):
     strips, _, _ = own.shape
     levels = own.shape[1] // 4
     face_maps(own_maps, near, far, maps, strips * STEPS * levels)
@@ -317,11 +324,12 @@
 
 
 def adjoint_part(
-    own, near, far, maps, later, own_classes, near_classes, far_classes,
-    own_sums, near_sums, far_sums, gradient, strips_out,
+    own, own_maps, near, far, later, own_classes, near_classes, far_classes,
+    own_sums, near_sums, far_sums, gradient, maps, strips_out,
 ):
     strips = own.shape[0]
     levels = own.shape[1] // 4
+    face_maps(own_maps, near, far, maps, strips * STEPS * levels)
     rows, lon_count = gradient.shape
     odd = is_odd()
 
@@ -415,6 +423,10 @@
     return [pl.BlockSpec(memory_space=pltpu.VMEM)] * count
 
 
+def cost(nanoseconds):
+    return pl.CostEstimate(flops=1153500 * nanoseconds, bytes_accessed=3690 * nanoseconds, transcendentals=0)
+
+
 def body(tracer, diffusivity, direction, column_depth, density_class, band_of_row, weights):
     levels, rows, lon_count = tracer.shape
     strips = lon_count // OWN
@@ -440,8 +452,10 @@
             jax.ShapeDtypeStruct((payload, LANES), f32),
             jax.ShapeDtypeStruct((payload, LANES), f32),
         ),
-        in_specs=vmem(4),
+        in_specs=[pl.BlockSpec(memory_space=pltpu.HBM)] * 4,
         out_specs=tuple(vmem(4)),
+        scratch_shapes=[pltpu.VMEM(x.shape, x.dtype) for x in (tracer, diffusivity, direction, column_depth)]
+        + [pltpu.SemaphoreType.DMA((4,))],
         compiler_params=params,
     )(tracer, diffusivity, direction, column_depth)
     far = to_far(far_out)
@@ -466,17 +480,18 @@
     far_classes = to_far(far_classes_out)
     near_classes = to_near(near_classes_out)
 
-    sums, maps, later = pl.pallas_call(
+    sums, later = pl.pallas_call(
         forward,
         name="forward",
         out_shape=(
             jax.ShapeDtypeStruct((8, LANES), f32),
-            jax.ShapeDtypeStruct((strips, 16 * MAP_FIELDS, LANES), f32),
             jax.ShapeDtypeStruct((strips, 12 * levels, LANES), f32),
         ),
         in_specs=vmem(6),
-        out_specs=tuple(vmem(3)),
+        out_specs=tuple(vmem(2)),
+        cost_estimate=cost(4000),
         scratch_shapes=[
+            pltpu.VMEM((strips, 16 * MAP_FIELDS, LANES), f32),
             pltpu.VMEM((2, 2 * HIGH_COUNT * levels, LOW_COUNT * levels), f32),
         ],
         compiler_params=params,
@@ -486,20 +501,32 @@
     far_sums = to_far(sums)
     gathered = jnp.concatenate([sums, near_sums], axis=0)
 
-    gradient = pl.pallas_call(
-        adjoint_part,
-        name="adjoint_part",
-        out_shape=jax.ShapeDtypeStruct((rows, lon_count), f32),
-        in_specs=vmem(11),
-        out_specs=pl.BlockSpec(memory_space=pltpu.VMEM),
-        scratch_shapes=[pltpu.VMEM((strips, 8, LANES), f32)],
-        compiler_params=params,
-    )(own, near, far, maps, later, own_classes, near_classes, far_classes, sums, near_sums, far_sums)
-
+    def sensitivities(near_classes, far_classes, far_sums):
+        return pl.pallas_call(
+            adjoint_part,
+            name="adjoint_part",
+            out_shape=jax.ShapeDtypeStruct((rows, lon_count), f32),
+            in_specs=vmem(11),
+            out_specs=pl.BlockSpec(memory_space=pltpu.VMEM),
+            scratch_shapes=[
+                pltpu.VMEM((strips, 16 * MAP_FIELDS, LANES), f32),
+                pltpu.VMEM((strips, 8, LANES), f32),
+            ],
+            cost_estimate=cost(4000),
+            compiler_params=params,
+        )(own, own_maps, near, far, later, own_classes, near_classes, far_classes, sums, near_sums, far_sums)
+
+    gathered, near_classes, far_classes = lax.optimization_barrier((gathered, near_classes, far_classes))
+    gradient = None
     step = 2
     while step < count:
         other = lax.ppermute(gathered, "lat", [(i, i ^ step) for i in range(count)])
+        if step == 4:
+            gradient = sensitivities(near_classes, far_classes, far_sums)
+            other, gradient = lax.optimization_barrier((other, gradient))
         gathered = jnp.concatenate([gathered, other], axis=0)
+        if step == 2:
+            gathered, far_sums = lax.optimization_barrier((gathered, far_sums))
         step *= 2
     band_own = weights.shape[0] // count
     finished = gathered.reshape(count, 8, LANES)[:, :2]

time: 47.4 us -> 43 us (0.907)
  Pallas kernels: 10.5 us -> 9.22 us
  waiting for transfers between devices: 9.77 us -> 8.52 us
  local copies, waits for them, and re-layouts: 6.79 us -> 5.74 us
  starting transfers between devices: 18.4 us -> 17.6 us
    ppermute x3, waiting for transfers between devices: 8.47 us -> 3.72 us  [body(): other = lax.ppermute(gathered, 'lat', [(i, i ^ step) for i in range(count)])]
    ppermute x3, waiting for transfers between devices: 1.29 us -> 3.97 us  [to_far(): return lax.ppermute(x, ('members', 'lat'), far_pairs(members, count))]
    unnamed x21 -> x15, local copies, waits for them, and re-layouts: 6.7 us -> 5.66 us
    pallas_call x1, Pallas kernels: 4.56 us -> 3.63 us  [sensitivities(): pl.pallas_call(adjoint_part, name='adjoint_part', out_shape=jax.ShapeDtyp...]
    ppermute x3, waiting for transfers between devices: 0.01 us -> 0.83 us  [to_near(): return lax.ppermute(x, 'lat', near_pairs(count))]
    ppermute x3, starting transfers between devices: 8.42 us -> 7.62 us  [body(): other = lax.ppermute(gathered, 'lat', [(i, i ^ step) for i in range(count)])]
    pallas_call x1, Pallas kernels: 1.65 us -> 0.94 us  [body(): pl.pallas_call(pack_classes, name='pack_classes', out_shape=(jax.ShapeDty...]
    ppermute x3, starting transfers between devices: 3.87 us -> 4.46 us  [to_near(): return lax.ppermute(x, 'lat', near_pairs(count))]
  transfers between devices with their start and end apart: 9 -> 9, of which waited for: 4 -> 5; matrix products, arithmetic and copies ran while one was open for 2% -> 0% of each run, Pallas kernels for 4% -> 20%
where the time goes in v3:
time: 43 us; the launch traced here: 42.6 us
  starting transfers between devices  17.6 us (41%)
  Pallas kernels  9.22 us (21%)
  waiting for transfers between devices  8.52 us (20%)
  local copies, waits for them, and re-layouts  5.74 us (13%)
  other arithmetic  0.76 us (2%)
  between operations  0.69 us (2%)
    ppermute x3, starting transfers between devices, body(): other = lax.ppermute(gathered, 'lat', [(i, i ^ step) for i in range(count)])  7.62 us
    unnamed x15, local copies, waits for them, and re-layouts  5.66 us
    ppermute x3, starting transfers between devices, to_far(): return lax.ppermute(x, ('members', 'lat'), far_pairs(members, count))  5.55 us
    ppermute x3, starting transfers between devices, to_near(): return lax.ppermute(x, 'lat', near_pairs(count))  4.46 us
    ppermute x3, waiting for transfers between devices, to_far(): return lax.ppermute(x, ('members', 'lat'), far_pairs(members, count))  3.97 us
    pallas_call x1, Pallas kernels, body(): pl.pallas_call(forward, name='forward', out_shape=(jax.ShapeDtypeStruct((...  3.79 us
    ppermute x3, waiting for transfers between devices, body(): other = lax.ppermute(gathered, 'lat', [(i, i ^ step) for i in range(count)])  3.72 us
    pallas_call x1, Pallas kernels, sensitivities(): pl.pallas_call(adjoint_part, name='adjoint_part', out_shape=jax.ShapeDtyp...  3.63 us
  transfers between devices with their start and end apart: 9, of which 5 were waited for; matrix products, arithmetic and copies ran while one was open for 0% of the time, Pallas kernels for 20%

profile of v3, /device:TPU:0, one launch (start us, length us, event | category | flops | bytes accessed | tf_op | source)
XLA Modules:
  0.0 42.6 jit_solution(7554135348088933862)
XLA Ops:
  0.6 1.0 %copy-done = f32[16,4,1440]{2,1,0:T(4,128)S(1)} copy-done((f32[16,4,1440]{2,1,0:T(4,128)S(1)}, f32[16,4,1440]{2,1,0:T(4,128)}, u32[]{:S(2)}) %copy-start) | copy-done | bytes 368664
  1.6 0.7 %copy-done.2 = f32[4,1440]{1,0:T(4,128)S(1)} copy-done((f32[4,1440]{1,0:T(4,128)S(1)}, f32[4,1440]{1,0:T(4,128)}, u32[]{:S(2)}) %copy-start.2) | copy-done | bytes 23064
  2.4 0.7 %copy-done.3 = f32[4,1440]{1,0:T(4,128)S(1)} copy-done((f32[4,1440]{1,0:T(4,128)S(1)}, f32[4,1440]{1,0:T(4,128)}, u32[]{:S(2)}) %copy-start.3) | copy-done | bytes 23064
  3.1 0.7 %copy-done.4 = s32[4,1440]{1,0:T(4,128)S(1)} copy-done((s32[4,1440]{1,0:T(4,128)S(1)}, s32[4,1440]{1,0:T(4,128)}, u32[]{:S(2)}) %copy-start.4) | copy-done | bytes 23064
  3.8 0.9 %pack_fields.1 = (f32[12,64,128]{2,1,0:T(8,128)S(1)}, f32[12,16,128]{2,1,0:T(8,128)S(1)}, f32[684,128]{1,0:T(8,128)S(1)}, f32[684,128]{1,0:T(8,128)S(1)}) custom-call(f32[16,4,1440]{2,1,0:T(4,128)S(1)} %copy-done, f32[4,1440]{1,0:T(4,128)S(1)} %copy-done.2, f32[4,1440]{1,0:T(4,128)S(1)} %copy-done.3, s32[4,1440]{1,0:T(4,128)S(1)} %copy-done.4), custom_call_target="tpu_custom_call" | custom-call | tf_op jit(solution)/shard_map/pack_fields/pallas_call | solution.py:446
  4.7 0.5 %collective-permute-start = (f32[684,128]{1,0:T(8,128)S(1)}, f32[684,128]{1,0:T(8,128)S(1)}, u32[]{:S(2)}, u32[]{:S(2)}) collective-permute-start(f32[684,128]{1,0:T(8,128)S(1)} %get-tuple-element.28), channel_id=1, source_target_pairs={{0,1},{1,0},{2,3},{3,2},{4,5},{5,4},{6,7},{7,6},{8,9},{9,8},{10,11... | collective-permute-start | bytes 1050632 | tf_op jit(solution)/shard_map/ppermute | solution.py:441
  5.2 2.6 %collective-permute-start.1 = (f32[684,128]{1,0:T(8,128)S(1)}, f32[684,128]{1,0:T(8,128)S(1)}, u32[]{:S(2)}, u32[]{:S(2)}) collective-permute-start(f32[684,128]{1,0:T(8,128)S(1)} %get-tuple-element.29), channel_id=1, source_target_pairs={{1,2},{2,1},{3,4},{4,3},{5,6},{6,5},{7,8},{8,7},{9,10},{10,9},{11,... | collective-permute-start | bytes 1050632 | tf_op jit(solution)/shard_map/ppermute | solution.py:444
  7.8 1.0 %copy-done.1 = s32[16,4,1440]{2,1,0:T(4,128)S(1)} copy-done((s32[16,4,1440]{2,1,0:T(4,128)S(1)}, s32[16,4,1440]{2,1,0:T(4,128)}, u32[]{:S(2)}) %copy-start.1) | copy-done | bytes 368664
  8.8 0.7 %copy-done.5 = f32[32,72]{1,0:T(8,128)S(1)} copy-done((f32[32,72]{1,0:T(8,128)S(1)}, f32[32,72]{1,0:T(8,128)}, u32[]{:S(2)}) %copy-start.5) | copy-done | bytes 9240
  9.5 0.7 %copy-done.6 = s32[4]{0:T(128)S(1)} copy-done((s32[4]{0:T(128)S(1)}, s32[4]{0:T(128)}, u32[]{:S(2)}) %copy-start.6) | copy-done | bytes 40
  10.2 0.9 %pack_classes.1 = (s32[12,64,128]{2,1,0:T(8,128)S(1)}, s32[576,128]{1,0:T(8,128)S(1)}, s32[576,128]{1,0:T(8,128)S(1)}, f32[8,128]{1,0:T(8,128)S(1)}) custom-call(s32[16,4,1440]{2,1,0:T(4,128)S(1)} %copy-done.1, f32[32,72]{1,0:T(8,128)S(1)} %copy-done.5, s32[4]{0:T(128)S(1)} %copy-done.6), custom_call_target="tpu_custom_call" | custom-call | tf_op jit(solution)/shard_map/pack_classes/pallas_call | solution.py:464
  11.1 0.0 collective-permute-done.near
  11.1 2.0 %collective-permute-done.1.far = f32[684,128]{1,0:T(8,128)S(1)} collective-permute-done((f32[684,128]{1,0:T(8,128)S(1)}, f32[684,128]{1,0:T(8,128)S(1)}, u32[]{:S(2)}, u32[]{:S(2)}) %collective-permute-start.1) | collective-permute-done | bytes 350240 | tf_op jit(solution)/shard_map/ppermute | solution.py:444
  13.1 2.9 %collective-permute-start.3 = (s32[576,128]{1,0:T(8,128)S(1)}, s32[576,128]{1,0:T(8,128)S(1)}, u32[]{:S(2)}, u32[]{:S(2)}) collective-permute-start(s32[576,128]{1,0:T(8,128)S(1)} %get-tuple-element.34), channel_id=1, source_target_pairs={{0,1},{1,0},{2,3},{3,2},{4,5},{5,4},{6,7},{7,6},{8,9},{9,8},{10,11... | collective-permute-start | bytes 884744 | tf_op jit(solution)/shard_map/ppermute | solution.py:441
  16.0 1.5 %collective-permute-start.4 = (s32[576,128]{1,0:T(8,128)S(1)}, s32[576,128]{1,0:T(8,128)S(1)}, u32[]{:S(2)}, u32[]{:S(2)}) collective-permute-start(s32[576,128]{1,0:T(8,128)S(1)} %get-tuple-element.35), channel_id=1, source_target_pairs={{1,2},{2,1},{3,4},{4,3},{5,6},{6,5},{7,8},{8,7},{9,10},{10,9},{11,... | collective-permute-start | bytes 884744 | tf_op jit(solution)/shard_map/ppermute | solution.py:444
  17.5 3.8 %forward.1 = (f32[8,128]{1,0:T(8,128)S(1)}, f32[12,192,128]{2,1,0:T(8,128)S(1)}) custom-call(f32[8,128]{1,0:T(8,128)S(1)} %get-tuple-element.23.scales, f32[12,64,128]{2,1,0:T(8,128)S(1)} %get-tuple-element.24.own, f32[12,16,128]{2,1,0:T(8,128)S(1)} %get-tuple-element.25.own_maps, f32[684,128]{1,0:T(8,128)S(1)} %collective-permute-done.near, ...), custom_call_target="tpu_custom_call" | custom-call | flops 4614000128 | bytes 14760000 | tf_op jit(solution)/shard_map/forward/pallas_call | solution.py:483
  21.3 1.1 %collective-permute-start.2 = (f32[8,128]{1,0:T(8,128)S(1)}, f32[8,128]{1,0:T(8,128)S(1)}, u32[]{:S(2)}, u32[]{:S(2)}) collective-permute-start(f32[8,128]{1,0:T(8,128)S(1)} %get-tuple-element.33.own_sums), channel_id=1, source_target_pairs={{0,1},{1,0},{2,3},{3,2},{4,5},{5,4},{6,7},{7,6},{8,9},{9,8},{10,11... | collective-permute-start | bytes 12296 | tf_op jit(solution)/shard_map/ppermute | solution.py:441
  22.3 0.8 %collective-permute-done.2.near_sums = f32[8,128]{1,0:T(8,128)S(1)} collective-permute-done((f32[8,128]{1,0:T(8,128)S(1)}, f32[8,128]{1,0:T(8,128)S(1)}, u32[]{:S(2)}, u32[]{:S(2)}) %collective-permute-start.2) | collective-permute-done | bytes 4128 | tf_op jit(solution)/shard_map/ppermute | solution.py:441
  23.2 0.0 collective-permute-done.3.near_classes
  23.2 4.5 %collective-permute-start.5 = (f32[16,128]{1,0:T(8,128)S(1)}, f32[16,128]{1,0:T(8,128)S(1)}, u32[]{:S(2)}, u32[]{:S(2)}) collective-permute-start(f32[16,128]{1,0:T(8,128)S(1)} %pad_maximum_fusion.2), channel_id=1, source_target_pairs={{0,2},{1,3},{2,0},{3,1},{4,6},{5,7},{6,4},{7,5},{8,10},{9,11},{10,... | collective-permute-start | bytes 24584 | tf_op jit(solution)/shard_map/ppermute | solution.py:523
  27.7 1.5 %collective-permute-start.6 = (f32[8,128]{1,0:T(8,128)S(1)}, f32[8,128]{1,0:T(8,128)S(1)}, u32[]{:S(2)}, u32[]{:S(2)}) collective-permute-start(f32[8,128]{1,0:T(8,128)S(1)} %get-tuple-element.33.own_sums), channel_id=1, source_target_pairs={{1,2},{2,1},{3,4},{4,3},{5,6},{6,5},{7,8},{8,7},{9,10},{10,9},{11,... | collective-permute-start | bytes 12296 | tf_op jit(solution)/shard_map/ppermute | solution.py:444
  29.2 0.1 collective-permute-done.5
  29.3 2.0 %collective-permute-done.6.far_sums = f32[8,128]{1,0:T(8,128)S(1)} collective-permute-done((f32[8,128]{1,0:T(8,128)S(1)}, f32[8,128]{1,0:T(8,128)S(1)}, u32[]{:S(2)}, u32[]{:S(2)}) %collective-permute-start.6) | collective-permute-done | bytes 4128 | tf_op jit(solution)/shard_map/ppermute | solution.py:444
  31.3 1.9 %collective-permute-start.7 = (f32[32,128]{1,0:T(8,128)S(1)}, f32[32,128]{1,0:T(8,128)S(1)}, u32[]{:S(2)}, u32[]{:S(2)}) collective-permute-start(f32[32,128]{1,0:T(8,128)S(1)} %pad_maximum_fusion.1), channel_id=1, source_target_pairs={{0,4},{1,5},{2,6},{3,7},{4,0},{5,1},{6,2},{7,3},{8,12},{9,13},{10,... | collective-permute-start | bytes 49160 | tf_op jit(solution)/shard_map/ppermute | solution.py:523
  33.2 3.6 %adjoint_part.1 = f32[4,1440]{1,0:T(4,128)} custom-call(f32[12,64,128]{2,1,0:T(8,128)S(1)} %get-tuple-element.24.own, f32[12,16,128]{2,1,0:T(8,128)S(1)} %get-tuple-element.25.own_maps, f32[684,128]{1,0:T(8,128)S(1)} %collective-permute-done.near, f32[684,128]{1,0:T(8,128)S(1)} %collective-permute-done.1.far, f32[12,192,128]{2,1,0:T(8,128)S(1)} %get-tuple-element.38.later, ...), custom_call_target="tpu_custom_call" | custom-call | flops 4614000128 | bytes 14760000 | tf_op jit(solution)/shard_map/adjoint_part/pallas_call | solution.py:505
  36.8 0.0 collective-permute-done.7
  36.8 1.2 %collective-permute-start.8 = (f32[64,128]{1,0:T(8,128)S(1)}, f32[64,128]{1,0:T(8,128)S(1)}, u32[]{:S(2)}, u32[]{:S(2)}) collective-permute-start(f32[64,128]{1,0:T(8,128)S(1)} %pad_maximum_fusion), channel_id=1, source_target_pairs={{0,8},{1,9},{2,10},{3,11},{4,12},{5,13},{6,14},{7,15},{8,0},{9,1},... | collective-permute-start | bytes 98312 | tf_op jit(solution)/shard_map/ppermute | solution.py:523
  38.0 3.6 %collective-permute-done.8 = f32[64,128]{1,0:T(8,128)S(1)} collective-permute-done((f32[64,128]{1,0:T(8,128)S(1)}, f32[64,128]{1,0:T(8,128)S(1)}, u32[]{:S(2)}, u32[]{:S(2)}) %collective-permute-start.8) | collective-permute-done | bytes 32800 | tf_op jit(solution)/shard_map/ppermute | solution.py:523
  41.6 0.1 slice.11
  41.7 0.1 copy.13
  41.8 0.1 broadcast_compare_fusion
  41.9 0.7 %select_reduce_fusion = f32[2,72]{1,0:T(2,128)} fusion(f32[16,2,72]{2,0,1:T(8,128)S(1)} %copy.12, pred[2,16,2]{1,2,0:T(4,128)(4,1)S(1)} %broadcast_compare_fusion), kind=kLoop, calls=%fused_computation.2 | loop fusion | flops 9072 | bytes 9856 | tf_op jit(solution)/shard_map/reduce_sum | solution.py:535
  (15 shorter events, 0.0 us)
Async XLA Ops:
  0.6 1.0 %copy-start = (f32[16,4,1440]{2,1,0:T(4,128)S(1)}, f32[16,4,1440]{2,1,0:T(4,128)}, u32[]{:S(2)}) copy-start(f32[16,4,1440]{2,1,0:T(4,128)} %refs_0_.1) | copy-start | bytes 1105924
  1.6 0.7 %copy-start.2 = (f32[4,1440]{1,0:T(4,128)S(1)}, f32[4,1440]{1,0:T(4,128)}, u32[]{:S(2)}) copy-start(f32[4,1440]{1,0:T(4,128)} %refs_1_.1) | copy-start | bytes 69124
  2.4 0.7 %copy-start.3 = (f32[4,1440]{1,0:T(4,128)S(1)}, f32[4,1440]{1,0:T(4,128)}, u32[]{:S(2)}) copy-start(f32[4,1440]{1,0:T(4,128)} %refs_2_.1) | copy-start | bytes 69124
  3.1 0.7 %copy-start.4 = (s32[4,1440]{1,0:T(4,128)S(1)}, s32[4,1440]{1,0:T(4,128)}, u32[]{:S(2)}) copy-start(s32[4,1440]{1,0:T(4,128)} %refs_3_.1) | copy-start | bytes 69124
  4.7 6.4 %collective-permute-start = (f32[684,128]{1,0:T(8,128)S(1)}, f32[684,128]{1,0:T(8,128)S(1)}, u32[]{:S(2)}, u32[]{:S(2)}) collective-permute-start(f32[684,128]{1,0:T(8,128)S(1)} %get-tuple-element.28), channel_id=1, source_target_pairs={{0,1},{1,0},{2,3},{3,2},{4,5},{5,4},{6,7},{7,6},{8,9},{9,8},{10,11... | collective-permute-start | bytes 1050632 | tf_op jit(solution)/shard_map/ppermute | solution.py:441
  5.2 7.9 %collective-permute-start.1 = (f32[684,128]{1,0:T(8,128)S(1)}, f32[684,128]{1,0:T(8,128)S(1)}, u32[]{:S(2)}, u32[]{:S(2)}) collective-permute-start(f32[684,128]{1,0:T(8,128)S(1)} %get-tuple-element.29), channel_id=1, source_target_pairs={{1,2},{2,1},{3,4},{4,3},{5,6},{6,5},{7,8},{8,7},{9,10},{10,9},{11,... | collective-permute-start | bytes 1050632 | tf_op jit(solution)/shard_map/ppermute | solution.py:444
  7.8 1.0 %copy-start.1 = (s32[16,4,1440]{2,1,0:T(4,128)S(1)}, s32[16,4,1440]{2,1,0:T(4,128)}, u32[]{:S(2)}) copy-start(s32[16,4,1440]{2,1,0:T(4,128)} %classes.1) | copy-start | bytes 1105924
  8.8 0.7 %copy-start.5 = (f32[32,72]{1,0:T(8,128)S(1)}, f32[32,72]{1,0:T(8,128)}, u32[]{:S(2)}) copy-start(f32[32,72]{1,0:T(8,128)} %weights.1) | copy-start | bytes 27652
  9.5 0.7 %copy-start.6 = (s32[4]{0:T(128)S(1)}, s32[4]{0:T(128)}, u32[]{:S(2)}) copy-start(s32[4]{0:T(128)} %band_of_row.1) | copy-start | bytes 52
  13.1 10.1 %collective-permute-start.3 = (s32[576,128]{1,0:T(8,128)S(1)}, s32[576,128]{1,0:T(8,128)S(1)}, u32[]{:S(2)}, u32[]{:S(2)}) collective-permute-start(s32[576,128]{1,0:T(8,128)S(1)} %get-tuple-element.34), channel_id=1, source_target_pairs={{0,1},{1,0},{2,3},{3,2},{4,5},{5,4},{6,7},{7,6},{8,9},{9,8},{10,11... | collective-permute-start | bytes 884744 | tf_op jit(solution)/shard_map/ppermute | solution.py:441
  16.0 7.2 %collective-permute-start.4 = (s32[576,128]{1,0:T(8,128)S(1)}, s32[576,128]{1,0:T(8,128)S(1)}, u32[]{:S(2)}, u32[]{:S(2)}) collective-permute-start(s32[576,128]{1,0:T(8,128)S(1)} %get-tuple-element.35), channel_id=1, source_target_pairs={{1,2},{2,1},{3,4},{4,3},{5,6},{6,5},{7,8},{8,7},{9,10},{10,9},{11,... | collective-permute-start | bytes 884744 | tf_op jit(solution)/shard_map/ppermute | solution.py:444
  21.3 1.9 %collective-permute-start.2 = (f32[8,128]{1,0:T(8,128)S(1)}, f32[8,128]{1,0:T(8,128)S(1)}, u32[]{:S(2)}, u32[]{:S(2)}) collective-permute-start(f32[8,128]{1,0:T(8,128)S(1)} %get-tuple-element.33.own_sums), channel_id=1, source_target_pairs={{0,1},{1,0},{2,3},{3,2},{4,5},{5,4},{6,7},{7,6},{8,9},{9,8},{10,11... | collective-permute-start | bytes 12296 | tf_op jit(solution)/shard_map/ppermute | solution.py:441
  23.2 6.1 %collective-permute-start.5 = (f32[16,128]{1,0:T(8,128)S(1)}, f32[16,128]{1,0:T(8,128)S(1)}, u32[]{:S(2)}, u32[]{:S(2)}) collective-permute-start(f32[16,128]{1,0:T(8,128)S(1)} %pad_maximum_fusion.2), channel_id=1, source_target_pairs={{0,2},{1,3},{2,0},{3,1},{4,6},{5,7},{6,4},{7,5},{8,10},{9,11},{10,... | collective-permute-start | bytes 24584 | tf_op jit(solution)/shard_map/ppermute | solution.py:523
  27.7 3.6 %collective-permute-start.6 = (f32[8,128]{1,0:T(8,128)S(1)}, f32[8,128]{1,0:T(8,128)S(1)}, u32[]{:S(2)}, u32[]{:S(2)}) collective-permute-start(f32[8,128]{1,0:T(8,128)S(1)} %get-tuple-element.33.own_sums), channel_id=1, source_target_pairs={{1,2},{2,1},{3,4},{4,3},{5,6},{6,5},{7,8},{8,7},{9,10},{10,9},{11,... | collective-permute-start | bytes 12296 | tf_op jit(solution)/shard_map/ppermute | solution.py:444
  31.3 5.5 %collective-permute-start.7 = (f32[32,128]{1,0:T(8,128)S(1)}, f32[32,128]{1,0:T(8,128)S(1)}, u32[]{:S(2)}, u32[]{:S(2)}) collective-permute-start(f32[32,128]{1,0:T(8,128)S(1)} %pad_maximum_fusion.1), channel_id=1, source_target_pairs={{0,4},{1,5},{2,6},{3,7},{4,0},{5,1},{6,2},{7,3},{8,12},{9,13},{10,... | collective-permute-start | bytes 49160 | tf_op jit(solution)/shard_map/ppermute | solution.py:523
  36.8 4.8 %collective-permute-start.8 = (f32[64,128]{1,0:T(8,128)S(1)}, f32[64,128]{1,0:T(8,128)S(1)}, u32[]{:S(2)}, u32[]{:S(2)}) collective-permute-start(f32[64,128]{1,0:T(8,128)S(1)} %pad_maximum_fusion), channel_id=1, source_target_pairs={{0,8},{1,9},{2,10},{3,11},{4,12},{5,13},{6,14},{7,15},{8,0},{9,1},... | collective-permute-start | bytes 98312 | tf_op jit(solution)/shard_map/ppermute | solution.py:523

commit v4 on v3

--- a/solution.py
+++ b/solution.py
@@ -13,10 +13,10 @@
 LANES = 128
 GHOST = 4
 OWN = LANES - 2 * GHOST
-HIGH_COUNT = 5
-LOW_COUNT = 16
-LOW_SHIFT = 4
-GROUP = 3
+HIGH_COUNT = 9
+LOW_COUNT = 8
+LOW_SHIFT = 3
+GROUP = 12
 VMEM_LIMIT = 16 * 1024 * 1024
 
 
@@ -42,13 +42,17 @@
     return jnp.where(odd, down, up)
 
 
-def pack_fields(*refs):
-    sources, (own, own_maps, near, far), held, arrived = refs[:4], refs[4:8], refs[8:12], refs[12]
+def bring(sources, held, arrived):
     copies = [pltpu.make_async_copy(a, b, arrived.at[i]) for i, (a, b) in enumerate(zip(sources, held))]
     for copy in copies:
         copy.start()
     for copy in copies:
         copy.wait()
+
+
+def pack_fields(*refs):
+    sources, (own, own_maps, near, far), held, arrived = refs[:4], refs[4:8], refs[8:12], refs[12]
+    bring(sources, held, arrived)
     tracer, mix, heading, depth = held
     levels, rows, lon_count = tracer.shape
     strips = lon_count // OWN
@@ -79,7 +83,10 @@
     own_maps[:, 12:, :] = jnp.zeros_like(own_maps[:, 12:, :])
 
 
-def pack_classes(classes, weights, band_of_row, own, near, far, scales):
+def pack_classes(*refs):
+    sources, (own, near, far, scales), held, arrived = refs[:3], refs[3:7], refs[7:10], refs[10]
+    bring(sources, held, arrived)
+    classes, weights, band_of_row = held
     levels, rows, lon_count = classes.shape
     strips = lon_count // OWN
     odd = is_odd()
@@ -95,16 +102,14 @@
                 at = (j * STEPS + rows - 1 - t) * levels
                 near[at : at + levels, :] = strip
     class_count = weights.shape[1]
-    label = lax.broadcasted_iota(jnp.int32, (1, LANES), 1)
     scale_rows, band_rows = [], []
     for pair in range(2):
         band = band_of_row[jnp.where(odd, 3 - 2 * pair, 2 * pair)]
         scale = weights[pl.ds(band, 1), :]
         scale_rows.append(jnp.concatenate([scale, jnp.zeros((1, LANES - class_count), jnp.float32)], axis=1))
-        band_rows.append(jnp.where(label == LANES - 1, band.astype(jnp.float32), 0.0))
-    scales[...] = jnp.concatenate(
-        scale_rows + band_rows + [jnp.zeros((4, LANES), jnp.float32)], axis=0
-    )
+        band_rows.append(jnp.full((1, LANES), band.astype(jnp.float32)))
+    blank = jnp.zeros((2, LANES), jnp.float32)
+    scales[...] = jnp.concatenate(scale_rows + [blank] + band_rows + [blank], axis=0)
 
 
 def east(x):
@@ -115,7 +120,7 @@
     return pltpu.roll(x, 1, 1)
 
 
-MAP_FIELDS = 10
+MAP_FIELDS = 7
 
 
 def level_order(levels):
@@ -125,9 +130,8 @@
 
 class Coefficients:
     blocks = {
-        "wet": 0, "east_open": 1, "west_open": 2, "north_open": 3,
-        "east_mix": 4, "west_mix": 5, "north_mix": 6,
-        "east_dir": 7, "west_dir": 8, "north_dir": 9,
+        "wet": 0, "east_open": 1, "north_open": 2,
+        "east_mix": 3, "north_mix": 4, "east_dir": 5, "north_dir": 6,
     }
 
     def __init__(self, maps, j, levels):
@@ -164,27 +168,42 @@
     return jnp.concatenate([after_even - pltpu.roll(after_odd, 1, 0), after_odd - after_even], axis=0)
 
 
-def gaps(field, rows):
-    to_east = {t: east(field[t]) - field[t] for t in rows}
-    to_west = {t: west(field[t]) - field[t] for t in rows}
-    to_north = {t: field[t + 1] - field[t] for t in range(rows[0] - 1, rows[-1] + 1)}
-    return to_east, to_west, to_north
-
-
-def spread(coef, kind, steps, rows):
-    to_east, to_west, to_north = steps
-    flux = {t: coef.get("north_" + kind, t) * to_north[t] for t in range(rows[0] - 1, rows[-1] + 1)}
-    return {
-        t: coef.get("east_" + kind, t) * to_east[t]
-        + coef.get("west_" + kind, t) * to_west[t]
-        + (flux[t] - flux[t - 1])
-        for t in rows
-    }
-
-
-def advance(coef, field, steps, rows):
-    moved = spread(coef, "mix", steps, rows)
-    return {t: field[t] + moved[t] + column(field[t], coef.get("column", t)) for t in rows}
+def gaps(fields, rows):
+    turned = [{t: east(field[t]) for t in rows} for field in fields]
+    to_east = [{t: turn[t] - field[t] for t in rows} for turn, field in zip(turned, fields)]
+    faces = range(rows[0] - 1, rows[-1] + 1)
+    to_north = [{t: field[t + 1] - field[t] for t in faces} for field in fields]
+    return list(zip(to_east, to_north))
+
+
+def fluxes(coefs, kind, steps):
+    return [
+        (
+            {t: coef.get("east_" + kind, t) * to_east[t] for t in to_east},
+            {t: coef.get("north_" + kind, t) * to_north[t] for t in to_north},
+        )
+        for coef, (to_east, to_north) in zip(coefs, steps)
+    ]
+
+
+def both(ones, others):
+    return [
+        tuple({t: a[t] + b[t] for t in a} for a, b in zip(one, other)) for one, other in zip(ones, others)
+    ]
+
+
+def gathered_in(flux, rows, fields=None, coefs=None):
+    turned = [{t: west(across[t]) for t in rows} for across, _ in flux]
+    still = [{t: along[t] - along[t - 1] for t in rows} for _, along in flux]
+    if fields is not None:
+        still = [
+            {t: rest[t] + (field[t] + column(field[t], coef.get("column", t))) for t in rows}
+            for rest, field, coef in zip(still, fields, coefs)
+        ]
+    return [
+        {t: rest[t] + (across[t] - turn[t]) for t in rows}
+        for rest, (across, _), turn in zip(still, flux, turned)
+    ]
 
 
 def face_maps(own_maps, near, far, maps, base):
@@ -205,8 +224,8 @@
             high = near[at : at + STEPS, :]
             whole.append(jnp.concatenate([low, own_maps[j, 4 * a : 4 * a + 4, :], high, high, high], axis=0))
         mix, heading, depth = whole
-        blocks = [depth] + [jnp.minimum(depth, f(depth)) for f in (east, west, north)]
-        blocks += [0.5 * (x + f(x)) for x in (mix, heading) for f in (east, west, north)]
+        blocks = [depth] + [jnp.minimum(depth, f(depth)) for f in (east, north)]
+        blocks += [0.5 * (x + f(x)) for x in (mix, heading) for f in (east, north)]
         for i, block in enumerate(blocks):
             maps[j, 16 * i : 16 * i + 16, :] = block
 
@@ -218,9 +237,9 @@
     low = (label & (LOW_COUNT - 1)).astype(jnp.float32).astype(jnp.bfloat16)
     none = jnp.zeros((levels, LANES), jnp.bfloat16)
     one = jnp.ones((levels, LANES), jnp.bfloat16)
-    picks = [high == jnp.bfloat16(h) for h in range(HIGH_COUNT)]
-    left = [jnp.where(p, part, none) for part in (top, bottom) for p in picks]
-    right = [jnp.where(low == jnp.bfloat16(l), one, none) for l in range(LOW_COUNT)]
+    left = [jnp.where(high == jnp.bfloat16(h), one, none) for h in range(HIGH_COUNT)]
+    picks = [low == jnp.bfloat16(l) for l in range(LOW_COUNT)]
+    right = [jnp.where(p, part, none) for part in (top, bottom) for p in picks]
     return jnp.concatenate(left, axis=0), jnp.concatenate(right, axis=0)
 
 
@@ -235,7 +254,7 @@
     def some_strips(i, carry):
         group = [i * GROUP + u for u in range(GROUP)]
         coefs = [Coefficients(maps, j, levels) for j in group]
-        fields, tangents = [], [None] * GROUP
+        fields, tangents = [], None
         for j in group:
             field = {}
             for s in range(STEPS):
@@ -247,15 +266,17 @@
             fields.append(field)
         for n in range(STEPS):
             rows = list(range(n + 1 - STEPS, 4 + STEPS - n - 1))
-            for u, j in enumerate(group):
-                steps = gaps(fields[u], rows)
-                pushed = spread(coefs[u], "dir", steps, rows)
-                if n > 0:
-                    carried = advance(coefs[u], tangents[u], gaps(tangents[u], rows), rows)
-                    pushed = {t: pushed[t] + carried[t] for t in rows}
-                tangents[u] = pushed
-                if n + 1 < STEPS:
-                    fields[u] = advance(coefs[u], fields[u], steps, rows)
+            steps = gaps(fields, rows)
+            push = fluxes(coefs, "dir", steps)
+            if n == 0:
+                following = gathered_in(push, rows)
+            else:
+                push = both(push, fluxes(coefs, "mix", gaps(tangents, rows)))
+                following = gathered_in(push, rows, tangents, coefs)
+            tangents = following
+            if n + 1 < STEPS:
+                fields = gathered_in(fluxes(coefs, "mix", steps), rows, fields, coefs)
+                for u, j in enumerate(group):
                     for t in range(-1, 5):
                         at = (n * 6 + t + 1) * levels
                         later[j, at : at + levels, :] = fields[u][t]
@@ -278,35 +299,32 @@
 
     lax.fori_loop(0, strips // GROUP, some_strips, 0)
 
-    width = LOW_COUNT * levels
+    width = 2 * LOW_COUNT * levels
     own_level = lax.broadcasted_iota(jnp.int32, (levels, width), 0)
     other_level = lax.broadcasted_iota(jnp.int32, (levels, width), 1) & (levels - 1)
     diagonal = own_level == other_level
     sheets = []
     for pair in range(2):
         for h in range(HIGH_COUNT):
-            both = (
-                grams[pair, h * levels : (h + 1) * levels, :]
-                + grams[pair, (HIGH_COUNT + h) * levels : (HIGH_COUNT + h + 1) * levels, :]
-            )
-            sheets.append(jnp.sum(jnp.where(diagonal, both, 0.0), axis=0, keepdims=True))
-        sheets.append(jnp.zeros((8 - HIGH_COUNT, width), jnp.float32))
+            sheet = jnp.where(diagonal, grams[pair, h * levels : (h + 1) * levels, :], 0.0)
+            sheets.append(jnp.sum(sheet, axis=0, keepdims=True))
+        sheets.append(jnp.zeros((16 - HIGH_COUNT, width), jnp.float32))
     rest = jnp.concatenate(sheets, axis=0)
     parts = []
     for _ in range(3):
         part = rest.astype(jnp.bfloat16)
         rest = rest - part.astype(jnp.float32)
         parts.append(part)
-    at_low = lax.broadcasted_iota(jnp.int32, (width, LANES), 0) >> (levels.bit_length() - 1)
+    at_low = (lax.broadcasted_iota(jnp.int32, (width, LANES), 0) >> (levels.bit_length() - 1)) & (LOW_COUNT - 1)
     of_low = lax.broadcasted_iota(jnp.int32, (width, LANES), 1) & (LOW_COUNT - 1)
     gather = jnp.where(at_low == of_low, 1.0, 0.0).astype(jnp.bfloat16)
     added = jnp.dot(jnp.concatenate(parts, axis=0), gather, preferred_element_type=jnp.float32)
-    added = (added[32:48] + added[16:32]) + added[0:16]
-    here = lax.broadcasted_iota(jnp.int32, (8, LANES), 0)
-    label = lax.broadcasted_iota(jnp.int32, (8, LANES), 1)
+    added = (added[64:96] + added[32:64]) + added[0:32]
+    here = lax.broadcasted_iota(jnp.int32, (16, LANES), 0)
+    label = lax.broadcasted_iota(jnp.int32, (16, LANES), 1)
     totals = [
         jnp.sum(
-            jnp.where(here == (label >> LOW_SHIFT), added[8 * p : 8 * p + 8], 0.0), axis=0, keepdims=True
+            jnp.where(here == (label >> LOW_SHIFT), added[16 * p : 16 * p + 16], 0.0), axis=0, keepdims=True
         )
         for p in range(2)
     ]
@@ -315,12 +333,22 @@
 
 def finish_sums(scales, totals, sums):
     weighted = [scales[p : p + 1, :] * totals[p] for p in range(2)]
-    sums[...] = jnp.concatenate(
-        [totals[p] + scales[2 + p : 3 + p, :] for p in range(2)]
-        + weighted
-        + [jnp.zeros((4, LANES), jnp.float32)],
-        axis=0,
-    )
+    sums[...] = jnp.concatenate(totals + weighted + [scales[4:8, :]], axis=0)
+
+
+def pick_bins(*refs):
+    pieces, binned = refs[:-1], refs[-1]
+    band_own, class_count = binned.shape
+    first = lax.axis_index("lat") * band_own
+    found = [jnp.zeros((2, LANES), jnp.float32) for _ in range(band_own)]
+    for piece in pieces:
+        for at in range(0, piece.shape[0], 8):
+            totals, bands = piece[at : at + 2, :], piece[at + 4 : at + 6, :]
+            for m in range(band_own):
+                hit = bands == (first + m).astype(jnp.float32)
+                found[m] = found[m] + jnp.where(hit, totals, 0.0)
+    whole = jnp.concatenate([jnp.sum(x, axis=0, keepdims=True) for x in found], axis=0)
+    binned[...] = whole[:, :class_count]
 
 
 def adjoint_part(
@@ -372,17 +400,15 @@
         north_total = [{t: 0.0 for t in range(-1, 4)} for _ in group]
         for n in reversed(range(STEPS)):
             rows_out = list(range(-n, 4 + n))
-            for u, j in enumerate(group):
-                steps = gaps(adjoints[u], rows_out)
-                field = fields[u][n]
+            steps = gaps(adjoints, rows_out)
+            base_steps = gaps([fields[u][n] for u in range(GROUP)], list(range(4)))
+            if n > 0:
+                adjoints = gathered_in(fluxes(coefs, "mix", steps), rows_out, adjoints, coefs)
+            for u in range(GROUP):
                 for t in range(4):
-                    gap = east(field[t]) - field[t]
-                    east_total[u][t] = east_total[u][t] + gap * steps[0][t]
+                    east_total[u][t] = east_total[u][t] + base_steps[u][0][t] * steps[u][0][t]
                 for t in range(-1, 4):
-                    gap = field[t + 1] - field[t]
-                    north_total[u][t] = north_total[u][t] + gap * steps[2][t]
-                if n > 0:
-                    adjoints[u] = advance(coefs[u], adjoints[u], steps, rows_out)
+                    north_total[u][t] = north_total[u][t] + base_steps[u][1][t] * steps[u][1][t]
         for u, j in enumerate(group):
             north_part = {
                 t: jnp.where(coefs[u].get("north_open", t), north_total[u][t], 0.0) for t in range(-1, 4)
@@ -419,6 +445,19 @@
     return pairs
 
 
+ADJOINT_AT = 1
+CLASSES_AT = 0
+
+
+def routes(count):
+    bits = count.bit_length() - 1
+    groups = [[1]] if bits % 2 else []
+    for bit in range(bits % 2, bits, 2):
+        one, two = 1 << bit, 2 << bit
+        groups.append([one + two, two, one] if bit == 0 else [one, one + two, two])
+    return groups
+
+
 def vmem(count):
     return [pl.BlockSpec(memory_space=pltpu.VMEM)] * count
 
@@ -457,7 +496,7 @@
         scratch_shapes=[pltpu.VMEM(x.shape, x.dtype) for x in (tracer, diffusivity, direction, column_depth)]
         + [pltpu.SemaphoreType.DMA((4,))],
         compiler_params=params,
-    )(tracer, diffusivity, direction, column_depth)
+    )(*[pltpu.with_memory_space_constraint(x, pltpu.HBM) for x in (tracer, diffusivity, direction, column_depth)])
     far = to_far(far_out)
     near = to_near(near_out)
 
@@ -470,10 +509,16 @@
             jax.ShapeDtypeStruct((halo, LANES), i32),
             jax.ShapeDtypeStruct((8, LANES), f32),
         ),
-        in_specs=vmem(2) + [pl.BlockSpec(memory_space=pltpu.SMEM)],
+        in_specs=[pl.BlockSpec(memory_space=pltpu.HBM)] * 3,
         out_specs=tuple(vmem(4)),
+        scratch_shapes=[
+            pltpu.VMEM(density_class.shape, i32),
+            pltpu.VMEM(weights.shape, f32),
+            pltpu.SMEM(band_of_row.shape, i32),
+            pltpu.SemaphoreType.DMA((3,)),
+        ],
         compiler_params=params,
-    )(density_class, weights, band_of_row)
+    )(*[pltpu.with_memory_space_constraint(x, pltpu.HBM) for x in (density_class, weights, band_of_row)])
     near_classes_out, far_classes_out, near, far = lax.optimization_barrier(
         (near_classes_out, far_classes_out, near, far)
     )
@@ -492,16 +537,14 @@
         cost_estimate=cost(4000),
         scratch_shapes=[
             pltpu.VMEM((strips, 16 * MAP_FIELDS, LANES), f32),
-            pltpu.VMEM((2, 2 * HIGH_COUNT * levels, LOW_COUNT * levels), f32),
+            pltpu.VMEM((2, HIGH_COUNT * levels, 2 * LOW_COUNT * levels), f32),
         ],
         compiler_params=params,
     )(scales, own, own_maps, near, far, own_classes)
 
-    near_sums = to_near(sums)
     far_sums = to_far(sums)
-    gathered = jnp.concatenate([sums, near_sums], axis=0)
-
-    def sensitivities(near_classes, far_classes, far_sums):
+
+    def sensitivities(near_classes, far_classes, near_sums, far_sums):
         return pl.pallas_call(
             adjoint_part,
             name="adjoint_part",
@@ -516,25 +559,30 @@
             compiler_params=params,
         )(own, own_maps, near, far, later, own_classes, near_classes, far_classes, sums, near_sums, far_sums)
 
-    gathered, near_classes, far_classes = lax.optimization_barrier((gathered, near_classes, far_classes))
-    gradient = None
-    step = 2
-    while step < count:
-        other = lax.ppermute(gathered, "lat", [(i, i ^ step) for i in range(count)])
-        if step == 4:
-            gradient = sensitivities(near_classes, far_classes, far_sums)
-            other, gradient = lax.optimization_barrier((other, gradient))
-        gathered = jnp.concatenate([gathered, other], axis=0)
-        if step == 2:
+    gathered, gradient, near_sums = sums, None, None
+    groups = routes(count)
+    for i, group in enumerate(groups):
+        others = [lax.ppermute(gathered, "lat", [(d, d ^ k) for d in range(count)]) for k in group]
+        if i == ADJOINT_AT:
+            gradient = sensitivities(near_classes, far_classes, near_sums, far_sums)
+            *others, gradient = lax.optimization_barrier((*others, gradient))
+        if i == 0:
+            near_sums = others[group.index(1)]
+        pieces = [gathered] + others
+        if i + 1 < len(groups):
+            gathered = jnp.concatenate(pieces, axis=0)
+        if i == CLASSES_AT:
+            gathered, near_classes, far_classes = lax.optimization_barrier((gathered, near_classes, far_classes))
+        if i + 1 == ADJOINT_AT:
             gathered, far_sums = lax.optimization_barrier((gathered, far_sums))
-        step *= 2
-    band_own = weights.shape[0] // count
-    finished = gathered.reshape(count, 8, LANES)[:, :2]
-    wanted = lax.axis_index("lat") * band_own + jnp.arange(band_own)
-    hits = finished[None, :, :, LANES - 1] == wanted[:, None, None].astype(f32)
-    binned = jnp.sum(
-        jnp.where(hits[..., None], finished[None, :, :, : weights.shape[1]], 0.0), axis=(1, 2)
-    )
+    binned = pl.pallas_call(
+        pick_bins,
+        name="pick_bins",
+        out_shape=jax.ShapeDtypeStruct((weights.shape[0] // count, weights.shape[1]), f32),
+        in_specs=vmem(len(pieces)),
+        out_specs=pl.BlockSpec(memory_space=pltpu.VMEM),
+        compiler_params=params,
+    )(*pieces)
     return binned, gradient
 
 

time: 43 us -> 33.7 us (0.78)
  local copies, waits for them, and re-layouts: 5.74 us -> 0 us
  waiting for transfers between devices: 8.52 us -> 6.88 us
  starting transfers between devices: 17.6 us -> 16.3 us
  other arithmetic: 0.76 us -> 0.01 us
  Pallas kernels: 9.22 us -> 9.72 us
    unnamed x15 -> x0, local copies, waits for them, and re-layouts: 5.66 us -> none
    ppermute x3 -> x6, waiting for transfers between devices: 3.72 us -> 2.45 us  [body(): lax.ppermute(gathered, 'lat', [(d, d ^ k) for d in range(count)])]
    ppermute x3 -> x2, starting transfers between devices: 4.46 us -> 3.4 us  [to_near(): return lax.ppermute(x, 'lat', near_pairs(count))]
    pallas_call x1, Pallas kernels: 3.79 us -> 2.88 us  [body(): pl.pallas_call(forward, name='forward', out_shape=(jax.ShapeDtypeStruct((...]
    ppermute x3 -> x2, waiting for transfers between devices: 0.83 us -> 0.01 us  [to_near(): return lax.ppermute(x, 'lat', near_pairs(count))]
    pallas_call x1, Pallas kernels: 0.86 us -> 1.58 us  [body(): pl.pallas_call(pack_fields, name='pack_fields', out_shape=(jax.ShapeDtype...]
    reduce_sum x1 -> x0, other arithmetic: 0.67 us -> none  [body(): jnp.sum(jnp.where(hits[..., None], finished[None, :, :, :weights.shape[1]...]
    pallas_call x0 -> x1, Pallas kernels: none -> 0.59 us  [body(): pl.pallas_call(pick_bins, name='pick_bins', out_shape=jax.ShapeDtypeStruc...]
  transfers between devices with their start and end apart: 9 -> 11, of which waited for: 5 -> 5; matrix products, arithmetic and copies ran while one was open for 0% -> 0% of each run, Pallas kernels for 20% -> 23%
where the time goes in v4:
time: 33.7 us; the launch traced here: 33.5 us
  starting transfers between devices  16.3 us (48%)
  Pallas kernels  9.72 us (29%)
  waiting for transfers between devices  6.88 us (20%)
  between operations  0.68 us (2%)
    ppermute x6, starting transfers between devices, body(): lax.ppermute(gathered, 'lat', [(d, d ^ k) for d in range(count)])  7.31 us
    ppermute x3, starting transfers between devices, to_far(): return lax.ppermute(x, ('members', 'lat'), far_pairs(members, count))  5.55 us
    ppermute x3, waiting for transfers between devices, to_far(): return lax.ppermute(x, ('members', 'lat'), far_pairs(members, count))  4.43 us
    ppermute x2, starting transfers between devices, to_near(): return lax.ppermute(x, 'lat', near_pairs(count))  3.4 us
    pallas_call x1, Pallas kernels, sensitivities(): pl.pallas_call(adjoint_part, name='adjoint_part', out_shape=jax.ShapeDtyp...  3.26 us
    pallas_call x1, Pallas kernels, body(): pl.pallas_call(forward, name='forward', out_shape=(jax.ShapeDtypeStruct((...  2.88 us
    ppermute x6, waiting for transfers between devices, body(): lax.ppermute(gathered, 'lat', [(d, d ^ k) for d in range(count)])  2.45 us
    pallas_call x1, Pallas kernels, body(): pl.pallas_call(pack_fields, name='pack_fields', out_shape=(jax.ShapeDtype...  1.58 us
  transfers between devices with their start and end apart: 11, of which 5 were waited for; matrix products, arithmetic and copies ran while one was open for 0% of the time, Pallas kernels for 23%

profile of v4, /device:TPU:0, one launch (start us, length us, event | category | flops | bytes accessed | tf_op | source)
XLA Modules:
  0.0 33.5 jit_solution(1647266155896595912)
XLA Ops:
  0.6 1.6 %pack_fields.1 = (f32[12,64,128]{2,1,0:T(8,128)S(1)}, f32[12,16,128]{2,1,0:T(8,128)S(1)}, f32[684,128]{1,0:T(8,128)S(1)}, f32[684,128]{1,0:T(8,128)S(1)}) custom-call(f32[16,4,1440]{2,1,0:T(4,128)} %refs_0_.3, f32[4,1440]{1,0:T(4,128)} %refs_1_.3, f32[4,1440]{1,0:T(4,128)} %refs_2_.3, s32[4,1440]{1,0:T(4,128)} %refs_3_.1), custom_call_target="tpu_custom_call" | custom-call | tf_op jit(solution)/shard_map/pack_fields/pallas_call | solution.py:485
  2.2 0.5 %collective-permute-start = (f32[684,128]{1,0:T(8,128)S(1)}, f32[684,128]{1,0:T(8,128)S(1)}, u32[]{:S(2)}, u32[]{:S(2)}) collective-permute-start(f32[684,128]{1,0:T(8,128)S(1)} %get-tuple-element.30), channel_id=1, source_target_pairs={{0,1},{1,0},{2,3},{3,2},{4,5},{5,4},{6,7},{7,6},{8,9},{9,8},{10,11... | collective-permute-start | bytes 1050632 | tf_op jit(solution)/shard_map/ppermute | solution.py:480
  2.7 2.6 %collective-permute-start.1 = (f32[684,128]{1,0:T(8,128)S(1)}, f32[684,128]{1,0:T(8,128)S(1)}, u32[]{:S(2)}, u32[]{:S(2)}) collective-permute-start(f32[684,128]{1,0:T(8,128)S(1)} %get-tuple-element.31), channel_id=1, source_target_pairs={{1,2},{2,1},{3,4},{4,3},{5,6},{6,5},{7,8},{8,7},{9,10},{10,9},{11,... | collective-permute-start | bytes 1050632 | tf_op jit(solution)/shard_map/ppermute | solution.py:483
  5.3 1.4 %pack_classes.1 = (s32[12,64,128]{2,1,0:T(8,128)S(1)}, s32[576,128]{1,0:T(8,128)S(1)}, s32[576,128]{1,0:T(8,128)S(1)}, f32[8,128]{1,0:T(8,128)S(1)}) custom-call(s32[16,4,1440]{2,1,0:T(4,128)} %refs_0_.2, f32[32,72]{1,0:T(8,128)} %refs_1_.2, s32[4]{0:T(128)} %refs_2_.2), custom_call_target="tpu_custom_call" | custom-call | tf_op jit(solution)/shard_map/pack_classes/pallas_call | solution.py:503
  6.7 0.0 collective-permute-done.near
  6.7 3.9 %collective-permute-done.1.far = f32[684,128]{1,0:T(8,128)S(1)} collective-permute-done((f32[684,128]{1,0:T(8,128)S(1)}, f32[684,128]{1,0:T(8,128)S(1)}, u32[]{:S(2)}, u32[]{:S(2)}) %collective-permute-start.1) | collective-permute-done | bytes 350240 | tf_op jit(solution)/shard_map/ppermute | solution.py:483
  10.6 2.9 %collective-permute-start.5 = (s32[576,128]{1,0:T(8,128)S(1)}, s32[576,128]{1,0:T(8,128)S(1)}, u32[]{:S(2)}, u32[]{:S(2)}) collective-permute-start(s32[576,128]{1,0:T(8,128)S(1)} %get-tuple-element.36), channel_id=1, source_target_pairs={{0,1},{1,0},{2,3},{3,2},{4,5},{5,4},{6,7},{7,6},{8,9},{9,8},{10,11... | collective-permute-start | bytes 884744 | tf_op jit(solution)/shard_map/ppermute | solution.py:480
  13.5 1.5 %collective-permute-start.6 = (s32[576,128]{1,0:T(8,128)S(1)}, s32[576,128]{1,0:T(8,128)S(1)}, u32[]{:S(2)}, u32[]{:S(2)}) collective-permute-start(s32[576,128]{1,0:T(8,128)S(1)} %get-tuple-element.37), channel_id=1, source_target_pairs={{1,2},{2,1},{3,4},{4,3},{5,6},{6,5},{7,8},{8,7},{9,10},{10,9},{11,... | collective-permute-start | bytes 884744 | tf_op jit(solution)/shard_map/ppermute | solution.py:483
  15.0 2.9 %forward.1 = (f32[8,128]{1,0:T(8,128)S(1)}, f32[12,192,128]{2,1,0:T(8,128)S(1)}) custom-call(f32[8,128]{1,0:T(8,128)S(1)} %get-tuple-element.25.scales, f32[12,64,128]{2,1,0:T(8,128)S(1)} %get-tuple-element.26.own, f32[12,16,128]{2,1,0:T(8,128)S(1)} %get-tuple-element.27.own_maps, f32[684,128]{1,0:T(8,128)S(1)} %collective-permute-done.near, ...), custom_call_target="tpu_custom_call" | custom-call | flops 4614000128 | bytes 14760000 | tf_op jit(solution)/shard_map/forward/pallas_call | solution.py:528
  17.9 1.1 %collective-permute-start.4 = (f32[8,128]{1,0:T(8,128)S(1)}, f32[8,128]{1,0:T(8,128)S(1)}, u32[]{:S(2)}, u32[]{:S(2)}) collective-permute-start(f32[8,128]{1,0:T(8,128)S(1)} %get-tuple-element.35.own_sums), channel_id=1, source_target_pairs={{0,1},{1,0},{2,3},{3,2},{4,5},{5,4},{6,7},{7,6},{8,9},{9,8},{10,11... | collective-permute-start | bytes 12296 | tf_op jit(solution)/shard_map/ppermute | solution.py:565
  18.9 1.9 %collective-permute-start.3 = (f32[8,128]{1,0:T(8,128)S(1)}, f32[8,128]{1,0:T(8,128)S(1)}, u32[]{:S(2)}, u32[]{:S(2)}) collective-permute-start(f32[8,128]{1,0:T(8,128)S(1)} %get-tuple-element.35.own_sums), channel_id=1, source_target_pairs={{0,2},{1,3},{2,0},{3,1},{4,6},{5,7},{6,4},{7,5},{8,10},{9,11},{10,... | collective-permute-start | bytes 12296 | tf_op jit(solution)/shard_map/ppermute | solution.py:565
  20.9 0.0 collective-permute-start.2
  20.9 0.0 collective-permute-done.4.near_sums
  20.9 1.5 %collective-permute-start.7 = (f32[8,128]{1,0:T(8,128)S(1)}, f32[8,128]{1,0:T(8,128)S(1)}, u32[]{:S(2)}, u32[]{:S(2)}) collective-permute-start(f32[8,128]{1,0:T(8,128)S(1)} %get-tuple-element.35.own_sums), channel_id=1, source_target_pairs={{1,2},{2,1},{3,4},{4,3},{5,6},{6,5},{7,8},{8,7},{9,10},{10,9},{11,... | collective-permute-start | bytes 12296 | tf_op jit(solution)/shard_map/ppermute | solution.py:483
  22.4 0.2 collective-permute-done.3
  22.5 1.4 %collective-permute-done.2 = f32[8,128]{1,0:T(8,128)S(1)} collective-permute-done((f32[8,128]{1,0:T(8,128)S(1)}, f32[8,128]{1,0:T(8,128)S(1)}, u32[]{:S(2)}, u32[]{:S(2)}) %collective-permute-start.2) | collective-permute-done | bytes 4128 | tf_op jit(solution)/shard_map/ppermute | solution.py:565
  23.9 0.0 collective-permute-done.5.near_classes
  24.0 0.0 collective-permute-done.6.far_classes
  24.0 0.5 %collective-permute-done.7.far_sums = f32[8,128]{1,0:T(8,128)S(1)} collective-permute-done((f32[8,128]{1,0:T(8,128)S(1)}, f32[8,128]{1,0:T(8,128)S(1)}, u32[]{:S(2)}, u32[]{:S(2)}) %collective-permute-start.7) | collective-permute-done | bytes 4128 | tf_op jit(solution)/shard_map/ppermute | solution.py:483
  24.5 2.9 %collective-permute-start.10 = (f32[32,128]{1,0:T(8,128)S(1)}, f32[32,128]{1,0:T(8,128)S(1)}, u32[]{:S(2)}, u32[]{:S(2)}) collective-permute-start(f32[32,128]{1,0:T(8,128)S(1)} %pad_maximum_fusion.refs_0_), channel_id=1, source_target_pairs={{0,8},{1,9},{2,10},{3,11},{4,12},{5,13},{6,14},{7,15},{8,0},{9,1},... | collective-permute-start | bytes 49160 | tf_op jit(solution)/shard_map/ppermute | solution.py:565
  27.4 1.3 %collective-permute-start.9 = (f32[32,128]{1,0:T(8,128)S(1)}, f32[32,128]{1,0:T(8,128)S(1)}, u32[]{:S(2)}, u32[]{:S(2)}) collective-permute-start(f32[32,128]{1,0:T(8,128)S(1)} %pad_maximum_fusion.refs_0_), channel_id=1, source_target_pairs={{0,12},{1,13},{2,14},{3,15},{4,8},{5,9},{6,10},{7,11},{8,4},{9,5},... | collective-permute-start | bytes 49160 | tf_op jit(solution)/shard_map/ppermute | solution.py:565
  28.8 0.0 collective-permute-start.8
  28.8 3.3 %adjoint_part.1 = f32[4,1440]{1,0:T(4,128)} custom-call(f32[12,64,128]{2,1,0:T(8,128)S(1)} %get-tuple-element.26.own, f32[12,16,128]{2,1,0:T(8,128)S(1)} %get-tuple-element.27.own_maps, f32[684,128]{1,0:T(8,128)S(1)} %collective-permute-done.near, f32[684,128]{1,0:T(8,128)S(1)} %collective-permute-done.1.far, f32[12,192,128]{2,1,0:T(8,128)S(1)} %get-tuple-element.40.later, ...), custom_call_target="tpu_custom_call" | custom-call | flops 4614000128 | bytes 14760000 | tf_op jit(solution)/shard_map/adjoint_part/pallas_call | solution.py:548
  32.1 0.0 collective-permute-done.10.refs_3_
  32.1 0.9 %collective-permute-done.9.refs_2_ = f32[32,128]{1,0:T(8,128)S(1)} collective-permute-done((f32[32,128]{1,0:T(8,128)S(1)}, f32[32,128]{1,0:T(8,128)S(1)}, u32[]{:S(2)}, u32[]{:S(2)}) %collective-permute-start.9) | collective-permute-done | bytes 16416 | tf_op jit(solution)/shard_map/ppermute | solution.py:565
  33.0 0.0 collective-permute-done.8.refs_1_
  33.0 0.6 %pick_bins.1 = f32[2,72]{1,0:T(2,128)} custom-call(f32[32,128]{1,0:T(8,128)S(1)} %pad_maximum_fusion.refs_0_, f32[32,128]{1,0:T(8,128)S(1)} %collective-permute-done.8.refs_1_, f32[32,128]{1,0:T(8,128)S(1)} %collective-permute-done.9.refs_2_, f32[32,128]{1,0:T(8,128)S(1)} %collective-permute-done.10.refs_3_), custom_call_target="tpu_custom_call" | custom-call | tf_op jit(solution)/shard_map/pick_bins/pallas_call | solution.py:578
  (1 shorter events, 0.0 us)
Async XLA Ops:
  2.2 4.5 %collective-permute-start = (f32[684,128]{1,0:T(8,128)S(1)}, f32[684,128]{1,0:T(8,128)S(1)}, u32[]{:S(2)}, u32[]{:S(2)}) collective-permute-start(f32[684,128]{1,0:T(8,128)S(1)} %get-tuple-element.30), channel_id=1, source_target_pairs={{0,1},{1,0},{2,3},{3,2},{4,5},{5,4},{6,7},{7,6},{8,9},{9,8},{10,11... | collective-permute-start | bytes 1050632 | tf_op jit(solution)/shard_map/ppermute | solution.py:480
  2.7 7.9 %collective-permute-start.1 = (f32[684,128]{1,0:T(8,128)S(1)}, f32[684,128]{1,0:T(8,128)S(1)}, u32[]{:S(2)}, u32[]{:S(2)}) collective-permute-start(f32[684,128]{1,0:T(8,128)S(1)} %get-tuple-element.31), channel_id=1, source_target_pairs={{1,2},{2,1},{3,4},{4,3},{5,6},{6,5},{7,8},{8,7},{9,10},{10,9},{11,... | collective-permute-start | bytes 1050632 | tf_op jit(solution)/shard_map/ppermute | solution.py:483
  10.6 13.3 %collective-permute-start.5 = (s32[576,128]{1,0:T(8,128)S(1)}, s32[576,128]{1,0:T(8,128)S(1)}, u32[]{:S(2)}, u32[]{:S(2)}) collective-permute-start(s32[576,128]{1,0:T(8,128)S(1)} %get-tuple-element.36), channel_id=1, source_target_pairs={{0,1},{1,0},{2,3},{3,2},{4,5},{5,4},{6,7},{7,6},{8,9},{9,8},{10,11... | collective-permute-start | bytes 884744 | tf_op jit(solution)/shard_map/ppermute | solution.py:480
  13.5 10.5 %collective-permute-start.6 = (s32[576,128]{1,0:T(8,128)S(1)}, s32[576,128]{1,0:T(8,128)S(1)}, u32[]{:S(2)}, u32[]{:S(2)}) collective-permute-start(s32[576,128]{1,0:T(8,128)S(1)} %get-tuple-element.37), channel_id=1, source_target_pairs={{1,2},{2,1},{3,4},{4,3},{5,6},{6,5},{7,8},{8,7},{9,10},{10,9},{11,... | collective-permute-start | bytes 884744 | tf_op jit(solution)/shard_map/ppermute | solution.py:483
  17.9 3.0 %collective-permute-start.4 = (f32[8,128]{1,0:T(8,128)S(1)}, f32[8,128]{1,0:T(8,128)S(1)}, u32[]{:S(2)}, u32[]{:S(2)}) collective-permute-start(f32[8,128]{1,0:T(8,128)S(1)} %get-tuple-element.35.own_sums), channel_id=1, source_target_pairs={{0,1},{1,0},{2,3},{3,2},{4,5},{5,4},{6,7},{7,6},{8,9},{9,8},{10,11... | collective-permute-start | bytes 12296 | tf_op jit(solution)/shard_map/ppermute | solution.py:565
  18.9 3.6 %collective-permute-start.3 = (f32[8,128]{1,0:T(8,128)S(1)}, f32[8,128]{1,0:T(8,128)S(1)}, u32[]{:S(2)}, u32[]{:S(2)}) collective-permute-start(f32[8,128]{1,0:T(8,128)S(1)} %get-tuple-element.35.own_sums), channel_id=1, source_target_pairs={{0,2},{1,3},{2,0},{3,1},{4,6},{5,7},{6,4},{7,5},{8,10},{9,11},{10,... | collective-permute-start | bytes 12296 | tf_op jit(solution)/shard_map/ppermute | solution.py:565
  20.9 3.1 %collective-permute-start.2 = (f32[8,128]{1,0:T(8,128)S(1)}, f32[8,128]{1,0:T(8,128)S(1)}, u32[]{:S(2)}, u32[]{:S(2)}) collective-permute-start(f32[8,128]{1,0:T(8,128)S(1)} %get-tuple-element.35.own_sums), channel_id=1, source_target_pairs={{0,3},{1,2},{2,1},{3,0},{4,7},{5,6},{6,5},{7,4},{8,11},{9,10},{10,... | collective-permute-start | bytes 12296 | tf_op jit(solution)/shard_map/ppermute | solution.py:565
  20.9 3.6 %collective-permute-start.7 = (f32[8,128]{1,0:T(8,128)S(1)}, f32[8,128]{1,0:T(8,128)S(1)}, u32[]{:S(2)}, u32[]{:S(2)}) collective-permute-start(f32[8,128]{1,0:T(8,128)S(1)} %get-tuple-element.35.own_sums), channel_id=1, source_target_pairs={{1,2},{2,1},{3,4},{4,3},{5,6},{6,5},{7,8},{8,7},{9,10},{10,9},{11,... | collective-permute-start | bytes 12296 | tf_op jit(solution)/shard_map/ppermute | solution.py:483
  24.5 7.6 %collective-permute-start.10 = (f32[32,128]{1,0:T(8,128)S(1)}, f32[32,128]{1,0:T(8,128)S(1)}, u32[]{:S(2)}, u32[]{:S(2)}) collective-permute-start(f32[32,128]{1,0:T(8,128)S(1)} %pad_maximum_fusion.refs_0_), channel_id=1, source_target_pairs={{0,8},{1,9},{2,10},{3,11},{4,12},{5,13},{6,14},{7,15},{8,0},{9,1},... | collective-permute-start | bytes 49160 | tf_op jit(solution)/shard_map/ppermute | solution.py:565
  27.4 5.5 %collective-permute-start.9 = (f32[32,128]{1,0:T(8,128)S(1)}, f32[32,128]{1,0:T(8,128)S(1)}, u32[]{:S(2)}, u32[]{:S(2)}) collective-permute-start(f32[32,128]{1,0:T(8,128)S(1)} %pad_maximum_fusion.refs_0_), channel_id=1, source_target_pairs={{0,12},{1,13},{2,14},{3,15},{4,8},{5,9},{6,10},{7,11},{8,4},{9,5},... | collective-permute-start | bytes 49160 | tf_op jit(solution)/shard_map/ppermute | solution.py:565
  28.8 4.2 %collective-permute-start.8 = (f32[32,128]{1,0:T(8,128)S(1)}, f32[32,128]{1,0:T(8,128)S(1)}, u32[]{:S(2)}, u32[]{:S(2)}) collective-permute-start(f32[32,128]{1,0:T(8,128)S(1)} %pad_maximum_fusion.refs_0_), channel_id=1, source_target_pairs={{0,4},{1,5},{2,6},{3,7},{4,0},{5,1},{6,2},{7,3},{8,12},{9,13},{10,... | collective-permute-start | bytes 49160 | tf_op jit(solution)/shard_map/ppermute | solution.py:565

commit v5 on v4

v5 whole, which is shorter than its diff:
```python
import functools

import jax
import jax.numpy as jnp
from jax import lax
from jax.experimental import pallas as pl
from jax.experimental.pallas import tpu as pltpu
from jax.sharding import PartitionSpec as P

STEPS = 3
vertical_mix = 0.05

LANES = 128
GHOST = 4
OWN = LANES - 2 * GHOST
HIGH_COUNT = 9
LOW_COUNT = 8
LOW_SHIFT = 3
PIECES = (0, 6, 12)
VMEM_LIMIT = 16 * 1024 * 1024


def strip_of(row, j, lon_count):
    first = OWN * j - GHOST
    last = first + LANES
    if first < 0:
        return jnp.concatenate([row[:, first + lon_count :], row[:, :last]], axis=1)
    if last > lon_count:
        return jnp.concatenate([row[:, first:], row[:, : last - lon_count]], axis=1)
    return row[:, first:last]


def piece_of(j):
    return max(p for p in range(len(PIECES) - 1) if PIECES[p] <= j)


def is_odd():
    return lax.rem(lax.axis_index("lat"), 2) == 1


def oriented(ref, t, odd):
    last = ref.shape[1] - 1
    order = level_order(ref.shape[0])
    up = jnp.concatenate([ref[k, t : t + 1, :] for k in order], axis=0)
    down = jnp.concatenate([ref[k, last - t : last - t + 1, :] for k in order], axis=0)
    return jnp.where(odd, down, up)


def bring(sources, held, arrived):
    copies = [pltpu.make_async_copy(a, b, arrived.at[i]) for i, (a, b) in enumerate(zip(sources, held))]
    for copy in copies:
        copy.start()
    for copy in copies:
        copy.wait()


def pack_fields(*refs):
    parts = len(PIECES) - 1
    sources, (own, own_maps, near), fars, held, arrived = (
        refs[:4], refs[4:7], refs[7 : 7 + parts], refs[7 + parts : 11 + parts], refs[11 + parts],
    )
    bring(sources, held, arrived)
    tracer, mix, heading, depth = held
    levels, rows, lon_count = tracer.shape
    strips = lon_count // OWN
    odd = is_odd()

    def far_place(j):
        piece = piece_of(j)
        return fars[piece], j - PIECES[piece], PIECES[piece + 1] - PIECES[piece]

    for t in range(rows):
        field = oriented(tracer, t, odd)
        for j in range(strips):
            strip = strip_of(field, j, lon_count)
            own[j, t * levels : (t + 1) * levels, :] = strip
            if t < STEPS:
                far, local, _ = far_place(j)
                at = (local * STEPS + STEPS - 1 - t) * levels
                far[at : at + levels, :] = strip
            if t > 0:
                at = (j * STEPS + rows - 1 - t) * levels
                near[at : at + levels, :] = strip
    for a, ref in enumerate((mix, heading, depth)):
        field = ref[...].astype(jnp.float32)
        flipped = jnp.concatenate([field[r : r + 1] for r in reversed(range(rows))], axis=0)
        up = jnp.where(odd, flipped, field)
        down = jnp.where(odd, field, flipped)
        for j in range(strips):
            own_maps[j, a * 4 : a * 4 + 4, :] = strip_of(up, j, lon_count)
            strip = strip_of(down, j, lon_count)
            at = strips * STEPS * levels + (3 * j + a) * STEPS
            near[at : at + STEPS, :] = strip[:STEPS]
            far, local, count = far_place(j)
            at = count * STEPS * levels + (3 * local + a) * STEPS
            far[at : at + STEPS, :] = strip[1:]
    own_maps[:, 12:, :] = jnp.zeros_like(own_maps[:, 12:, :])


def pack_classes(*refs):
    sources, (own, scales), held, arrived = refs[:3], refs[3:5], refs[5:8], refs[8]
    bring(sources, held, arrived)
    classes, weights, band_of_row = held
    levels, rows, lon_count = classes.shape
    strips = lon_count // OWN
    odd = is_odd()
    for t in range(rows):
        field = oriented(classes, t, odd)
        for j in range(strips):
            strip = strip_of(field, j, lon_count)
            own[j, t * levels : (t + 1) * levels, :] = strip
    class_count = weights.shape[1]
    scale_rows, band_rows = [], []
    for pair in range(2):
        band = band_of_row[jnp.where(odd, 3 - 2 * pair, 2 * pair)]
        scale = weights[pl.ds(band, 1), :]
        scale_rows.append(jnp.concatenate([scale, jnp.zeros((1, LANES - class_count), jnp.float32)], axis=1))
        band_rows.append(jnp.full((1, LANES), band.astype(jnp.float32)))
    blank = jnp.zeros((2, LANES), jnp.float32)
    scales[...] = jnp.concatenate(scale_rows + [blank] + band_rows + [blank], axis=0)


def east(x):
    return pltpu.roll(x, LANES - 1, 1)


def west(x):
    return pltpu.roll(x, 1, 1)


MAP_FIELDS = 7


def level_order(levels):
    half = levels // 2
    return [2 * (i % half) + i // half for i in range(levels)]


class Coefficients:
    blocks = {
        "wet": 0, "east_open": 1, "north_open": 2,
        "east_mix": 3, "north_mix": 4, "east_dir": 5, "north_dir": 6,
    }

    def __init__(self, maps, j, levels):
        order = lax.broadcasted_iota(jnp.int32, (levels, LANES), 0)
        half = levels // 2
        self.level = (2 * (order & (half - 1)) + jnp.where(order < half, 0, 1)).astype(jnp.float32)
        self.levels = levels
        self.maps = maps
        self.j = j
        self.cache = {}

    def row(self, kind, t):
        at = 16 * self.blocks[kind] + t + STEPS
        return jnp.broadcast_to(self.maps[self.j, at : at + 1, :], (self.levels, LANES))

    def get(self, kind, t):
        if (kind, t) not in self.cache:
            side, _, what = kind.partition("_")
            if kind == "column":
                value = jnp.where(self.level + 1.0 < self.row("wet", t), vertical_mix, 0.0)
            elif kind == "wet" or what == "open":
                value = self.level < self.row(kind, t)
            else:
                value = jnp.where(self.get(side + "_open", t), self.row(kind, t), 0.0)
            self.cache[kind, t] = value
        return self.cache[kind, t]


def column(field, coefficient):
    half = field.shape[0] // 2
    even, odd = field[:half], field[half:]
    after_even = coefficient[:half] * (odd - even)
    after_odd = coefficient[half:] * (pltpu.roll(even, half - 1, 0) - odd)
    return jnp.concatenate([after_even - pltpu.roll(after_odd, 1, 0), after_odd - after_even], axis=0)


def gaps(fields, rows):
    turned = [{t: east(field[t]) for t in rows} for field in fields]
    to_east = [{t: turn[t] - field[t] for t in rows} for turn, field in zip(turned, fields)]
    faces = range(rows[0] - 1, rows[-1] + 1)
    to_north = [{t: field[t + 1] - field[t] for t in faces} for field in fields]
    return list(zip(to_east, to_north))


def fluxes(coefs, kind, steps):
    return [
        (
            {t: coef.get("east_" + kind, t) * to_east[t] for t in to_east},
            {t: coef.get("north_" + kind, t) * to_north[t] for t in to_north},
        )
        for coef, (to_east, to_north) in zip(coefs, steps)
    ]


def both(ones, others):
    return [
        tuple({t: a[t] + b[t] for t in a} for a, b in zip(one, other)) for one, other in zip(ones, others)
    ]


def gathered_in(flux, rows, fields=None, coefs=None):
    turned = [{t: west(across[t]) for t in rows} for across, _ in flux]
    still = [{t: along[t] - along[t - 1] for t in rows} for _, along in flux]
    if fields is not None:
        still = [
            {t: rest[t] + (field[t] + column(field[t], coef.get("column", t))) for t in rows}
            for rest, field, coef in zip(still, fields, coefs)
        ]
    return [
        {t: rest[t] + (across[t] - turn[t]) for t in rows}
        for rest, (across, _), turn in zip(still, flux, turned)
    ]


def face_maps(own_maps, near, fars, maps, strips, levels):
    count, edge = lax.axis_size("lat"), lax.axis_index("lat")
    keep = jnp.where(jnp.logical_and(edge != 0, edge != count - 1), 1.0, 0.0)

    def north(x):
        return pltpu.roll(x, 15, 0)

    for i, j in enumerate(strips):
        whole = []
        piece = piece_of(j)
        for a in range(3):
            at = (PIECES[piece + 1] - PIECES[piece]) * STEPS * levels + (3 * (j - PIECES[piece]) + a) * STEPS
            low = fars[piece][at : at + STEPS, :]
            if a == 2:
                low = low * keep
            at = PIECES[-1] * STEPS * levels + (3 * j + a) * STEPS
            high = near[at : at + STEPS, :]
            whole.append(jnp.concatenate([low, own_maps[j, 4 * a : 4 * a + 4, :], high, high, high], axis=0))
        mix, heading, depth = whole
        blocks = [depth] + [jnp.minimum(depth, f(depth)) for f in (east, north)]
        blocks += [0.5 * (x + f(x)) for x in (mix, heading) for f in (east, north)]
        for b, block in enumerate(blocks):
            maps[i, 16 * b : 16 * b + 16, :] = block


def class_hits(value, label, levels):
    top = value.astype(jnp.bfloat16)
    bottom = (value - top.astype(jnp.float32)).astype(jnp.bfloat16)
    high = (label >> LOW_SHIFT).astype(jnp.float32).astype(jnp.bfloat16)
    low = (label & (LOW_COUNT - 1)).astype(jnp.float32).astype(jnp.bfloat16)
    none = jnp.zeros((levels, LANES), jnp.bfloat16)
    one = jnp.ones((levels, LANES), jnp.bfloat16)
    left = [jnp.where(high == jnp.bfloat16(h), one, none) for h in range(HIGH_COUNT)]
    picks = [low == jnp.bfloat16(l) for l in range(LOW_COUNT)]
    right = [jnp.where(p, part, none) for part in (top, bottom) for p in picks]
    return jnp.concatenate(left, axis=0), jnp.concatenate(right, axis=0)


def later_row(n, t):
    return (n - 1) * 8 + t + STEPS - n


def forward(piece, *refs):
    last = piece + 2 == len(PIECES)
    refs = list(refs)
    own, own_maps, near, far, classes = refs[:5]
    del refs[:5]
    before = refs.pop(0) if piece > 0 else None
    scales = refs.pop(0) if last else None
    out, later, maps = refs[:3]
    grams = refs[3] if last else out
    levels = own.shape[1] // 4
    group = list(range(PIECES[piece], PIECES[piece + 1]))
    face_maps(own_maps, near, {piece: far}, maps, group, levels)
    lane = lax.broadcasted_iota(jnp.int32, (levels, LANES), 1)
    inner = jnp.logical_and(lane >= GHOST, lane < LANES - GHOST)
    coefs = [Coefficients(maps, u, levels) for u in range(len(group))]
    fields, tangents = [], None
    for u, j in enumerate(group):
        field = {t: own[j, t * levels : (t + 1) * levels, :] for t in range(4)}
        for s in range(STEPS):
            at = (u * STEPS + s) * levels
            field[s - STEPS] = far[at : at + levels, :]
            at = (j * STEPS + s) * levels
            field[4 + s] = near[at : at + levels, :]
        fields.append(field)
    for n in range(STEPS):
        rows = list(range(n + 1 - STEPS, 4 + STEPS - n - 1))
        steps = gaps(fields, rows)
        push = fluxes(coefs, "dir", steps)
        if n == 0:
            following = gathered_in(push, rows)
        else:
            push = both(push, fluxes(coefs, "mix", gaps(tangents, rows)))
            following = gathered_in(push, rows, tangents, coefs)
        tangents = following
        if n + 1 < STEPS:
            fields = gathered_in(fluxes(coefs, "mix", steps), rows, fields, coefs)
            for u in range(len(group)):
                for t in rows:
                    at = later_row(n + 1, t) * levels
                    later[u, at : at + levels, :] = fields[u][t]
    for pair in range(2):
        lefts, rights = [], []
        for u, j in enumerate(group):
            for t in (2 * pair, 2 * pair + 1):
                chosen = jnp.logical_and(inner, coefs[u].get("wet", t))
                value = jnp.where(chosen, tangents[u][t], 0.0)
                left, right = class_hits(value, classes[j, t * levels : (t + 1) * levels, :], levels)
                lefts.append(left)
                rights.append(right)
        gram = lax.dot_general(
            jnp.concatenate(lefts, axis=1),
            jnp.concatenate(rights, axis=1),
            (((1,), (1,)), ((), ())),
            preferred_element_type=jnp.float32,
        )
        grams[pair] = gram if before is None else before[pair] + gram
    if last:
        class_sums(grams, scales, out, levels)


def class_sums(grams, scales, sums, levels):
    width = 2 * LOW_COUNT * levels
    own_level = lax.broadcasted_iota(jnp.int32, (levels, width), 0)
    other_level = lax.broadcasted_iota(jnp.int32, (levels, width), 1) & (levels - 1)
    diagonal = own_level == other_level
    sheets = []
    for pair in range(2):
        for h in range(HIGH_COUNT):
            sheet = jnp.where(diagonal, grams[pair, h * levels : (h + 1) * levels, :], 0.0)
            sheets.append(jnp.sum(sheet, axis=0, keepdims=True))
        sheets.append(jnp.zeros((16 - HIGH_COUNT, width), jnp.float32))
    rest = jnp.concatenate(sheets, axis=0)
    parts = []
    for _ in range(3):
        part = rest.astype(jnp.bfloat16)
        rest = rest - part.astype(jnp.float32)
        parts.append(part)
    at_low = (lax.broadcasted_iota(jnp.int32, (width, LANES), 0) >> (levels.bit_length() - 1)) & (LOW_COUNT - 1)
    of_low = lax.broadcasted_iota(jnp.int32, (width, LANES), 1) & (LOW_COUNT - 1)
    gather = jnp.where(at_low == of_low, 1.0, 0.0).astype(jnp.bfloat16)
    added = jnp.dot(jnp.concatenate(parts, axis=0), gather, preferred_element_type=jnp.float32)
    added = (added[64:96] + added[32:64]) + added[0:32]
    here = lax.broadcasted_iota(jnp.int32, (16, LANES), 0)
    label = lax.broadcasted_iota(jnp.int32, (16, LANES), 1)
    totals = [
        jnp.sum(
            jnp.where(here == (label >> LOW_SHIFT), added[16 * p : 16 * p + 16], 0.0), axis=0, keepdims=True
        )
        for p in range(2)
    ]
    finish_sums(scales, totals, sums)


def finish_sums(scales, totals, sums):
    weighted = [scales[p : p + 1, :] * totals[p] for p in range(2)]
    sums[...] = jnp.concatenate(totals + weighted + [scales[4:8, :]], axis=0)


def finish(own_share, near_share, far_share, *refs):
    pieces, binned, gradient = refs[:-2], refs[-2], refs[-1]
    up = own_share[...] + (near_share[...] + far_share[...])
    down = jnp.concatenate([up[t : t + 1] for t in reversed(range(up.shape[0]))], axis=0)
    gradient[...] = jnp.where(is_odd(), down, up)
    band_own, class_count = binned.shape
    first = lax.axis_index("lat") * band_own
    found = [jnp.zeros((2, LANES), jnp.float32) for _ in range(band_own)]
    for piece in pieces:
        for at in range(0, piece.shape[0], 8):
            totals, bands = piece[at : at + 2, :], piece[at + 4 : at + 6, :]
            for m in range(band_own):
                hit = bands == (first + m).astype(jnp.float32)
                found[m] = found[m] + jnp.where(hit, totals, 0.0)
    whole = jnp.concatenate([jnp.sum(x, axis=0, keepdims=True) for x in found], axis=0)
    binned[...] = whole[:, :class_count]


def adjoint_part(own, own_maps, near, classes, sums, *refs):
    parts = len(PIECES) - 1
    fars, laters = refs[:parts], refs[parts : 2 * parts]
    own_share, near_share, far_share, maps = refs[2 * parts :]
    strips = own.shape[0]
    levels = own.shape[1] // 4
    group = list(range(strips))
    face_maps(own_maps, near, fars, maps, group, levels)
    coefs = [Coefficients(maps, j, levels) for j in group]
    adjoints = []
    for j in group:
        adjoint = {}
        for t in range(4):
            label = classes[j, t * levels : (t + 1) * levels, :]
            row = 2 + t // 2
            table = jnp.broadcast_to(sums[row : row + 1, :], (8, LANES))
            value = jnp.concatenate(
                [jnp.take_along_axis(table, label[k : k + 8, :], axis=1) for k in range(0, levels, 8)], axis=0
            )
            adjoint[t] = jnp.where(coefs[j].get("wet", t), value, 0.0)
        adjoints.append(adjoint)

    def base(n, j):
        piece = piece_of(j)
        local = j - PIECES[piece]
        field = {}
        for t in range(n - STEPS, 4 + STEPS - n):
            if n > 0:
                at = later_row(n, t) * levels
                field[t] = laters[piece][local, at : at + levels, :]
            elif t < 0:
                at = (local * STEPS + t + STEPS) * levels
                field[t] = fars[piece][at : at + levels, :]
            elif t < 4:
                field[t] = own[j, t * levels : (t + 1) * levels, :]
            else:
                at = (j * STEPS + t - 4) * levels
                field[t] = near[at : at + levels, :]
        return field

    east_total = [{} for _ in group]
    north_total = [{} for _ in group]
    for n in reversed(range(STEPS)):
        rows = list(range(n + 1 - STEPS, 3 + STEPS - n))
        low, high = rows[0], rows[-1]
        turned = [{t: east(field[t]) for t in rows} for field in adjoints]
        base_steps = gaps([base(n, j) for j in group], rows)
        to_east = [{t: turn[t] - field[t] for t in rows} for turn, field in zip(turned, adjoints)]
        to_north = [
            {low - 1: field[low], high: -field[high], **{t: field[t + 1] - field[t] for t in rows[:-1]}}
            for field in adjoints
        ]
        if n > 0:
            across = [{t: coef.get("east_mix", t) * x[t] for t in rows} for coef, x in zip(coefs, to_east)]
            turned = [{t: west(x[t]) for t in rows} for x in across]
            along = [{t: coef.get("north_mix", t) * x[t] for t in x} for coef, x in zip(coefs, to_north)]
            following = []
            for j in group:
                field, flux = adjoints[j], along[j]
                new = {low - 1: flux[low - 1], high + 1: -flux[high]}
                for t in rows:
                    still = field[t] + column(field[t], coefs[j].get("column", t)) + (flux[t] - flux[t - 1])
                    new[t] = still + (across[j][t] - turned[j][t])
                following.append(new)
            adjoints = following
        for j in group:
            for total, steps, basis in (
                (east_total[j], to_east[j], base_steps[j][0]),
                (north_total[j], to_north[j], base_steps[j][1]),
            ):
                for t in steps:
                    term = steps[t] * basis[t]
                    total[t] = total[t] + term if t in total else term
    strip_shares = []
    east_sums = []
    none = jnp.zeros((1, LANES), jnp.float32)
    for j in group:
        east_sums.append(
            jnp.concatenate(
                [none]
                + [
                    jnp.sum(jnp.where(coefs[j].get("east_open", t), east_total[j][t], 0.0), axis=0, keepdims=True)
                    for t in range(-2, 6)
                ]
                + [none] * 7,
                axis=0,
            )
        )
    turned = [west(x) for x in east_sums]
    for j in group:
        north = {
            t: jnp.sum(jnp.where(coefs[j].get("north_open", t), north_total[j][t], 0.0), axis=0, keepdims=True)
            for t in range(-3, 6)
        }
        north[-4] = north[6] = none
        rows = [north[t] + north[t - 1] for t in range(-3, 7)] + [none] * 6
        strip_shares.append(-0.5 * (jnp.concatenate(rows, axis=0) + (east_sums[j] + turned[j])))
    share = jnp.concatenate([x[:, GHOST : LANES - GHOST] for x in strip_shares], axis=1)

    def take(order):
        return jnp.concatenate([share[t + 3 : t + 4] for t in order], axis=0)

    own_share[...] = share[3:7]
    far_share[...] = jnp.concatenate([take([-1, -2, -3]), jnp.zeros_like(share[:1])], axis=0)
    near_share[...] = jnp.concatenate([jnp.zeros_like(share[:1]), take([6, 5, 4])], axis=0)


def near_pairs(count):
    return [(i, i ^ 1) for i in range(count)]


def far_pairs(members, count):
    pairs = []
    for m in range(members):
        for i in range(1, count - 1, 2):
            pairs += [(m * count + i, m * count + i + 1), (m * count + i + 1, m * count + i)]
        for i in (0, count - 1):
            pairs.append((m * count + i, (m ^ 1) * count + i))
    return pairs


def routes(count):
    bits = count.bit_length() - 1
    groups = [[1]] if bits % 2 else []
    for bit in range(bits % 2, bits, 2):
        one, two = 1 << bit, 2 << bit
        groups.append([one + two, two, one] if bit == 0 else [one, one + two, two])
    return groups


def vmem(count):
    return [pl.BlockSpec(memory_space=pltpu.VMEM)] * count


def cost(nanoseconds):
    return pl.CostEstimate(flops=1153500 * nanoseconds, bytes_accessed=3690 * nanoseconds, transcendentals=0)


def body(tracer, diffusivity, direction, column_depth, density_class, band_of_row, weights):
    levels, rows, lon_count = tracer.shape
    strips = lon_count // OWN
    count = lax.axis_size("lat")
    members = lax.axis_size("members")
    params = pltpu.CompilerParams(vmem_limit_bytes=VMEM_LIMIT)
    f32, i32 = jnp.float32, jnp.int32
    halo = strips * STEPS * levels
    payload = halo + strips * 9

    def to_near(x):
        return lax.ppermute(x, "lat", near_pairs(count))

    def to_far(x):
        return lax.ppermute(x, ("members", "lat"), far_pairs(members, count))

    sizes = [b - a for a, b in zip(PIECES, PIECES[1:])]
    fields = (tracer, diffusivity, direction, column_depth)
    own, own_maps, near_out, *fars_out = pl.pallas_call(
        pack_fields,
        name="pack_fields",
        out_shape=(
            jax.ShapeDtypeStruct((strips, rows * levels, LANES), f32),
            jax.ShapeDtypeStruct((strips, 16, LANES), f32),
            jax.ShapeDtypeStruct((payload, LANES), f32),
        )
        + tuple(jax.ShapeDtypeStruct((payload // strips * size, LANES), f32) for size in sizes),
        in_specs=[pl.BlockSpec(memory_space=pltpu.HBM)] * 4,
        out_specs=tuple(vmem(3 + len(sizes))),
        scratch_shapes=[pltpu.VMEM(x.shape, x.dtype) for x in fields] + [pltpu.SemaphoreType.DMA((4,))],
        compiler_params=params,
    )(*[pltpu.with_memory_space_constraint(x, pltpu.HBM) for x in fields])
    fars = [to_far(x) for x in fars_out]
    near = to_near(near_out)

    own_classes, scales = pl.pallas_call(
        pack_classes,
        name="pack_classes",
        out_shape=(
            jax.ShapeDtypeStruct((strips, rows * levels, LANES), i32),
            jax.ShapeDtypeStruct((8, LANES), f32),
        ),
        in_specs=[pl.BlockSpec(memory_space=pltpu.HBM)] * 3,
        out_specs=tuple(vmem(2)),
        scratch_shapes=[
            pltpu.VMEM(density_class.shape, i32),
            pltpu.VMEM(weights.shape, f32),
            pltpu.SMEM(band_of_row.shape, i32),
            pltpu.SemaphoreType.DMA((3,)),
        ],
        compiler_params=params,
    )(*[pltpu.with_memory_space_constraint(x, pltpu.HBM) for x in (density_class, weights, band_of_row)])
    laters, sums = [], None
    gram_shape = (2, HIGH_COUNT * levels, 2 * LOW_COUNT * levels)
    for piece, size in enumerate(sizes):
        last = piece + 1 == len(sizes)
        given = [own, own_maps, near, fars[piece], own_classes]
        given += ([sums] if piece > 0 else []) + ([scales] if last else [])
        sums, later = pl.pallas_call(
            functools.partial(forward, piece),
            name="forward",
            out_shape=(
                jax.ShapeDtypeStruct((8, LANES) if last else gram_shape, f32),
                jax.ShapeDtypeStruct((size, 14 * levels, LANES), f32),
            ),
            in_specs=vmem(len(given)),
            out_specs=tuple(vmem(2)),
            cost_estimate=cost(2000),
            scratch_shapes=[pltpu.VMEM((size, 16 * MAP_FIELDS, LANES), f32)]
            + ([pltpu.VMEM(gram_shape, f32)] if last else []),
            compiler_params=params,
        )(*given)
        laters.append(later)

    gathered, shares = sums, None
    groups = routes(count)
    for i, group in enumerate(groups):
        others = [lax.ppermute(gathered, "lat", [(d, d ^ k) for d in range(count)]) for k in group]
        if i == 0:
            shares = pl.pallas_call(
                adjoint_part,
                name="adjoint_part",
                out_shape=(jax.ShapeDtypeStruct((rows, lon_count), f32),) * 3,
                in_specs=vmem(5 + 2 * len(sizes)),
                out_specs=tuple(vmem(3)),
                scratch_shapes=[pltpu.VMEM((strips, 16 * MAP_FIELDS, LANES), f32)],
                compiler_params=params,
            )(own, own_maps, near, own_classes, sums, *fars, *laters)
        pieces = [gathered] + others
        if i == 0:
            *pieces, own_share, near_share, far_share = lax.optimization_barrier((*pieces, *shares))
            near_share, far_share = to_near(near_share), to_far(far_share)
        if i + 1 < len(groups):
            gathered = jnp.concatenate(pieces, axis=0)
    binned, gradient = pl.pallas_call(
        finish,
        name="finish",
        out_shape=(
            jax.ShapeDtypeStruct((weights.shape[0] // count, weights.shape[1]), f32),
            jax.ShapeDtypeStruct((rows, lon_count), f32),
        ),
        in_specs=vmem(3 + len(pieces)),
        out_specs=tuple(vmem(2)),
        compiler_params=params,
    )(own_share, near_share, far_share, *pieces)
    return binned, gradient


def solution(mesh):
    placed = (
        P(None, ("members", "lat"), None),
        P("lat", None),
        P(("members", "lat"), None),
        P("lat", None),
        P(None, ("members", "lat"), None),
        P("lat"),
        P(),
    )
    return jax.shard_map(
        body,
        mesh=mesh,
        in_specs=placed,
        out_specs=(P(("members", "lat"), None), P(("members", "lat"), None)),
        check_vma=False,
    )
```

time: 33.7 us -> 31 us (0.920)
  starting transfers between devices: 16.3 us -> 14 us
  Pallas kernels: 9.72 us -> 9.36 us
    ppermute x2, starting transfers between devices: 3.4 us -> 0.68 us  [to_near(): return lax.ppermute(x, 'lat', near_pairs(count))]
    ppermute x3, waiting for transfers between devices: 4.43 us -> 2.39 us  [to_far(): return lax.ppermute(x, ('members', 'lat'), far_pairs(members, count))]
    ppermute x6, waiting for transfers between devices: 2.45 us -> 4.39 us  [body(): lax.ppermute(gathered, 'lat', [(d, d ^ k) for d in range(count)])]
    ppermute x6, starting transfers between devices: 7.31 us -> 9.22 us  [body(): lax.ppermute(gathered, 'lat', [(d, d ^ k) for d in range(count)])]
    ppermute x3, starting transfers between devices: 5.55 us -> 4.13 us  [to_far(): return lax.ppermute(x, ('members', 'lat'), far_pairs(members, count))]
    pallas_call x3 -> x4, Pallas kernels: 6.73 us -> 6.36 us  [the longest x2 3.22 us: body(): pl.pallas_call(functools.partial(forward, piece), name='forward', out_sha...]
  transfers between devices with their start and end apart: 11 -> 11, of which waited for: 5 -> 5; matrix products, arithmetic and copies ran while one was open for 0% -> 0% of each run, Pallas kernels for 23% -> 18%
where the time goes in v5:
time: 31 us; the launch traced here: 30.9 us
  starting transfers between devices  14 us (45%)
  Pallas kernels  9.36 us (30%)
  waiting for transfers between devices  6.79 us (22%)
  between operations  0.7 us (2%)
    ppermute x6, starting transfers between devices, body(): lax.ppermute(gathered, 'lat', [(d, d ^ k) for d in range(count)])  9.22 us
    ppermute x6, waiting for transfers between devices, body(): lax.ppermute(gathered, 'lat', [(d, d ^ k) for d in range(count)])  4.39 us
    ppermute x3, starting transfers between devices, to_far(): return lax.ppermute(x, ('members', 'lat'), far_pairs(members, count))  4.13 us
    pallas_call x2, Pallas kernels, body(): pl.pallas_call(functools.partial(forward, piece), name='forward', out_sha...  3.22 us
    pallas_call x1, Pallas kernels, body(): pl.pallas_call(adjoint_part, name='adjoint_part', out_shape=(jax.ShapeDty...  2.51 us
    ppermute x3, waiting for transfers between devices, to_far(): return lax.ppermute(x, ('members', 'lat'), far_pairs(members, count))  2.39 us
    pallas_call x1, Pallas kernels, body(): pl.pallas_call(pack_fields, name='pack_fields', out_shape=(jax.ShapeDtype...  1.58 us
    pallas_call x1, Pallas kernels, body(): pl.pallas_call(pack_classes, name='pack_classes', out_shape=(jax.ShapeDty...  1.42 us
  transfers between devices with their start and end apart: 11, of which 5 were waited for; matrix products, arithmetic and copies ran while one was open for 0% of the time, Pallas kernels for 18%

profile of v5, /device:TPU:0, one launch (start us, length us, event | category | flops | bytes accessed | tf_op | source)
XLA Modules:
  0.0 30.9 jit_solution(717426604450509292)
XLA Ops:
  0.6 1.6 %pack_fields.1 = (f32[12,64,128]{2,1,0:T(8,128)S(1)}, f32[12,16,128]{2,1,0:T(8,128)S(1)}, f32[684,128]{1,0:T(8,128)S(1)}, f32[342,128]{1,0:T(8,128)S(1)}, f32[342,128]{1,0:T(8,128)S(1)}) custom-call(f32[16,4,1440]{2,1,0:T(4,128)} %refs_0_.2, f32[4,1440]{1,0:T(4,128)} %refs_1_.2, f32[4,1440]{1,0:T(4,128)} %refs_2_.2, s32[4,1440]{1,0:T(4,128)} %refs_3_.1), custom_call_target="tpu_custom_call" | custom-call | tf_op jit(solution)/shard_map/pack_fields/pallas_call | solution.py:531
  2.2 0.5 %collective-permute-start = (f32[684,128]{1,0:T(8,128)S(1)}, f32[684,128]{1,0:T(8,128)S(1)}, u32[]{:S(2)}, u32[]{:S(2)}) collective-permute-start(f32[684,128]{1,0:T(8,128)S(1)} %get-tuple-element.25), channel_id=1, source_target_pairs={{0,1},{1,0},{2,3},{3,2},{4,5},{5,4},{6,7},{7,6},{8,9},{9,8},{10,11... | collective-permute-start | bytes 1050632 | tf_op jit(solution)/shard_map/ppermute | solution.py:524
  2.7 2.6 %collective-permute-start.2 = (f32[342,128]{1,0:T(8,128)S(1)}, f32[342,128]{1,0:T(8,128)S(1)}, u32[]{:S(2)}, u32[]{:S(2)}) collective-permute-start(f32[342,128]{1,0:T(8,128)S(1)} %get-tuple-element.28), channel_id=1, source_target_pairs={{1,2},{2,1},{3,4},{4,3},{5,6},{6,5},{7,8},{8,7},{9,10},{10,9},{11,... | collective-permute-start | bytes 525320 | tf_op jit(solution)/shard_map/ppermute | solution.py:527
  5.3 0.1 collective-permute-start.1
  5.4 1.4 %pack_classes.1 = (s32[12,64,128]{2,1,0:T(8,128)S(1)}, f32[8,128]{1,0:T(8,128)S(1)}) custom-call(s32[16,4,1440]{2,1,0:T(4,128)} %refs_0_.3, f32[32,72]{1,0:T(8,128)} %refs_1_.3, s32[4]{0:T(128)} %refs_2_.3), custom_call_target="tpu_custom_call" | custom-call | tf_op jit(solution)/shard_map/pack_classes/pallas_call | solution.py:548
  6.8 1.9 %collective-permute-done.2.refs_3_.refs_0_ = f32[342,128]{1,0:T(8,128)S(1)} collective-permute-done((f32[342,128]{1,0:T(8,128)S(1)}, f32[342,128]{1,0:T(8,128)S(1)}, u32[]{:S(2)}, u32[]{:S(2)}) %collective-permute-start.2) | collective-permute-done | bytes 175136 | tf_op jit(solution)/shard_map/ppermute | solution.py:527
  8.7 0.0 collective-permute-done.refs_2_.near
  8.7 1.5 %forward.2 = (f32[2,144,256]{2,1,0:T(8,128)S(1)}, f32[6,224,128]{2,1,0:T(8,128)S(1)}) custom-call(f32[12,64,128]{2,1,0:T(8,128)S(1)} %get-tuple-element.23.refs_0_.own, f32[12,16,128]{2,1,0:T(8,128)S(1)} %get-tuple-element.24.refs_1_.own_maps, f32[684,128]{1,0:T(8,128)S(1)} %collective-permute-done.refs_2_.near, ...), custom_call_target="tpu_custom_call" | custom-call | flops 2307000064 | bytes 7380000 | tf_op jit(solution)/shard_map/forward/pallas_call | solution.py:571
  10.3 0.5 %collective-permute-done.1.refs_3_.refs_1_ = f32[342,128]{1,0:T(8,128)S(1)} collective-permute-done((f32[342,128]{1,0:T(8,128)S(1)}, f32[342,128]{1,0:T(8,128)S(1)}, u32[]{:S(2)}, u32[]{:S(2)}) %collective-permute-start.1) | collective-permute-done | bytes 175136 | tf_op jit(solution)/shard_map/ppermute | solution.py:527
  10.8 1.7 %forward.3 = (f32[8,128]{1,0:T(8,128)S(1)}, f32[6,224,128]{2,1,0:T(8,128)S(1)}) custom-call(f32[12,64,128]{2,1,0:T(8,128)S(1)} %get-tuple-element.23.refs_0_.own, f32[12,16,128]{2,1,0:T(8,128)S(1)} %get-tuple-element.24.refs_1_.own_maps, f32[684,128]{1,0:T(8,128)S(1)} %collective-permute-done.refs_2_.near, ...), custom_call_target="tpu_custom_call" | custom-call | flops 2307000064 | bytes 7380000 | tf_op jit(solution)/shard_map/forward/pallas_call | solution.py:571
  12.4 2.8 %collective-permute-start.5 = (f32[8,128]{1,0:T(8,128)S(1)}, f32[8,128]{1,0:T(8,128)S(1)}, u32[]{:S(2)}, u32[]{:S(2)}) collective-permute-start(f32[8,128]{1,0:T(8,128)S(1)} %get-tuple-element.40.sums), channel_id=1, source_target_pairs={{0,1},{1,0},{2,3},{3,2},{4,5},{5,4},{6,7},{7,6},{8,9},{9,8},{10,11... | collective-permute-start | bytes 12296 | tf_op jit(solution)/shard_map/ppermute | solution.py:590
  15.2 2.4 %collective-permute-start.4 = (f32[8,128]{1,0:T(8,128)S(1)}, f32[8,128]{1,0:T(8,128)S(1)}, u32[]{:S(2)}, u32[]{:S(2)}) collective-permute-start(f32[8,128]{1,0:T(8,128)S(1)} %get-tuple-element.40.sums), channel_id=1, source_target_pairs={{0,2},{1,3},{2,0},{3,1},{4,6},{5,7},{6,4},{7,5},{8,10},{9,11},{10,... | collective-permute-start | bytes 12296 | tf_op jit(solution)/shard_map/ppermute | solution.py:590
  17.7 0.1 collective-permute-start.3
  17.8 2.5 %adjoint_part.1 = (f32[4,1440]{1,0:T(4,128)S(1)}, f32[4,1440]{1,0:T(4,128)S(1)}, f32[4,1440]{1,0:T(4,128)S(1)}) custom-call(f32[12,64,128]{2,1,0:T(8,128)S(1)} %get-tuple-element.23.refs_0_.own, f32[12,16,128]{2,1,0:T(8,128)S(1)} %get-tuple-element.24.refs_1_.own_maps, f32[684,128]{1,0:T(8,128)S(1)} %collective-permute-done.refs_2_.near, ...), custom_call_target="tpu_custom_call" | custom-call | tf_op jit(solution)/shard_map/adjoint_part/pallas_call | solution.py:592
  20.3 0.0 collective-permute-done.5
  20.3 0.0 collective-permute-done.4
  20.3 0.4 %collective-permute-done.3 = f32[8,128]{1,0:T(8,128)S(1)} collective-permute-done((f32[8,128]{1,0:T(8,128)S(1)}, f32[8,128]{1,0:T(8,128)S(1)}, u32[]{:S(2)}, u32[]{:S(2)}) %collective-permute-start.3) | collective-permute-done | bytes 4128 | tf_op jit(solution)/shard_map/ppermute | solution.py:590
  20.7 0.2 collective-permute-start.6
  20.9 1.5 %collective-permute-start.7 = (f32[4,1440]{1,0:T(4,128)S(1)}, f32[4,1440]{1,0:T(4,128)S(1)}, u32[]{:S(2)}, u32[]{:S(2)}) collective-permute-start(f32[4,1440]{1,0:T(4,128)S(1)} %get-tuple-element.39), channel_id=1, source_target_pairs={{1,2},{2,1},{3,4},{4,3},{5,6},{6,5},{7,8},{8,7},{9,10},{10,9},{11,... | collective-permute-start | bytes 69128 | tf_op jit(solution)/shard_map/ppermute | solution.py:527
  22.4 2.3 %collective-permute-start.10 = (f32[32,128]{1,0:T(8,128)S(1)}, f32[32,128]{1,0:T(8,128)S(1)}, u32[]{:S(2)}, u32[]{:S(2)}) collective-permute-start(f32[32,128]{1,0:T(8,128)S(1)} %constant_dynamic-update-slice_fusion.refs_0_), channel_id=1, source_target_pairs={{0,8},{1,9},{2,10},{3,11},{4,12},{5,13},{6,14},{7,15},{8,0},{9,1},... | collective-permute-start | bytes 49160 | tf_op jit(solution)/shard_map/ppermute | solution.py:590
  24.7 1.3 %collective-permute-start.9 = (f32[32,128]{1,0:T(8,128)S(1)}, f32[32,128]{1,0:T(8,128)S(1)}, u32[]{:S(2)}, u32[]{:S(2)}) collective-permute-start(f32[32,128]{1,0:T(8,128)S(1)} %constant_dynamic-update-slice_fusion.refs_0_), channel_id=1, source_target_pairs={{0,12},{1,13},{2,14},{3,15},{4,8},{5,9},{6,10},{7,11},{8,4},{9,5},... | collective-permute-start | bytes 49160 | tf_op jit(solution)/shard_map/ppermute | solution.py:590
  26.1 0.2 collective-permute-start.8
  26.3 0.7 %collective-permute-done.10.refs_3_ = f32[32,128]{1,0:T(8,128)S(1)} collective-permute-done((f32[32,128]{1,0:T(8,128)S(1)}, f32[32,128]{1,0:T(8,128)S(1)}, u32[]{:S(2)}, u32[]{:S(2)}) %collective-permute-start.10) | collective-permute-done | bytes 16416 | tf_op jit(solution)/shard_map/ppermute | solution.py:590
  27.0 3.2 %collective-permute-done.9.refs_2_ = f32[32,128]{1,0:T(8,128)S(1)} collective-permute-done((f32[32,128]{1,0:T(8,128)S(1)}, f32[32,128]{1,0:T(8,128)S(1)}, u32[]{:S(2)}, u32[]{:S(2)}) %collective-permute-start.9) | collective-permute-done | bytes 16416 | tf_op jit(solution)/shard_map/ppermute | solution.py:590
  30.2 0.0 collective-permute-done.8.refs_1_
  30.2 0.0 collective-permute-done.6.near_share
  30.3 0.0 collective-permute-done.7.far_share
  30.3 0.6 %finish.1 = (f32[2,72]{1,0:T(2,128)}, f32[4,1440]{1,0:T(4,128)}) custom-call(f32[4,1440]{1,0:T(4,128)S(1)} %get-tuple-element.37.own_share, f32[4,1440]{1,0:T(4,128)S(1)} %collective-permute-done.6.near_share, f32[4,1440]{1,0:T(4,128)S(1)} %collective-permute-done.7.far_share, f32[32,128]{1,0:T(8,128)S(1)} %constant_dynamic-update-slice_fusion.refs_0_, ...), custom_call_target="tpu_custom_call" | custom-call | tf_op jit(solution)/shard_map/finish/pallas_call | solution.py:607
  (4 shorter events, 0.0 us)
Async XLA Ops:
  2.2 6.5 %collective-permute-start = (f32[684,128]{1,0:T(8,128)S(1)}, f32[684,128]{1,0:T(8,128)S(1)}, u32[]{:S(2)}, u32[]{:S(2)}) collective-permute-start(f32[684,128]{1,0:T(8,128)S(1)} %get-tuple-element.25), channel_id=1, source_target_pairs={{0,1},{1,0},{2,3},{3,2},{4,5},{5,4},{6,7},{7,6},{8,9},{9,8},{10,11... | collective-permute-start | bytes 1050632 | tf_op jit(solution)/shard_map/ppermute | solution.py:524
  2.7 6.0 %collective-permute-start.2 = (f32[342,128]{1,0:T(8,128)S(1)}, f32[342,128]{1,0:T(8,128)S(1)}, u32[]{:S(2)}, u32[]{:S(2)}) collective-permute-start(f32[342,128]{1,0:T(8,128)S(1)} %get-tuple-element.28), channel_id=1, source_target_pairs={{1,2},{2,1},{3,4},{4,3},{5,6},{6,5},{7,8},{8,7},{9,10},{10,9},{11,... | collective-permute-start | bytes 525320 | tf_op jit(solution)/shard_map/ppermute | solution.py:527
  5.3 5.5 %collective-permute-start.1 = (f32[342,128]{1,0:T(8,128)S(1)}, f32[342,128]{1,0:T(8,128)S(1)}, u32[]{:S(2)}, u32[]{:S(2)}) collective-permute-start(f32[342,128]{1,0:T(8,128)S(1)} %get-tuple-element.26), channel_id=1, source_target_pairs={{1,2},{2,1},{3,4},{4,3},{5,6},{6,5},{7,8},{8,7},{9,10},{10,9},{11,... | collective-permute-start | bytes 525320 | tf_op jit(solution)/shard_map/ppermute | solution.py:527
  12.4 7.8 %collective-permute-start.5 = (f32[8,128]{1,0:T(8,128)S(1)}, f32[8,128]{1,0:T(8,128)S(1)}, u32[]{:S(2)}, u32[]{:S(2)}) collective-permute-start(f32[8,128]{1,0:T(8,128)S(1)} %get-tuple-element.40.sums), channel_id=1, source_target_pairs={{0,1},{1,0},{2,3},{3,2},{4,5},{5,4},{6,7},{7,6},{8,9},{9,8},{10,11... | collective-permute-start | bytes 12296 | tf_op jit(solution)/shard_map/ppermute | solution.py:590
  15.2 5.0 %collective-permute-start.4 = (f32[8,128]{1,0:T(8,128)S(1)}, f32[8,128]{1,0:T(8,128)S(1)}, u32[]{:S(2)}, u32[]{:S(2)}) collective-permute-start(f32[8,128]{1,0:T(8,128)S(1)} %get-tuple-element.40.sums), channel_id=1, source_target_pairs={{0,2},{1,3},{2,0},{3,1},{4,6},{5,7},{6,4},{7,5},{8,10},{9,11},{10,... | collective-permute-start | bytes 12296 | tf_op jit(solution)/shard_map/ppermute | solution.py:590
  17.7 3.0 %collective-permute-start.3 = (f32[8,128]{1,0:T(8,128)S(1)}, f32[8,128]{1,0:T(8,128)S(1)}, u32[]{:S(2)}, u32[]{:S(2)}) collective-permute-start(f32[8,128]{1,0:T(8,128)S(1)} %get-tuple-element.40.sums), channel_id=1, source_target_pairs={{0,3},{1,2},{2,1},{3,0},{4,7},{5,6},{6,5},{7,4},{8,11},{9,10},{10,... | collective-permute-start | bytes 12296 | tf_op jit(solution)/shard_map/ppermute | solution.py:590
  20.7 9.5 %collective-permute-start.6 = (f32[4,1440]{1,0:T(4,128)S(1)}, f32[4,1440]{1,0:T(4,128)S(1)}, u32[]{:S(2)}, u32[]{:S(2)}) collective-permute-start(f32[4,1440]{1,0:T(4,128)S(1)} %get-tuple-element.38), channel_id=1, source_target_pairs={{0,1},{1,0},{2,3},{3,2},{4,5},{5,4},{6,7},{7,6},{8,9},{9,8},{10,11... | collective-permute-start | bytes 69128 | tf_op jit(solution)/shard_map/ppermute | solution.py:524
  20.9 9.4 %collective-permute-start.7 = (f32[4,1440]{1,0:T(4,128)S(1)}, f32[4,1440]{1,0:T(4,128)S(1)}, u32[]{:S(2)}, u32[]{:S(2)}) collective-permute-start(f32[4,1440]{1,0:T(4,128)S(1)} %get-tuple-element.39), channel_id=1, source_target_pairs={{1,2},{2,1},{3,4},{4,3},{5,6},{6,5},{7,8},{8,7},{9,10},{10,9},{11,... | collective-permute-start | bytes 69128 | tf_op jit(solution)/shard_map/ppermute | solution.py:527
  22.4 4.6 %collective-permute-start.10 = (f32[32,128]{1,0:T(8,128)S(1)}, f32[32,128]{1,0:T(8,128)S(1)}, u32[]{:S(2)}, u32[]{:S(2)}) collective-permute-start(f32[32,128]{1,0:T(8,128)S(1)} %constant_dynamic-update-slice_fusion.refs_0_), channel_id=1, source_target_pairs={{0,8},{1,9},{2,10},{3,11},{4,12},{5,13},{6,14},{7,15},{8,0},{9,1},... | collective-permute-start | bytes 49160 | tf_op jit(solution)/shard_map/ppermute | solution.py:590
  24.7 5.5 %collective-permute-start.9 = (f32[32,128]{1,0:T(8,128)S(1)}, f32[32,128]{1,0:T(8,128)S(1)}, u32[]{:S(2)}, u32[]{:S(2)}) collective-permute-start(f32[32,128]{1,0:T(8,128)S(1)} %constant_dynamic-update-slice_fusion.refs_0_), channel_id=1, source_target_pairs={{0,12},{1,13},{2,14},{3,15},{4,8},{5,9},{6,10},{7,11},{8,4},{9,5},... | collective-permute-start | bytes 49160 | tf_op jit(solution)/shard_map/ppermute | solution.py:590
  26.1 4.2 %collective-permute-start.8 = (f32[32,128]{1,0:T(8,128)S(1)}, f32[32,128]{1,0:T(8,128)S(1)}, u32[]{:S(2)}, u32[]{:S(2)}) collective-permute-start(f32[32,128]{1,0:T(8,128)S(1)} %constant_dynamic-update-slice_fusion.refs_0_), channel_id=1, source_target_pairs={{0,4},{1,5},{2,6},{3,7},{4,0},{5,1},{6,2},{7,3},{8,12},{9,13},{10,... | collective-permute-start | bytes 49160 | tf_op jit(solution)/shard_map/ppermute | solution.py:590

commit v6 on v5

--- a/solution.py
+++ b/solution.py
@@ -16,7 +16,8 @@
 HIGH_COUNT = 9
 LOW_COUNT = 8
 LOW_SHIFT = 3
-PIECES = (0, 6, 12)
+PIECES = (0, 7, 12)
+NEAR_PIECES = (0, 4, 8, 12)
 VMEM_LIMIT = 16 * 1024 * 1024
 
 
@@ -30,8 +31,15 @@
     return row[:, first:last]
 
 
-def piece_of(j):
-    return max(p for p in range(len(PIECES) - 1) if PIECES[p] <= j)
+def piece_of(j, bounds=None):
+    bounds = PIECES if bounds is None else bounds
+    return max(p for p in range(len(bounds) - 1) if bounds[p] <= j)
+
+
+def near_place(nears, j):
+    piece = piece_of(j, NEAR_PIECES)
+    first, last = NEAR_PIECES[piece : piece + 2]
+    return nears[piece], j - first, last - first
 
 
 def is_odd():
@@ -54,46 +62,63 @@
         copy.wait()
 
 
+def flipped_map(ref, odd):
+    field = ref[...].astype(jnp.float32)
+    flipped = jnp.concatenate([field[r : r + 1] for r in reversed(range(field.shape[0]))], axis=0)
+    return jnp.where(odd, field, flipped), jnp.where(odd, flipped, field)
+
+
+def fill_far(piece, far, held):
+    tracer, maps = held[0], held[1:]
+    levels, _, lon_count = tracer.shape
+    odd = is_odd()
+    group = range(PIECES[piece], PIECES[piece + 1])
+    for t in range(STEPS):
+        field = oriented(tracer, t, odd)
+        for u, j in enumerate(group):
+            at = (u * STEPS + STEPS - 1 - t) * levels
+            far[at : at + levels, :] = strip_of(field, j, lon_count)
+    for a, ref in enumerate(maps):
+        down, _ = flipped_map(ref, odd)
+        for u, j in enumerate(group):
+            at = len(group) * STEPS * levels + (3 * u + a) * STEPS
+            far[at : at + STEPS, :] = strip_of(down, j, lon_count)[1:]
+
+
+def pack_first(*refs):
+    sources, far, held, arrived = refs[:4], refs[4], refs[5:9], refs[9]
+    bring(sources, held, arrived)
+    fill_far(0, far, held)
+
+
 def pack_fields(*refs):
-    parts = len(PIECES) - 1
-    sources, (own, own_maps, near), fars, held, arrived = (
-        refs[:4], refs[4:7], refs[7 : 7 + parts], refs[7 + parts : 11 + parts], refs[11 + parts],
-    )
+    parts, near_parts = len(PIECES) - 2, len(NEAR_PIECES) - 1
+    sources, (own, own_maps) = refs[:4], refs[4:6]
+    nears, refs = refs[6 : 6 + near_parts], refs[6 + near_parts :]
+    fars, held, arrived = refs[:parts], refs[parts : 4 + parts], refs[4 + parts]
     bring(sources, held, arrived)
-    tracer, mix, heading, depth = held
+    tracer = held[0]
     levels, rows, lon_count = tracer.shape
     strips = lon_count // OWN
     odd = is_odd()
-
-    def far_place(j):
-        piece = piece_of(j)
-        return fars[piece], j - PIECES[piece], PIECES[piece + 1] - PIECES[piece]
-
+    for i, far in enumerate(fars):
+        fill_far(i + 1, far, held)
     for t in range(rows):
         field = oriented(tracer, t, odd)
         for j in range(strips):
             strip = strip_of(field, j, lon_count)
             own[j, t * levels : (t + 1) * levels, :] = strip
-            if t < STEPS:
-                far, local, _ = far_place(j)
-                at = (local * STEPS + STEPS - 1 - t) * levels
-                far[at : at + levels, :] = strip
             if t > 0:
-                at = (j * STEPS + rows - 1 - t) * levels
+                near, local, _ = near_place(nears, j)
+                at = (local * STEPS + rows - 1 - t) * levels
                 near[at : at + levels, :] = strip
-    for a, ref in enumerate((mix, heading, depth)):
-        field = ref[...].astype(jnp.float32)
-        flipped = jnp.concatenate([field[r : r + 1] for r in reversed(range(rows))], axis=0)
-        up = jnp.where(odd, flipped, field)
-        down = jnp.where(odd, field, flipped)
+    for a, ref in enumerate(held[1:]):
+        down, up = flipped_map(ref, odd)
         for j in range(strips):
             own_maps[j, a * 4 : a * 4 + 4, :] = strip_of(up, j, lon_count)
-            strip = strip_of(down, j, lon_count)
-            at = strips * STEPS * levels + (3 * j + a) * STEPS
-            near[at : at + STEPS, :] = strip[:STEPS]
-            far, local, count = far_place(j)
+            near, local, count = near_place(nears, j)
             at = count * STEPS * levels + (3 * local + a) * STEPS
-            far[at : at + STEPS, :] = strip[1:]
+            near[at : at + STEPS, :] = strip_of(down, j, lon_count)[:STEPS]
     own_maps[:, 12:, :] = jnp.zeros_like(own_maps[:, 12:, :])
 
 
@@ -110,12 +135,13 @@
             strip = strip_of(field, j, lon_count)
             own[j, t * levels : (t + 1) * levels, :] = strip
     class_count = weights.shape[1]
+    label = lax.broadcasted_iota(jnp.int32, (1, LANES), 1)
     scale_rows, band_rows = [], []
     for pair in range(2):
         band = band_of_row[jnp.where(odd, 3 - 2 * pair, 2 * pair)]
         scale = weights[pl.ds(band, 1), :]
         scale_rows.append(jnp.concatenate([scale, jnp.zeros((1, LANES - class_count), jnp.float32)], axis=1))
-        band_rows.append(jnp.full((1, LANES), band.astype(jnp.float32)))
+        band_rows.append(jnp.where(label == LANES - 1, band.astype(jnp.float32), 0.0))
     blank = jnp.zeros((2, LANES), jnp.float32)
     scales[...] = jnp.concatenate(scale_rows + [blank] + band_rows + [blank], axis=0)
 
@@ -214,7 +240,7 @@
     ]
 
 
-def face_maps(own_maps, near, fars, maps, strips, levels):
+def face_maps(own_maps, nears, fars, maps, strips, levels):
     count, edge = lax.axis_size("lat"), lax.axis_index("lat")
     keep = jnp.where(jnp.logical_and(edge != 0, edge != count - 1), 1.0, 0.0)
 
@@ -229,7 +255,8 @@
             low = fars[piece][at : at + STEPS, :]
             if a == 2:
                 low = low * keep
-            at = PIECES[-1] * STEPS * levels + (3 * j + a) * STEPS
+            near, local, size = near_place(nears, j)
+            at = size * STEPS * levels + (3 * local + a) * STEPS
             high = near[at : at + STEPS, :]
             whole.append(jnp.concatenate([low, own_maps[j, 4 * a : 4 * a + 4, :], high, high, high], axis=0))
         mix, heading, depth = whole
@@ -259,15 +286,17 @@
 def forward(piece, *refs):
     last = piece + 2 == len(PIECES)
     refs = list(refs)
-    own, own_maps, near, far, classes = refs[:5]
-    del refs[:5]
+    near_parts = len(NEAR_PIECES) - 1
+    own, own_maps, far, classes = refs[:4]
+    nears = refs[4 : 4 + near_parts]
+    del refs[: 4 + near_parts]
     before = refs.pop(0) if piece > 0 else None
     scales = refs.pop(0) if last else None
-    out, later, maps = refs[:3]
-    grams = refs[3] if last else out
+    out, later = refs[:2]
+    weighted, maps, grams = refs[2:] if last else (None, refs[2], out)
     levels = own.shape[1] // 4
     group = list(range(PIECES[piece], PIECES[piece + 1]))
-    face_maps(own_maps, near, {piece: far}, maps, group, levels)
+    face_maps(own_maps, nears, {piece: far}, maps, group, levels)
     lane = lax.broadcasted_iota(jnp.int32, (levels, LANES), 1)
     inner = jnp.logical_and(lane >= GHOST, lane < LANES - GHOST)
     coefs = [Coefficients(maps, u, levels) for u in range(len(group))]
@@ -277,7 +306,8 @@
         for s in range(STEPS):
             at = (u * STEPS + s) * levels
             field[s - STEPS] = far[at : at + levels, :]
-            at = (j * STEPS + s) * levels
+            near, local, _ = near_place(nears, j)
+            at = (local * STEPS + s) * levels
             field[4 + s] = near[at : at + levels, :]
         fields.append(field)
     for n in range(STEPS):
@@ -313,10 +343,10 @@
         )
         grams[pair] = gram if before is None else before[pair] + gram
     if last:
-        class_sums(grams, scales, out, levels)
-
-
-def class_sums(grams, scales, sums, levels):
+        class_sums(grams, scales, out, weighted, levels)
+
+
+def class_sums(grams, scales, sums, weighted, levels):
     width = 2 * LOW_COUNT * levels
     own_level = lax.broadcasted_iota(jnp.int32, (levels, width), 0)
     other_level = lax.broadcasted_iota(jnp.int32, (levels, width), 1) & (levels - 1)
@@ -346,12 +376,12 @@
         )
         for p in range(2)
     ]
-    finish_sums(scales, totals, sums)
-
-
-def finish_sums(scales, totals, sums):
-    weighted = [scales[p : p + 1, :] * totals[p] for p in range(2)]
-    sums[...] = jnp.concatenate(totals + weighted + [scales[4:8, :]], axis=0)
+    finish_sums(scales, totals, sums, weighted)
+
+
+def finish_sums(scales, totals, sums, weighted):
+    sums[...] = jnp.concatenate([totals[p] + scales[4 + p : 5 + p, :] for p in range(2)], axis=0)
+    weighted[0:2, :] = jnp.concatenate([scales[p : p + 1, :] * totals[p] for p in range(2)], axis=0)
 
 
 def finish(own_share, near_share, far_share, *refs):
@@ -361,33 +391,35 @@
     gradient[...] = jnp.where(is_odd(), down, up)
     band_own, class_count = binned.shape
     first = lax.axis_index("lat") * band_own
-    found = [jnp.zeros((2, LANES), jnp.float32) for _ in range(band_own)]
+    found = [jnp.zeros((1, LANES), jnp.float32) for _ in range(band_own)]
     for piece in pieces:
-        for at in range(0, piece.shape[0], 8):
-            totals, bands = piece[at : at + 2, :], piece[at + 4 : at + 6, :]
-            for m in range(band_own):
-                hit = bands == (first + m).astype(jnp.float32)
-                found[m] = found[m] + jnp.where(hit, totals, 0.0)
-    whole = jnp.concatenate([jnp.sum(x, axis=0, keepdims=True) for x in found], axis=0)
+        totals = piece[...]
+        bands = jnp.broadcast_to(totals[:, LANES - 1 :], totals.shape)
+        for m in range(band_own):
+            hit = jnp.where(bands == (first + m).astype(jnp.float32), totals, 0.0)
+            found[m] = found[m] + jnp.sum(hit, axis=0, keepdims=True)
+    whole = jnp.concatenate(found, axis=0)
     binned[...] = whole[:, :class_count]
 
 
-def adjoint_part(own, own_maps, near, classes, sums, *refs):
+def adjoint_part(own, own_maps, classes, weighted, *refs):
     parts = len(PIECES) - 1
+    near_parts = len(NEAR_PIECES) - 1
+    nears, refs = refs[:near_parts], refs[near_parts:]
     fars, laters = refs[:parts], refs[parts : 2 * parts]
     own_share, near_share, far_share, maps = refs[2 * parts :]
     strips = own.shape[0]
     levels = own.shape[1] // 4
     group = list(range(strips))
-    face_maps(own_maps, near, fars, maps, group, levels)
+    face_maps(own_maps, nears, fars, maps, group, levels)
     coefs = [Coefficients(maps, j, levels) for j in group]
     adjoints = []
     for j in group:
         adjoint = {}
         for t in range(4):
             label = classes[j, t * levels : (t + 1) * levels, :]
-            row = 2 + t // 2
-            table = jnp.broadcast_to(sums[row : row + 1, :], (8, LANES))
+            row = t // 2
+            table = jnp.broadcast_to(weighted[row : row + 1, :], (8, LANES))
             value = jnp.concatenate(
                 [jnp.take_along_axis(table, label[k : k + 8, :], axis=1) for k in range(0, levels, 8)], axis=0
             )
@@ -408,7 +440,8 @@
             elif t < 4:
                 field[t] = own[j, t * levels : (t + 1) * levels, :]
             else:
-                at = (j * STEPS + t - 4) * levels
+                near, place, _ = near_place(nears, j)
+                at = (place * STEPS + t - 4) * levels
                 field[t] = near[at : at + levels, :]
         return field
 
@@ -527,23 +560,39 @@
         return lax.ppermute(x, ("members", "lat"), far_pairs(members, count))
 
     sizes = [b - a for a, b in zip(PIECES, PIECES[1:])]
+    near_sizes = [b - a for a, b in zip(NEAR_PIECES, NEAR_PIECES[1:])]
     fields = (tracer, diffusivity, direction, column_depth)
-    own, own_maps, near_out, *fars_out = pl.pallas_call(
+    in_place = [pltpu.with_memory_space_constraint(x, pltpu.HBM) for x in fields]
+    taken = dict(
+        in_specs=[pl.BlockSpec(memory_space=pltpu.HBM)] * 4,
+        scratch_shapes=[pltpu.VMEM(x.shape, x.dtype) for x in fields] + [pltpu.SemaphoreType.DMA((4,))],
+        compiler_params=params,
+    )
+    far_shapes = [jax.ShapeDtypeStruct((payload // strips * size, LANES), f32) for size in sizes]
+    first_out = pl.pallas_call(
+        pack_first,
+        name="pack_first",
+        out_shape=far_shapes[0],
+        out_specs=pl.BlockSpec(memory_space=pltpu.VMEM),
+        **taken,
+    )(*in_place)
+    fars = [to_far(first_out)]
+    late_fields = lax.optimization_barrier((*fields, first_out))[: len(fields)]
+    in_place = [pltpu.with_memory_space_constraint(x, pltpu.HBM) for x in late_fields]
+    own, own_maps, *outs = pl.pallas_call(
         pack_fields,
         name="pack_fields",
         out_shape=(
             jax.ShapeDtypeStruct((strips, rows * levels, LANES), f32),
             jax.ShapeDtypeStruct((strips, 16, LANES), f32),
-            jax.ShapeDtypeStruct((payload, LANES), f32),
-        )
-        + tuple(jax.ShapeDtypeStruct((payload // strips * size, LANES), f32) for size in sizes),
-        in_specs=[pl.BlockSpec(memory_space=pltpu.HBM)] * 4,
-        out_specs=tuple(vmem(3 + len(sizes))),
-        scratch_shapes=[pltpu.VMEM(x.shape, x.dtype) for x in fields] + [pltpu.SemaphoreType.DMA((4,))],
-        compiler_params=params,
-    )(*[pltpu.with_memory_space_constraint(x, pltpu.HBM) for x in fields])
-    fars = [to_far(x) for x in fars_out]
-    near = to_near(near_out)
+            *[jax.ShapeDtypeStruct((payload // strips * size, LANES), f32) for size in near_sizes],
+            *far_shapes[1:],
+        ),
+        out_specs=tuple(vmem(1 + len(near_sizes) + len(sizes))),
+        **taken,
+    )(*in_place)
+    nears = [to_near(x) for x in outs[: len(near_sizes)]]
+    fars += [to_far(x) for x in outs[len(near_sizes) :]]
 
     own_classes, scales = pl.pallas_call(
         pack_classes,
@@ -566,17 +615,18 @@
     gram_shape = (2, HIGH_COUNT * levels, 2 * LOW_COUNT * levels)
     for piece, size in enumerate(sizes):
         last = piece + 1 == len(sizes)
-        given = [own, own_maps, near, fars[piece], own_classes]
+        given = [own, own_maps, fars[piece], own_classes, *nears]
         given += ([sums] if piece > 0 else []) + ([scales] if last else [])
-        sums, later = pl.pallas_call(
+        sums, later, *weighted = pl.pallas_call(
             functools.partial(forward, piece),
             name="forward",
             out_shape=(
-                jax.ShapeDtypeStruct((8, LANES) if last else gram_shape, f32),
+                jax.ShapeDtypeStruct((2, LANES) if last else gram_shape, f32),
                 jax.ShapeDtypeStruct((size, 14 * levels, LANES), f32),
-            ),
+            )
+            + ((jax.ShapeDtypeStruct((8, LANES), f32),) if last else ()),
             in_specs=vmem(len(given)),
-            out_specs=tuple(vmem(2)),
+            out_specs=tuple(vmem(3 if last else 2)),
             cost_estimate=cost(2000),
             scratch_shapes=[pltpu.VMEM((size, 16 * MAP_FIELDS, LANES), f32)]
             + ([pltpu.VMEM(gram_shape, f32)] if last else []),
@@ -593,11 +643,11 @@
                 adjoint_part,
                 name="adjoint_part",
                 out_shape=(jax.ShapeDtypeStruct((rows, lon_count), f32),) * 3,
-                in_specs=vmem(5 + 2 * len(sizes)),
+                in_specs=vmem(4 + len(nears) + 2 * len(sizes)),
                 out_specs=tuple(vmem(3)),
                 scratch_shapes=[pltpu.VMEM((strips, 16 * MAP_FIELDS, LANES), f32)],
                 compiler_params=params,
-            )(own, own_maps, near, own_classes, sums, *fars, *laters)
+            )(own, own_maps, own_classes, weighted[0], *nears, *fars, *laters)
         pieces = [gathered] + others
         if i == 0:
             *pieces, own_share, near_share, far_share = lax.optimization_barrier((*pieces, *shares))

time: 31 us -> 30.4 us (0.981)
  waiting for transfers between devices: 6.79 us -> 4.73 us
  Pallas kernels: 9.36 us -> 10.8 us
    ppermute x6, starting transfers between devices: 9.22 us -> 7.08 us  [body(): lax.ppermute(gathered, 'lat', [(d, d ^ k) for d in range(count)])]
    ppermute x3, waiting for transfers between devices: 2.39 us -> 0.42 us  [to_far(): return lax.ppermute(x, ('members', 'lat'), far_pairs(members, count))]
    ppermute x3, starting transfers between devices: 4.13 us -> 5.99 us  [to_far(): return lax.ppermute(x, ('members', 'lat'), far_pairs(members, count))]
    pallas_call x0 -> x1, Pallas kernels: none -> 1.3 us  [body(): pl.pallas_call(pack_first, name='pack_first', out_shape=far_shapes[0], ou...]
    ppermute x2 -> x4, starting transfers between devices: 0.68 us -> 0.88 us  [to_near(): return lax.ppermute(x, 'lat', near_pairs(count))]
  transfers between devices with their start and end apart: 11 -> 13, of which waited for: 5 -> 4; matrix products, arithmetic and copies ran while one was open for 0% -> 0% of each run, Pallas kernels for 18% -> 24%
where the time goes in v6:
time: 30.4 us; the launch traced here: 30.2 us
  starting transfers between devices  14 us (46%)
  Pallas kernels  10.8 us (36%)
  waiting for transfers between devices  4.73 us (16%)
  between operations  0.73 us (2%)
    ppermute x6, starting transfers between devices, body(): lax.ppermute(gathered, 'lat', [(d, d ^ k) for d in range(count)])  7.08 us
    ppermute x3, starting transfers between devices, to_far(): return lax.ppermute(x, ('members', 'lat'), far_pairs(members, count))  5.99 us
    ppermute x6, waiting for transfers between devices, body(): lax.ppermute(gathered, 'lat', [(d, d ^ k) for d in range(count)])  4.31 us
    pallas_call x2, Pallas kernels, body(): pl.pallas_call(functools.partial(forward, piece), name='forward', out_sha...  3.24 us
    pallas_call x1, Pallas kernels, body(): pl.pallas_call(adjoint_part, name='adjoint_part', out_shape=(jax.ShapeDty...  2.42 us
    pallas_call x1, Pallas kernels, body(): pl.pallas_call(pack_fields, name='pack_fields', out_shape=(jax.ShapeDtype...  1.73 us
    pallas_call x1, Pallas kernels, body(): pl.pallas_call(pack_classes, name='pack_classes', out_shape=(jax.ShapeDty...  1.42 us
    pallas_call x1, Pallas kernels, body(): pl.pallas_call(pack_first, name='pack_first', out_shape=far_shapes[0], ou...  1.3 us
  transfers between devices with their start and end apart: 13, of which 4 were waited for; matrix products, arithmetic and copies ran while one was open for 0% of the time, Pallas kernels for 24%

profile of v6, /device:TPU:0, one launch (start us, length us, event | category | flops | bytes accessed | tf_op | source)
XLA Modules:
  0.0 30.2 jit_solution(9603661087702665416)
XLA Ops:
  0.6 1.3 %pack_first.1 = f32[399,128]{1,0:T(8,128)S(1)} custom-call(f32[16,4,1440]{2,1,0:T(4,128)} %refs_0_.3, f32[4,1440]{1,0:T(4,128)} %refs_1_.3, f32[4,1440]{1,0:T(4,128)} %refs_2_.3, s32[4,1440]{1,0:T(4,128)} %refs_3_.2), custom_call_target="tpu_custom_call" | custom-call | tf_op jit(solution)/shard_map/pack_first/pallas_call | solution.py:572
  1.9 3.0 %collective-permute-start.4 = (f32[399,128]{1,0:T(8,128)S(1)}, f32[399,128]{1,0:T(8,128)S(1)}, u32[]{:S(2)}, u32[]{:S(2)}) collective-permute-start(f32[399,128]{1,0:T(8,128)S(1)} %pack_first.1), channel_id=1, source_target_pairs={{1,2},{2,1},{3,4},{4,3},{5,6},{6,5},{7,8},{8,7},{9,10},{10,9},{11,... | collective-permute-start | bytes 612872 | tf_op jit(solution)/shard_map/ppermute | solution.py:560
  4.9 1.7 %pack_fields.1 = (f32[12,64,128]{2,1,0:T(8,128)S(1)}, f32[12,16,128]{2,1,0:T(8,128)S(1)}, f32[228,128]{1,0:T(8,128)S(1)}, f32[228,128]{1,0:T(8,128)S(1)}, f32[22...) custom-call(f32[16,4,1440]{2,1,0:T(4,128)} %refs_0_.3, f32[4,1440]{1,0:T(4,128)} %refs_1_.3, f32[4,1440]{1,0:T(4,128)} %refs_2_.3, ...), custom_call_target="tpu_custom_call" | custom-call | tf_op jit(solution)/shard_map/pack_fields/pallas_call | solution.py:582
  6.7 0.2 collective-permute-start.1
  6.9 0.4 %collective-permute-start.2 = (f32[228,128]{1,0:T(8,128)S(1)}, f32[228,128]{1,0:T(8,128)S(1)}, u32[]{:S(2)}, u32[]{:S(2)}) collective-permute-start(f32[228,128]{1,0:T(8,128)S(1)} %get-tuple-element.38), channel_id=1, source_target_pairs={{0,1},{1,0},{2,3},{3,2},{4,5},{5,4},{6,7},{7,6},{8,9},{9,8},{10,11... | collective-permute-start | bytes 350216 | tf_op jit(solution)/shard_map/ppermute | solution.py:557
  7.3 0.1 collective-permute-start.3
  7.4 1.5 %collective-permute-start = (f32[285,128]{1,0:T(8,128)S(1)}, f32[285,128]{1,0:T(8,128)S(1)}, u32[]{:S(2)}, u32[]{:S(2)}) collective-permute-start(f32[285,128]{1,0:T(8,128)S(1)} %get-tuple-element.35), channel_id=1, source_target_pairs={{1,2},{2,1},{3,4},{4,3},{5,6},{6,5},{7,8},{8,7},{9,10},{10,9},{11,... | collective-permute-start | bytes 437768 | tf_op jit(solution)/shard_map/ppermute | solution.py:560
  8.9 1.4 %pack_classes.1 = (s32[12,64,128]{2,1,0:T(8,128)S(1)}, f32[8,128]{1,0:T(8,128)S(1)}) custom-call(s32[16,4,1440]{2,1,0:T(4,128)} %refs_0_.4, f32[32,72]{1,0:T(8,128)} %refs_1_.4, s32[4]{0:T(128)} %refs_2_.4), custom_call_target="tpu_custom_call" | custom-call | tf_op jit(solution)/shard_map/pack_classes/pallas_call | solution.py:597
  10.3 0.0 collective-permute-done.1.refs_4_.refs_0_
  10.3 0.0 collective-permute-done.2.refs_5_.refs_1_
  10.3 0.0 collective-permute-done.3.refs_6_.refs_2_
  10.4 0.0 collective-permute-done.4.refs_2_.refs_3_
  10.4 1.8 %forward.2 = (f32[2,144,256]{2,1,0:T(8,128)S(1)}, f32[7,224,128]{2,1,0:T(8,128)S(1)}) custom-call(f32[12,64,128]{2,1,0:T(8,128)S(1)} %get-tuple-element.33.refs_0_.own, f32[12,16,128]{2,1,0:T(8,128)S(1)} %get-tuple-element.34.refs_1_.own_maps, f32[399,128]{1,0:T(8,128)S(1)} %collective-permute-done.4.refs_2_.refs_3_, ...), custom_call_target="tpu_custom_call" | custom-call | flops 2307000064 | bytes 7380000 | tf_op jit(solution)/shard_map/forward/pallas_call | solution.py:620
  12.1 0.4 %collective-permute-done.refs_2_.refs_4_ = f32[285,128]{1,0:T(8,128)S(1)} collective-permute-done((f32[285,128]{1,0:T(8,128)S(1)}, f32[285,128]{1,0:T(8,128)S(1)}, u32[]{:S(2)}, u32[]{:S(2)}) %collective-permute-start) | collective-permute-done | bytes 145952 | tf_op jit(solution)/shard_map/ppermute | solution.py:560
  12.5 1.5 %forward.3 = (f32[2,128]{1,0:T(2,128)S(1)}, f32[5,224,128]{2,1,0:T(8,128)S(1)}, f32[8,128]{1,0:T(8,128)S(1)}) custom-call(f32[12,64,128]{2,1,0:T(8,128)S(1)} %get-tuple-element.33.refs_0_.own, f32[12,16,128]{2,1,0:T(8,128)S(1)} %get-tuple-element.34.refs_1_.own_maps, f32[285,128]{1,0:T(8,128)S(1)} %collective-permute-done.refs_2_.refs_4_, ...), custom_call_target="tpu_custom_call" | custom-call | flops 2307000064 | bytes 7380000 | tf_op jit(solution)/shard_map/forward/pallas_call | solution.py:620
  14.0 0.7 %collective-permute-start.7 = (f32[2,128]{1,0:T(2,128)S(1)}, f32[2,128]{1,0:T(2,128)S(1)}, u32[]{:S(2)}, u32[]{:S(2)}) collective-permute-start(f32[2,128]{1,0:T(2,128)S(1)} %get-tuple-element.52), channel_id=1, source_target_pairs={{0,1},{1,0},{2,3},{3,2},{4,5},{5,4},{6,7},{7,6},{8,9},{9,8},{10,11... | collective-permute-start | bytes 3080 | tf_op jit(solution)/shard_map/ppermute | solution.py:640
  14.7 2.4 %collective-permute-start.6 = (f32[2,128]{1,0:T(2,128)S(1)}, f32[2,128]{1,0:T(2,128)S(1)}, u32[]{:S(2)}, u32[]{:S(2)}) collective-permute-start(f32[2,128]{1,0:T(2,128)S(1)} %get-tuple-element.52), channel_id=1, source_target_pairs={{0,2},{1,3},{2,0},{3,1},{4,6},{5,7},{6,4},{7,5},{8,10},{9,11},{10,... | collective-permute-start | bytes 3080 | tf_op jit(solution)/shard_map/ppermute | solution.py:640
  17.1 0.1 collective-permute-start.5
  17.2 2.4 %adjoint_part.1 = (f32[4,1440]{1,0:T(4,128)S(1)}, f32[4,1440]{1,0:T(4,128)S(1)}, f32[4,1440]{1,0:T(4,128)S(1)}) custom-call(f32[12,64,128]{2,1,0:T(8,128)S(1)} %get-tuple-element.33.refs_0_.own, f32[12,16,128]{2,1,0:T(8,128)S(1)} %get-tuple-element.34.refs_1_.own_maps, s32[12,64,128]{2,1,0:T(8,128)S(1)} %get-tuple-element.36.refs_3_.classes, ...), custom_call_target="tpu_custom_call" | custom-call | tf_op jit(solution)/shard_map/adjoint_part/pallas_call | solution.py:642
  19.6 0.0 collective-permute-done.7
  19.6 0.0 collective-permute-done.6
  19.6 0.5 %collective-permute-done.5 = f32[2,128]{1,0:T(2,128)S(1)} collective-permute-done((f32[2,128]{1,0:T(2,128)S(1)}, f32[2,128]{1,0:T(2,128)S(1)}, u32[]{:S(2)}, u32[]{:S(2)}) %collective-permute-start.5) | collective-permute-done | bytes 1056 | tf_op jit(solution)/shard_map/ppermute | solution.py:640
  20.1 0.2 collective-permute-start.8
  20.3 1.5 %collective-permute-start.9 = (f32[4,1440]{1,0:T(4,128)S(1)}, f32[4,1440]{1,0:T(4,128)S(1)}, u32[]{:S(2)}, u32[]{:S(2)}) collective-permute-start(f32[4,1440]{1,0:T(4,128)S(1)} %get-tuple-element.51), channel_id=1, source_target_pairs={{1,2},{2,1},{3,4},{4,3},{5,6},{6,5},{7,8},{8,7},{9,10},{10,9},{11,... | collective-permute-start | bytes 69128 | tf_op jit(solution)/shard_map/ppermute | solution.py:560
  21.8 2.3 %collective-permute-start.12 = (f32[8,128]{1,0:T(8,128)S(1)}, f32[8,128]{1,0:T(8,128)S(1)}, u32[]{:S(2)}, u32[]{:S(2)}) collective-permute-start(f32[8,128]{1,0:T(8,128)S(1)} %pad_maximum_fusion.refs_0_), channel_id=1, source_target_pairs={{0,8},{1,9},{2,10},{3,11},{4,12},{5,13},{6,14},{7,15},{8,0},{9,1},... | collective-permute-start | bytes 12296 | tf_op jit(solution)/shard_map/ppermute | solution.py:640
  24.1 1.3 %collective-permute-start.11 = (f32[8,128]{1,0:T(8,128)S(1)}, f32[8,128]{1,0:T(8,128)S(1)}, u32[]{:S(2)}, u32[]{:S(2)}) collective-permute-start(f32[8,128]{1,0:T(8,128)S(1)} %pad_maximum_fusion.refs_0_), channel_id=1, source_target_pairs={{0,12},{1,13},{2,14},{3,15},{4,8},{5,9},{6,10},{7,11},{8,4},{9,5},... | collective-permute-start | bytes 12296 | tf_op jit(solution)/shard_map/ppermute | solution.py:640
  25.5 0.2 collective-permute-start.10
  25.7 0.7 %collective-permute-done.12.refs_3_ = f32[8,128]{1,0:T(8,128)S(1)} collective-permute-done((f32[8,128]{1,0:T(8,128)S(1)}, f32[8,128]{1,0:T(8,128)S(1)}, u32[]{:S(2)}, u32[]{:S(2)}) %collective-permute-start.12) | collective-permute-done | bytes 4128 | tf_op jit(solution)/shard_map/ppermute | solution.py:640
  26.4 3.2 %collective-permute-done.11.refs_2_ = f32[8,128]{1,0:T(8,128)S(1)} collective-permute-done((f32[8,128]{1,0:T(8,128)S(1)}, f32[8,128]{1,0:T(8,128)S(1)}, u32[]{:S(2)}, u32[]{:S(2)}) %collective-permute-start.11) | collective-permute-done | bytes 4128 | tf_op jit(solution)/shard_map/ppermute | solution.py:640
  29.5 0.0 collective-permute-done.10.refs_1_
  29.5 0.0 collective-permute-done.9.far_share
  29.5 0.7 %finish.1 = (f32[2,72]{1,0:T(2,128)}, f32[4,1440]{1,0:T(4,128)}) custom-call(f32[4,1440]{1,0:T(4,128)S(1)} %get-tuple-element.49.own_share, f32[4,1440]{1,0:T(4,128)S(1)} %collective-permute-done.8.near_share, f32[4,1440]{1,0:T(4,128)S(1)} %collective-permute-done.9.far_share, f32[8,128]{1,0:T(8,128)S(1)} %pad_maximum_fusion.refs_0_, ...), custom_call_target="tpu_custom_call" | custom-call | tf_op jit(solution)/shard_map/finish/pallas_call | solution.py:657
  (2 shorter events, 0.0 us)
Async XLA Ops:
  1.9 8.4 %collective-permute-start.4 = (f32[399,128]{1,0:T(8,128)S(1)}, f32[399,128]{1,0:T(8,128)S(1)}, u32[]{:S(2)}, u32[]{:S(2)}) collective-permute-start(f32[399,128]{1,0:T(8,128)S(1)} %pack_first.1), channel_id=1, source_target_pairs={{1,2},{2,1},{3,4},{4,3},{5,6},{6,5},{7,8},{8,7},{9,10},{10,9},{11,... | collective-permute-start | bytes 612872 | tf_op jit(solution)/shard_map/ppermute | solution.py:560
  6.7 3.6 %collective-permute-start.1 = (f32[228,128]{1,0:T(8,128)S(1)}, f32[228,128]{1,0:T(8,128)S(1)}, u32[]{:S(2)}, u32[]{:S(2)}) collective-permute-start(f32[228,128]{1,0:T(8,128)S(1)} %get-tuple-element.37), channel_id=1, source_target_pairs={{0,1},{1,0},{2,3},{3,2},{4,5},{5,4},{6,7},{7,6},{8,9},{9,8},{10,11... | collective-permute-start | bytes 350216 | tf_op jit(solution)/shard_map/ppermute | solution.py:557
  6.9 3.4 %collective-permute-start.2 = (f32[228,128]{1,0:T(8,128)S(1)}, f32[228,128]{1,0:T(8,128)S(1)}, u32[]{:S(2)}, u32[]{:S(2)}) collective-permute-start(f32[228,128]{1,0:T(8,128)S(1)} %get-tuple-element.38), channel_id=1, source_target_pairs={{0,1},{1,0},{2,3},{3,2},{4,5},{5,4},{6,7},{7,6},{8,9},{9,8},{10,11... | collective-permute-start | bytes 350216 | tf_op jit(solution)/shard_map/ppermute | solution.py:557
  7.3 3.1 %collective-permute-start.3 = (f32[228,128]{1,0:T(8,128)S(1)}, f32[228,128]{1,0:T(8,128)S(1)}, u32[]{:S(2)}, u32[]{:S(2)}) collective-permute-start(f32[228,128]{1,0:T(8,128)S(1)} %get-tuple-element.39), channel_id=1, source_target_pairs={{0,1},{1,0},{2,3},{3,2},{4,5},{5,4},{6,7},{7,6},{8,9},{9,8},{10,11... | collective-permute-start | bytes 350216 | tf_op jit(solution)/shard_map/ppermute | solution.py:557
  7.4 5.1 %collective-permute-start = (f32[285,128]{1,0:T(8,128)S(1)}, f32[285,128]{1,0:T(8,128)S(1)}, u32[]{:S(2)}, u32[]{:S(2)}) collective-permute-start(f32[285,128]{1,0:T(8,128)S(1)} %get-tuple-element.35), channel_id=1, source_target_pairs={{1,2},{2,1},{3,4},{4,3},{5,6},{6,5},{7,8},{8,7},{9,10},{10,9},{11,... | collective-permute-start | bytes 437768 | tf_op jit(solution)/shard_map/ppermute | solution.py:560
  14.0 5.6 %collective-permute-start.7 = (f32[2,128]{1,0:T(2,128)S(1)}, f32[2,128]{1,0:T(2,128)S(1)}, u32[]{:S(2)}, u32[]{:S(2)}) collective-permute-start(f32[2,128]{1,0:T(2,128)S(1)} %get-tuple-element.52), channel_id=1, source_target_pairs={{0,1},{1,0},{2,3},{3,2},{4,5},{5,4},{6,7},{7,6},{8,9},{9,8},{10,11... | collective-permute-start | bytes 3080 | tf_op jit(solution)/shard_map/ppermute | solution.py:640
  14.7 5.0 %collective-permute-start.6 = (f32[2,128]{1,0:T(2,128)S(1)}, f32[2,128]{1,0:T(2,128)S(1)}, u32[]{:S(2)}, u32[]{:S(2)}) collective-permute-start(f32[2,128]{1,0:T(2,128)S(1)} %get-tuple-element.52), channel_id=1, source_target_pairs={{0,2},{1,3},{2,0},{3,1},{4,6},{5,7},{6,4},{7,5},{8,10},{9,11},{10,... | collective-permute-start | bytes 3080 | tf_op jit(solution)/shard_map/ppermute | solution.py:640
  17.1 3.0 %collective-permute-start.5 = (f32[2,128]{1,0:T(2,128)S(1)}, f32[2,128]{1,0:T(2,128)S(1)}, u32[]{:S(2)}, u32[]{:S(2)}) collective-permute-start(f32[2,128]{1,0:T(2,128)S(1)} %get-tuple-element.52), channel_id=1, source_target_pairs={{0,3},{1,2},{2,1},{3,0},{4,7},{5,6},{6,5},{7,4},{8,11},{9,10},{10,... | collective-permute-start | bytes 3080 | tf_op jit(solution)/shard_map/ppermute | solution.py:640
  20.1 9.4 %collective-permute-start.8 = (f32[4,1440]{1,0:T(4,128)S(1)}, f32[4,1440]{1,0:T(4,128)S(1)}, u32[]{:S(2)}, u32[]{:S(2)}) collective-permute-start(f32[4,1440]{1,0:T(4,128)S(1)} %get-tuple-element.50), channel_id=1, source_target_pairs={{0,1},{1,0},{2,3},{3,2},{4,5},{5,4},{6,7},{7,6},{8,9},{9,8},{10,11... | collective-permute-start | bytes 69128 | tf_op jit(solution)/shard_map/ppermute | solution.py:557
  20.3 9.2 %collective-permute-start.9 = (f32[4,1440]{1,0:T(4,128)S(1)}, f32[4,1440]{1,0:T(4,128)S(1)}, u32[]{:S(2)}, u32[]{:S(2)}) collective-permute-start(f32[4,1440]{1,0:T(4,128)S(1)} %get-tuple-element.51), channel_id=1, source_target_pairs={{1,2},{2,1},{3,4},{4,3},{5,6},{6,5},{7,8},{8,7},{9,10},{10,9},{11,... | collective-permute-start | bytes 69128 | tf_op jit(solution)/shard_map/ppermute | solution.py:560
  21.8 4.6 %collective-permute-start.12 = (f32[8,128]{1,0:T(8,128)S(1)}, f32[8,128]{1,0:T(8,128)S(1)}, u32[]{:S(2)}, u32[]{:S(2)}) collective-permute-start(f32[8,128]{1,0:T(8,128)S(1)} %pad_maximum_fusion.refs_0_), channel_id=1, source_target_pairs={{0,8},{1,9},{2,10},{3,11},{4,12},{5,13},{6,14},{7,15},{8,0},{9,1},... | collective-permute-start | bytes 12296 | tf_op jit(solution)/shard_map/ppermute | solution.py:640
  24.1 5.4 %collective-permute-start.11 = (f32[8,128]{1,0:T(8,128)S(1)}, f32[8,128]{1,0:T(8,128)S(1)}, u32[]{:S(2)}, u32[]{:S(2)}) collective-permute-start(f32[8,128]{1,0:T(8,128)S(1)} %pad_maximum_fusion.refs_0_), channel_id=1, source_target_pairs={{0,12},{1,13},{2,14},{3,15},{4,8},{5,9},{6,10},{7,11},{8,4},{9,5},... | collective-permute-start | bytes 12296 | tf_op jit(solution)/shard_map/ppermute | solution.py:640
  25.5 4.1 %collective-permute-start.10 = (f32[8,128]{1,0:T(8,128)S(1)}, f32[8,128]{1,0:T(8,128)S(1)}, u32[]{:S(2)}, u32[]{:S(2)}) collective-permute-start(f32[8,128]{1,0:T(8,128)S(1)} %pad_maximum_fusion.refs_0_), channel_id=1, source_target_pairs={{0,4},{1,5},{2,6},{3,7},{4,0},{5,1},{6,2},{7,3},{8,12},{9,13},{10,... | collective-permute-start | bytes 12296 | tf_op jit(solution)/shard_map/ppermute | solution.py:640

commit v7 on v6

--- a/solution.py
+++ b/solution.py
@@ -240,7 +240,7 @@
     ]
 
 
-def face_maps(own_maps, nears, fars, maps, strips, levels):
+def face_maps(own_maps, nears, fars, maps, strips, levels, kinds=3):
     count, edge = lax.axis_size("lat"), lax.axis_index("lat")
     keep = jnp.where(jnp.logical_and(edge != 0, edge != count - 1), 1.0, 0.0)
 
@@ -250,7 +250,7 @@
     for i, j in enumerate(strips):
         whole = []
         piece = piece_of(j)
-        for a in range(3):
+        for a in range(3 - kinds, 3):
             at = (PIECES[piece + 1] - PIECES[piece]) * STEPS * levels + (3 * (j - PIECES[piece]) + a) * STEPS
             low = fars[piece][at : at + STEPS, :]
             if a == 2:
@@ -259,9 +259,9 @@
             at = size * STEPS * levels + (3 * local + a) * STEPS
             high = near[at : at + STEPS, :]
             whole.append(jnp.concatenate([low, own_maps[j, 4 * a : 4 * a + 4, :], high, high, high], axis=0))
-        mix, heading, depth = whole
+        depth = whole.pop()
         blocks = [depth] + [jnp.minimum(depth, f(depth)) for f in (east, north)]
-        blocks += [0.5 * (x + f(x)) for x in (mix, heading) for f in (east, north)]
+        blocks += [0.5 * (x + f(x)) for x in whole for f in (east, north)]
         for b, block in enumerate(blocks):
             maps[i, 16 * b : 16 * b + 16, :] = block
 
@@ -402,12 +402,66 @@
     binned[...] = whole[:, :class_count]
 
 
+def base_rows(n, j, rows, own, nears, fars, laters):
+    levels = own.shape[1] // 4
+    piece = piece_of(j)
+    local = j - PIECES[piece]
+    field = {}
+    for t in rows:
+        if n > 0:
+            at = later_row(n, t) * levels
+            field[t] = laters[piece][local, at : at + levels, :]
+        elif t < 0:
+            at = (local * STEPS + t + STEPS) * levels
+            field[t] = fars[piece][at : at + levels, :]
+        elif t < 4:
+            field[t] = own[j, t * levels : (t + 1) * levels, :]
+        else:
+            near, place, _ = near_place(nears, j)
+            at = (place * STEPS + t - 4) * levels
+            field[t] = near[at : at + levels, :]
+    return field
+
+
+def kept_row(n, t):
+    return t if n == STEPS - 1 else 4 + 6 * (STEPS - 2 - n) + t + 1
+
+
+def add_terms(total, basis, steps, places, shift):
+    for t in places:
+        gap = (shift(basis[t]) if shift else basis[t + 1]) - basis[t]
+        term = gap * steps[t]
+        total[t] = total[t] + term if t in total else term
+
+
+def shares(coefs, east_total, north_total, rows):
+    none = jnp.zeros((1, LANES), jnp.float32)
+    pad = [none] * (-len(rows) % 8)
+
+    def summed(coef, kind, total):
+        return {
+            t: jnp.sum(jnp.where(coef.get(kind, t), x, 0.0), axis=0, keepdims=True) for t, x in total.items()
+        }
+
+    across = []
+    for coef, total in zip(coefs, east_total):
+        sums = summed(coef, "east_open", total)
+        across.append(jnp.concatenate([sums.get(t, none) for t in rows] + pad, axis=0))
+    turned = [west(x) for x in across]
+    strips = []
+    for coef, total, x, turn in zip(coefs, north_total, across, turned):
+        sums = summed(coef, "north_open", total)
+        along = [sums.get(t, none) + sums.get(t - 1, none) for t in rows]
+        strips.append(-0.5 * (jnp.concatenate(along + pad, axis=0) + (x + turn)))
+    whole = jnp.concatenate([x[:, GHOST : LANES - GHOST] for x in strips], axis=1)
+    return {t: whole[i : i + 1] for i, t in enumerate(rows)}
+
+
 def adjoint_part(own, own_maps, classes, weighted, *refs):
-    parts = len(PIECES) - 1
-    near_parts = len(NEAR_PIECES) - 1
+    parts, near_parts = len(PIECES) - 1, len(NEAR_PIECES) - 1
     nears, refs = refs[:near_parts], refs[near_parts:]
     fars, laters = refs[:parts], refs[parts : 2 * parts]
-    own_share, near_share, far_share, maps = refs[2 * parts :]
+    near_share, far_share, kept, maps = refs[2 * parts :]
     strips = own.shape[0]
     levels = own.shape[1] // 4
     group = list(range(strips))
@@ -425,34 +479,19 @@
             )
             adjoint[t] = jnp.where(coefs[j].get("wet", t), value, 0.0)
         adjoints.append(adjoint)
-
-    def base(n, j):
-        piece = piece_of(j)
-        local = j - PIECES[piece]
-        field = {}
-        for t in range(n - STEPS, 4 + STEPS - n):
-            if n > 0:
-                at = later_row(n, t) * levels
-                field[t] = laters[piece][local, at : at + levels, :]
-            elif t < 0:
-                at = (local * STEPS + t + STEPS) * levels
-                field[t] = fars[piece][at : at + levels, :]
-            elif t < 4:
-                field[t] = own[j, t * levels : (t + 1) * levels, :]
-            else:
-                near, place, _ = near_place(nears, j)
-                at = (place * STEPS + t - 4) * levels
-                field[t] = near[at : at + levels, :]
-        return field
-
     east_total = [{} for _ in group]
     north_total = [{} for _ in group]
     for n in reversed(range(STEPS)):
         rows = list(range(n + 1 - STEPS, 3 + STEPS - n))
         low, high = rows[0], rows[-1]
-        turned = [{t: east(field[t]) for t in rows} for field in adjoints]
-        base_steps = gaps([base(n, j) for j in group], rows)
-        to_east = [{t: turn[t] - field[t] for t in rows} for turn, field in zip(turned, adjoints)]
+        for j in group:
+            for t in range(max(low, -1), min(high, 4) + 1):
+                at = kept_row(n, t) * levels
+                kept[j, at : at + levels, :] = adjoints[j][t]
+        outer = [t for t in rows if t < 0 or t > 3]
+        turning = rows if n > 0 else outer
+        turned = [{t: east(field[t]) for t in turning} for field in adjoints]
+        to_east = [{t: turn[t] - field[t] for t in turn} for turn, field in zip(turned, adjoints)]
         to_north = [
             {low - 1: field[low], high: -field[high], **{t: field[t + 1] - field[t] for t in rows[:-1]}}
             for field in adjoints
@@ -471,45 +510,43 @@
                 following.append(new)
             adjoints = following
         for j in group:
-            for total, steps, basis in (
-                (east_total[j], to_east[j], base_steps[j][0]),
-                (north_total[j], to_north[j], base_steps[j][1]),
-            ):
-                for t in steps:
-                    term = steps[t] * basis[t]
-                    total[t] = total[t] + term if t in total else term
-    strip_shares = []
-    east_sums = []
-    none = jnp.zeros((1, LANES), jnp.float32)
-    for j in group:
-        east_sums.append(
-            jnp.concatenate(
-                [none]
-                + [
-                    jnp.sum(jnp.where(coefs[j].get("east_open", t), east_total[j][t], 0.0), axis=0, keepdims=True)
-                    for t in range(-2, 6)
-                ]
-                + [none] * 7,
-                axis=0,
-            )
-        )
-    turned = [west(x) for x in east_sums]
-    for j in group:
-        north = {
-            t: jnp.sum(jnp.where(coefs[j].get("north_open", t), north_total[j][t], 0.0), axis=0, keepdims=True)
-            for t in range(-3, 6)
-        }
-        north[-4] = north[6] = none
-        rows = [north[t] + north[t - 1] for t in range(-3, 7)] + [none] * 6
-        strip_shares.append(-0.5 * (jnp.concatenate(rows, axis=0) + (east_sums[j] + turned[j])))
-    share = jnp.concatenate([x[:, GHOST : LANES - GHOST] for x in strip_shares], axis=1)
-
-    def take(order):
-        return jnp.concatenate([share[t + 3 : t + 4] for t in order], axis=0)
-
-    own_share[...] = share[3:7]
-    far_share[...] = jnp.concatenate([take([-1, -2, -3]), jnp.zeros_like(share[:1])], axis=0)
-    near_share[...] = jnp.concatenate([jnp.zeros_like(share[:1]), take([6, 5, 4])], axis=0)
+            needed = [t for t in range(low - 1, high + 2) if t <= 0 or t >= 3]
+            basis = base_rows(n, j, needed, own, nears, fars, laters)
+            faces = [t for t in to_north[j] if t < 0 or t > 2]
+            add_terms(east_total[j], basis, to_east[j], outer, east)
+            add_terms(north_total[j], basis, to_north[j], faces, None)
+    low_rows, high_rows = [-3, -2, -1], [4, 5, 6]
+    share = shares(coefs, east_total, north_total, low_rows + high_rows)
+    blank = jnp.zeros_like(share[-1])
+    far_share[...] = jnp.concatenate([share[-1], share[-2], share[-3], blank], axis=0)
+    near_share[...] = jnp.concatenate([blank, share[6], share[5], share[4]], axis=0)
+
+
+def own_part(own, own_maps, kept, *refs):
+    parts, near_parts = len(PIECES) - 1, len(NEAR_PIECES) - 1
+    nears, refs = refs[:near_parts], refs[near_parts:]
+    fars, laters = refs[:parts], refs[parts : 2 * parts]
+    own_share, maps = refs[2 * parts :]
+    levels = own.shape[1] // 4
+    group = list(range(own.shape[0]))
+    face_maps(own_maps, nears, fars, maps, group, levels, kinds=1)
+    coefs = [Coefficients(maps, j, levels) for j in group]
+    east_total = [{} for _ in group]
+    north_total = [{} for _ in group]
+    for n in range(STEPS):
+        last = n == STEPS - 1
+        for j in group:
+            rows = range(4) if last else range(-1, 5)
+            adjoint = {t: kept[j, kept_row(n, t) * levels : (kept_row(n, t) + 1) * levels, :] for t in rows}
+            to_east = {t: east(adjoint[t]) - adjoint[t] for t in range(4)}
+            to_north = {t: adjoint[t + 1] - adjoint[t] for t in rows[:-1]}
+            if last:
+                to_north.update({-1: adjoint[0], 3: -adjoint[3]})
+            basis = base_rows(n, j, range(-1, 5), own, nears, fars, laters)
+            add_terms(east_total[j], basis, to_east, range(4), east)
+            add_terms(north_total[j], basis, to_north, range(-1, 4), None)
+    share = shares(coefs, east_total, north_total, list(range(4)))
+    own_share[...] = jnp.concatenate([share[t] for t in range(4)], axis=0)
 
 
 def near_pairs(count):
@@ -531,7 +568,7 @@
     groups = [[1]] if bits % 2 else []
     for bit in range(bits % 2, bits, 2):
         one, two = 1 << bit, 2 << bit
-        groups.append([one + two, two, one] if bit == 0 else [one, one + two, two])
+        groups.append([one + two, two, one] if bit == 0 else [two, one + two, one])
     return groups
 
 
@@ -634,26 +671,38 @@
         )(*given)
         laters.append(later)
 
-    gathered, shares = sums, None
+    gathered = sums
     groups = routes(count)
     for i, group in enumerate(groups):
         others = [lax.ppermute(gathered, "lat", [(d, d ^ k) for d in range(count)]) for k in group]
+        pieces = [gathered] + others
         if i == 0:
-            shares = pl.pallas_call(
+            near_share, far_share, kept = pl.pallas_call(
                 adjoint_part,
                 name="adjoint_part",
-                out_shape=(jax.ShapeDtypeStruct((rows, lon_count), f32),) * 3,
+                out_shape=(
+                    jax.ShapeDtypeStruct((rows, lon_count), f32),
+                    jax.ShapeDtypeStruct((rows, lon_count), f32),
+                    jax.ShapeDtypeStruct((strips, 16 * levels, LANES), f32),
+                ),
                 in_specs=vmem(4 + len(nears) + 2 * len(sizes)),
                 out_specs=tuple(vmem(3)),
                 scratch_shapes=[pltpu.VMEM((strips, 16 * MAP_FIELDS, LANES), f32)],
                 compiler_params=params,
             )(own, own_maps, own_classes, weighted[0], *nears, *fars, *laters)
-        pieces = [gathered] + others
-        if i == 0:
-            *pieces, own_share, near_share, far_share = lax.optimization_barrier((*pieces, *shares))
+            *pieces, near_share, far_share = lax.optimization_barrier((*pieces, near_share, far_share))
             near_share, far_share = to_near(near_share), to_far(far_share)
         if i + 1 < len(groups):
             gathered = jnp.concatenate(pieces, axis=0)
+    own_share = pl.pallas_call(
+        own_part,
+        name="own_part",
+        out_shape=jax.ShapeDtypeStruct((rows, lon_count), f32),
+        in_specs=vmem(3 + len(nears) + 2 * len(sizes)),
+        out_specs=pl.BlockSpec(memory_space=pltpu.VMEM),
+        scratch_shapes=[pltpu.VMEM((strips, 16 * 3, LANES), f32)],
+        compiler_params=params,
+    )(own, own_maps, kept, *nears, *fars, *laters)
     binned, gradient = pl.pallas_call(
         finish,
         name="finish",

time: 30.4 us -> 29.8 us (0.980)
  waiting for transfers between devices: 4.73 us -> 3.27 us
  Pallas kernels: 10.8 us -> 11.4 us
    ppermute x6, waiting for transfers between devices: 4.31 us -> 2.9 us  [body(): lax.ppermute(gathered, 'lat', [(d, d ^ k) for d in range(count)])]
    pallas_call x0 -> x1, Pallas kernels: none -> 1.2 us  [body(): pl.pallas_call(own_part, name='own_part', out_shape=jax.ShapeDtypeStruct(...]
    pallas_call x1, Pallas kernels: 2.42 us -> 1.82 us  [body(): pl.pallas_call(adjoint_part, name='adjoint_part', out_shape=(jax.ShapeDty...]
  transfers between devices with their start and end apart: 13 -> 13, of which waited for: 4 -> 3; matrix products, arithmetic and copies ran while one was open for 0% -> 0% of each run, Pallas kernels for 24% -> 27%
where the time goes in v7:
time: 29.8 us; the launch traced here: 29.6 us
  starting transfers between devices  14.1 us (47%)
  Pallas kernels  11.4 us (38%)
  waiting for transfers between devices  3.27 us (11%)
  between operations  0.73 us (2%)
    ppermute x6, starting transfers between devices, body(): lax.ppermute(gathered, 'lat', [(d, d ^ k) for d in range(count)])  7.14 us
    ppermute x3, starting transfers between devices, to_far(): return lax.ppermute(x, ('members', 'lat'), far_pairs(members, count))  5.99 us
    pallas_call x2, Pallas kernels, body(): pl.pallas_call(functools.partial(forward, piece), name='forward', out_sha...  3.32 us
    ppermute x6, waiting for transfers between devices, body(): lax.ppermute(gathered, 'lat', [(d, d ^ k) for d in range(count)])  2.9 us
    pallas_call x1, Pallas kernels, body(): pl.pallas_call(adjoint_part, name='adjoint_part', out_shape=(jax.ShapeDty...  1.82 us
    pallas_call x1, Pallas kernels, body(): pl.pallas_call(pack_fields, name='pack_fields', out_shape=(jax.ShapeDtype...  1.73 us
    pallas_call x1, Pallas kernels, body(): pl.pallas_call(pack_classes, name='pack_classes', out_shape=(jax.ShapeDty...  1.42 us
    pallas_call x1, Pallas kernels, body(): pl.pallas_call(pack_first, name='pack_first', out_shape=far_shapes[0], ou...  1.3 us
  transfers between devices with their start and end apart: 13, of which 3 were waited for; matrix products, arithmetic and copies ran while one was open for 0% of the time, Pallas kernels for 27%

profile of v7, /device:TPU:0, one launch (start us, length us, event | category | flops | bytes accessed | tf_op | source)
XLA Modules:
  0.0 29.6 jit_solution(6011519809475406747)
XLA Ops:
  0.6 1.3 %pack_first.1 = f32[399,128]{1,0:T(8,128)S(1)} custom-call(f32[16,4,1440]{2,1,0:T(4,128)} %refs_0_.3, f32[4,1440]{1,0:T(4,128)} %refs_1_.3, f32[4,1440]{1,0:T(4,128)} %refs_2_.3, s32[4,1440]{1,0:T(4,128)} %refs_3_.2), custom_call_target="tpu_custom_call" | custom-call | tf_op jit(solution)/shard_map/pack_first/pallas_call | solution.py:609
  1.9 3.0 %collective-permute-start.4 = (f32[399,128]{1,0:T(8,128)S(1)}, f32[399,128]{1,0:T(8,128)S(1)}, u32[]{:S(2)}, u32[]{:S(2)}) collective-permute-start(f32[399,128]{1,0:T(8,128)S(1)} %pack_first.1), channel_id=1, source_target_pairs={{1,2},{2,1},{3,4},{4,3},{5,6},{6,5},{7,8},{8,7},{9,10},{10,9},{11,... | collective-permute-start | bytes 612872 | tf_op jit(solution)/shard_map/ppermute | solution.py:597
  4.9 1.7 %pack_fields.1 = (f32[12,64,128]{2,1,0:T(8,128)S(1)}, f32[12,16,128]{2,1,0:T(8,128)S(1)}, f32[228,128]{1,0:T(8,128)S(1)}, f32[228,128]{1,0:T(8,128)S(1)}, f32[22...) custom-call(f32[16,4,1440]{2,1,0:T(4,128)} %refs_0_.3, f32[4,1440]{1,0:T(4,128)} %refs_1_.3, f32[4,1440]{1,0:T(4,128)} %refs_2_.3, ...), custom_call_target="tpu_custom_call" | custom-call | tf_op jit(solution)/shard_map/pack_fields/pallas_call | solution.py:619
  6.7 0.2 collective-permute-start.1
  6.9 0.4 %collective-permute-start.2 = (f32[228,128]{1,0:T(8,128)S(1)}, f32[228,128]{1,0:T(8,128)S(1)}, u32[]{:S(2)}, u32[]{:S(2)}) collective-permute-start(f32[228,128]{1,0:T(8,128)S(1)} %get-tuple-element.37), channel_id=1, source_target_pairs={{0,1},{1,0},{2,3},{3,2},{4,5},{5,4},{6,7},{7,6},{8,9},{9,8},{10,11... | collective-permute-start | bytes 350216 | tf_op jit(solution)/shard_map/ppermute | solution.py:594
  7.3 0.1 collective-permute-start.3
  7.4 1.5 %collective-permute-start = (f32[285,128]{1,0:T(8,128)S(1)}, f32[285,128]{1,0:T(8,128)S(1)}, u32[]{:S(2)}, u32[]{:S(2)}) collective-permute-start(f32[285,128]{1,0:T(8,128)S(1)} %get-tuple-element.35), channel_id=1, source_target_pairs={{1,2},{2,1},{3,4},{4,3},{5,6},{6,5},{7,8},{8,7},{9,10},{10,9},{11,... | collective-permute-start | bytes 437768 | tf_op jit(solution)/shard_map/ppermute | solution.py:597
  8.9 1.4 %pack_classes.1 = (s32[12,64,128]{2,1,0:T(8,128)S(1)}, f32[8,128]{1,0:T(8,128)S(1)}) custom-call(s32[16,4,1440]{2,1,0:T(4,128)} %refs_0_.4, f32[32,72]{1,0:T(8,128)} %refs_1_.4, s32[4]{0:T(128)} %refs_2_.4), custom_call_target="tpu_custom_call" | custom-call | tf_op jit(solution)/shard_map/pack_classes/pallas_call | solution.py:634
  10.3 0.0 collective-permute-done.1.refs_4_.refs_0_
  10.3 0.0 collective-permute-done.2.refs_5_.refs_1_
  10.3 0.0 collective-permute-done.3.refs_6_.refs_2_
  10.4 0.0 collective-permute-done.4.refs_2_.refs_3_
  10.4 1.8 %forward.2 = (f32[2,144,256]{2,1,0:T(8,128)S(1)}, f32[7,224,128]{2,1,0:T(8,128)S(1)}) custom-call(f32[12,64,128]{2,1,0:T(8,128)S(1)} %get-tuple-element.32.refs_0_.own, f32[12,16,128]{2,1,0:T(8,128)S(1)} %get-tuple-element.33.refs_1_.own_maps, f32[399,128]{1,0:T(8,128)S(1)} %collective-permute-done.4.refs_2_.refs_3_, ...), custom_call_target="tpu_custom_call" | custom-call | flops 2307000064 | bytes 7380000 | tf_op jit(solution)/shard_map/forward/pallas_call | solution.py:657
  12.2 0.4 %collective-permute-done.refs_2_.refs_4_ = f32[285,128]{1,0:T(8,128)S(1)} collective-permute-done((f32[285,128]{1,0:T(8,128)S(1)}, f32[285,128]{1,0:T(8,128)S(1)}, u32[]{:S(2)}, u32[]{:S(2)}) %collective-permute-start) | collective-permute-done | bytes 145952 | tf_op jit(solution)/shard_map/ppermute | solution.py:597
  12.5 1.5 %forward.3 = (f32[2,128]{1,0:T(2,128)S(1)}, f32[5,224,128]{2,1,0:T(8,128)S(1)}, f32[8,128]{1,0:T(8,128)S(1)}) custom-call(f32[12,64,128]{2,1,0:T(8,128)S(1)} %get-tuple-element.32.refs_0_.own, f32[12,16,128]{2,1,0:T(8,128)S(1)} %get-tuple-element.33.refs_1_.own_maps, f32[285,128]{1,0:T(8,128)S(1)} %collective-permute-done.refs_2_.refs_4_, ...), custom_call_target="tpu_custom_call" | custom-call | flops 2307000064 | bytes 7380000 | tf_op jit(solution)/shard_map/forward/pallas_call | solution.py:657
  14.0 1.7 %collective-permute-start.5 = (f32[2,128]{1,0:T(2,128)S(1)}, f32[2,128]{1,0:T(2,128)S(1)}, u32[]{:S(2)}, u32[]{:S(2)}) collective-permute-start(f32[2,128]{1,0:T(2,128)S(1)} %get-tuple-element.50), channel_id=1, source_target_pairs={{0,3},{1,2},{2,1},{3,0},{4,7},{5,6},{6,5},{7,4},{8,11},{9,10},{10,... | collective-permute-start | bytes 3080 | tf_op jit(solution)/shard_map/ppermute | solution.py:677
  15.7 1.4 %collective-permute-start.6 = (f32[2,128]{1,0:T(2,128)S(1)}, f32[2,128]{1,0:T(2,128)S(1)}, u32[]{:S(2)}, u32[]{:S(2)}) collective-permute-start(f32[2,128]{1,0:T(2,128)S(1)} %get-tuple-element.50), channel_id=1, source_target_pairs={{0,2},{1,3},{2,0},{3,1},{4,6},{5,7},{6,4},{7,5},{8,10},{9,11},{10,... | collective-permute-start | bytes 3080 | tf_op jit(solution)/shard_map/ppermute | solution.py:677
  17.2 0.0 collective-permute-start.7
  17.2 1.8 %adjoint_part.1 = (f32[4,1440]{1,0:T(4,128)S(1)}, f32[4,1440]{1,0:T(4,128)S(1)}, f32[12,256,128]{2,1,0:T(8,128)S(1)}) custom-call(f32[12,64,128]{2,1,0:T(8,128)S(1)} %get-tuple-element.32.refs_0_.own, f32[12,16,128]{2,1,0:T(8,128)S(1)} %get-tuple-element.33.refs_1_.own_maps, s32[12,64,128]{2,1,0:T(8,128)S(1)} %get-tuple-element.34.refs_3_.classes, ...), custom_call_target="tpu_custom_call" | custom-call | tf_op jit(solution)/shard_map/adjoint_part/pallas_call | solution.py:680
  19.0 0.0 collective-permute-done.5
  19.0 0.3 collective-permute-done.6
  19.3 0.3 %collective-permute-start.8 = (f32[4,1440]{1,0:T(4,128)S(1)}, f32[4,1440]{1,0:T(4,128)S(1)}, u32[]{:S(2)}, u32[]{:S(2)}) collective-permute-start(f32[4,1440]{1,0:T(4,128)S(1)} %get-tuple-element.48), channel_id=1, source_target_pairs={{0,1},{1,0},{2,3},{3,2},{4,5},{5,4},{6,7},{7,6},{8,9},{9,8},{10,11... | collective-permute-start | bytes 69128 | tf_op jit(solution)/shard_map/ppermute | solution.py:594
  19.6 1.5 %collective-permute-start.9 = (f32[4,1440]{1,0:T(4,128)S(1)}, f32[4,1440]{1,0:T(4,128)S(1)}, u32[]{:S(2)}, u32[]{:S(2)}) collective-permute-start(f32[4,1440]{1,0:T(4,128)S(1)} %get-tuple-element.49), channel_id=1, source_target_pairs={{1,2},{2,1},{3,4},{4,3},{5,6},{6,5},{7,8},{8,7},{9,10},{10,9},{11,... | collective-permute-start | bytes 69128 | tf_op jit(solution)/shard_map/ppermute | solution.py:597
  21.1 2.4 %collective-permute-start.10 = (f32[8,128]{1,0:T(8,128)S(1)}, f32[8,128]{1,0:T(8,128)S(1)}, u32[]{:S(2)}, u32[]{:S(2)}) collective-permute-start(f32[8,128]{1,0:T(8,128)S(1)} %pad_maximum_fusion.refs_0_), channel_id=1, source_target_pairs={{0,8},{1,9},{2,10},{3,11},{4,12},{5,13},{6,14},{7,15},{8,0},{9,1},... | collective-permute-start | bytes 12296 | tf_op jit(solution)/shard_map/ppermute | solution.py:677
  23.5 1.3 %collective-permute-start.11 = (f32[8,128]{1,0:T(8,128)S(1)}, f32[8,128]{1,0:T(8,128)S(1)}, u32[]{:S(2)}, u32[]{:S(2)}) collective-permute-start(f32[8,128]{1,0:T(8,128)S(1)} %pad_maximum_fusion.refs_0_), channel_id=1, source_target_pairs={{0,12},{1,13},{2,14},{3,15},{4,8},{5,9},{6,10},{7,11},{8,4},{9,5},... | collective-permute-start | bytes 12296 | tf_op jit(solution)/shard_map/ppermute | solution.py:677
  24.9 0.2 collective-permute-start.12
  25.1 1.2 %own_part.1.own_share = f32[4,1440]{1,0:T(4,128)S(1)} custom-call(f32[12,64,128]{2,1,0:T(8,128)S(1)} %get-tuple-element.32.refs_0_.own, f32[12,16,128]{2,1,0:T(8,128)S(1)} %get-tuple-element.33.refs_1_.own_maps, f32[12,256,128]{2,1,0:T(8,128)S(1)} %get-tuple-element.44.kept, f32[228,128]{1,0:T(8,128)S(1)} %collective-permute-done.1.refs_4_.refs_0_, ...), custom_call_target="tpu_custom_call" | custom-call | tf_op jit(solution)/shard_map/own_part/pallas_call | solution.py:697
  26.3 2.6 %collective-permute-done.11.refs_2_ = f32[8,128]{1,0:T(8,128)S(1)} collective-permute-done((f32[8,128]{1,0:T(8,128)S(1)}, f32[8,128]{1,0:T(8,128)S(1)}, u32[]{:S(2)}, u32[]{:S(2)}) %collective-permute-start.11) | collective-permute-done | bytes 4128 | tf_op jit(solution)/shard_map/ppermute | solution.py:677
  28.9 0.0 collective-permute-done.12.refs_3_
  28.9 0.0 collective-permute-done.8.near_share
  28.9 0.0 collective-permute-done.9.far_share
  28.9 0.7 %finish.1 = (f32[2,72]{1,0:T(2,128)}, f32[4,1440]{1,0:T(4,128)}) custom-call(f32[4,1440]{1,0:T(4,128)S(1)} %own_part.1.own_share, f32[4,1440]{1,0:T(4,128)S(1)} %collective-permute-done.8.near_share, f32[4,1440]{1,0:T(4,128)S(1)} %collective-permute-done.9.far_share, f32[8,128]{1,0:T(8,128)S(1)} %pad_maximum_fusion.refs_0_, ...), custom_call_target="tpu_custom_call" | custom-call | tf_op jit(solution)/shard_map/finish/pallas_call | solution.py:706
  (3 shorter events, 0.0 us)
Async XLA Ops:
  1.9 8.4 %collective-permute-start.4 = (f32[399,128]{1,0:T(8,128)S(1)}, f32[399,128]{1,0:T(8,128)S(1)}, u32[]{:S(2)}, u32[]{:S(2)}) collective-permute-start(f32[399,128]{1,0:T(8,128)S(1)} %pack_first.1), channel_id=1, source_target_pairs={{1,2},{2,1},{3,4},{4,3},{5,6},{6,5},{7,8},{8,7},{9,10},{10,9},{11,... | collective-permute-start | bytes 612872 | tf_op jit(solution)/shard_map/ppermute | solution.py:597
  6.7 3.6 %collective-permute-start.1 = (f32[228,128]{1,0:T(8,128)S(1)}, f32[228,128]{1,0:T(8,128)S(1)}, u32[]{:S(2)}, u32[]{:S(2)}) collective-permute-start(f32[228,128]{1,0:T(8,128)S(1)} %get-tuple-element.36), channel_id=1, source_target_pairs={{0,1},{1,0},{2,3},{3,2},{4,5},{5,4},{6,7},{7,6},{8,9},{9,8},{10,11... | collective-permute-start | bytes 350216 | tf_op jit(solution)/shard_map/ppermute | solution.py:594
  6.9 3.4 %collective-permute-start.2 = (f32[228,128]{1,0:T(8,128)S(1)}, f32[228,128]{1,0:T(8,128)S(1)}, u32[]{:S(2)}, u32[]{:S(2)}) collective-permute-start(f32[228,128]{1,0:T(8,128)S(1)} %get-tuple-element.37), channel_id=1, source_target_pairs={{0,1},{1,0},{2,3},{3,2},{4,5},{5,4},{6,7},{7,6},{8,9},{9,8},{10,11... | collective-permute-start | bytes 350216 | tf_op jit(solution)/shard_map/ppermute | solution.py:594
  7.3 3.1 %collective-permute-start.3 = (f32[228,128]{1,0:T(8,128)S(1)}, f32[228,128]{1,0:T(8,128)S(1)}, u32[]{:S(2)}, u32[]{:S(2)}) collective-permute-start(f32[228,128]{1,0:T(8,128)S(1)} %get-tuple-element.38), channel_id=1, source_target_pairs={{0,1},{1,0},{2,3},{3,2},{4,5},{5,4},{6,7},{7,6},{8,9},{9,8},{10,11... | collective-permute-start | bytes 350216 | tf_op jit(solution)/shard_map/ppermute | solution.py:594
  7.4 5.1 %collective-permute-start = (f32[285,128]{1,0:T(8,128)S(1)}, f32[285,128]{1,0:T(8,128)S(1)}, u32[]{:S(2)}, u32[]{:S(2)}) collective-permute-start(f32[285,128]{1,0:T(8,128)S(1)} %get-tuple-element.35), channel_id=1, source_target_pairs={{1,2},{2,1},{3,4},{4,3},{5,6},{6,5},{7,8},{8,7},{9,10},{10,9},{11,... | collective-permute-start | bytes 437768 | tf_op jit(solution)/shard_map/ppermute | solution.py:597
  14.0 5.0 %collective-permute-start.5 = (f32[2,128]{1,0:T(2,128)S(1)}, f32[2,128]{1,0:T(2,128)S(1)}, u32[]{:S(2)}, u32[]{:S(2)}) collective-permute-start(f32[2,128]{1,0:T(2,128)S(1)} %get-tuple-element.50), channel_id=1, source_target_pairs={{0,3},{1,2},{2,1},{3,0},{4,7},{5,6},{6,5},{7,4},{8,11},{9,10},{10,... | collective-permute-start | bytes 3080 | tf_op jit(solution)/shard_map/ppermute | solution.py:677
  15.7 3.6 %collective-permute-start.6 = (f32[2,128]{1,0:T(2,128)S(1)}, f32[2,128]{1,0:T(2,128)S(1)}, u32[]{:S(2)}, u32[]{:S(2)}) collective-permute-start(f32[2,128]{1,0:T(2,128)S(1)} %get-tuple-element.50), channel_id=1, source_target_pairs={{0,2},{1,3},{2,0},{3,1},{4,6},{5,7},{6,4},{7,5},{8,10},{9,11},{10,... | collective-permute-start | bytes 3080 | tf_op jit(solution)/shard_map/ppermute | solution.py:677
  17.2 2.2 %collective-permute-start.7 = (f32[2,128]{1,0:T(2,128)S(1)}, f32[2,128]{1,0:T(2,128)S(1)}, u32[]{:S(2)}, u32[]{:S(2)}) collective-permute-start(f32[2,128]{1,0:T(2,128)S(1)} %get-tuple-element.50), channel_id=1, source_target_pairs={{0,1},{1,0},{2,3},{3,2},{4,5},{5,4},{6,7},{7,6},{8,9},{9,8},{10,11... | collective-permute-start | bytes 3080 | tf_op jit(solution)/shard_map/ppermute | solution.py:677
  19.3 9.6 %collective-permute-start.8 = (f32[4,1440]{1,0:T(4,128)S(1)}, f32[4,1440]{1,0:T(4,128)S(1)}, u32[]{:S(2)}, u32[]{:S(2)}) collective-permute-start(f32[4,1440]{1,0:T(4,128)S(1)} %get-tuple-element.48), channel_id=1, source_target_pairs={{0,1},{1,0},{2,3},{3,2},{4,5},{5,4},{6,7},{7,6},{8,9},{9,8},{10,11... | collective-permute-start | bytes 69128 | tf_op jit(solution)/shard_map/ppermute | solution.py:594
  19.6 9.3 %collective-permute-start.9 = (f32[4,1440]{1,0:T(4,128)S(1)}, f32[4,1440]{1,0:T(4,128)S(1)}, u32[]{:S(2)}, u32[]{:S(2)}) collective-permute-start(f32[4,1440]{1,0:T(4,128)S(1)} %get-tuple-element.49), channel_id=1, source_target_pairs={{1,2},{2,1},{3,4},{4,3},{5,6},{6,5},{7,8},{8,7},{9,10},{10,9},{11,... | collective-permute-start | bytes 69128 | tf_op jit(solution)/shard_map/ppermute | solution.py:597
  21.1 5.2 %collective-permute-start.10 = (f32[8,128]{1,0:T(8,128)S(1)}, f32[8,128]{1,0:T(8,128)S(1)}, u32[]{:S(2)}, u32[]{:S(2)}) collective-permute-start(f32[8,128]{1,0:T(8,128)S(1)} %pad_maximum_fusion.refs_0_), channel_id=1, source_target_pairs={{0,8},{1,9},{2,10},{3,11},{4,12},{5,13},{6,14},{7,15},{8,0},{9,1},... | collective-permute-start | bytes 12296 | tf_op jit(solution)/shard_map/ppermute | solution.py:677
  23.5 5.4 %collective-permute-start.11 = (f32[8,128]{1,0:T(8,128)S(1)}, f32[8,128]{1,0:T(8,128)S(1)}, u32[]{:S(2)}, u32[]{:S(2)}) collective-permute-start(f32[8,128]{1,0:T(8,128)S(1)} %pad_maximum_fusion.refs_0_), channel_id=1, source_target_pairs={{0,12},{1,13},{2,14},{3,15},{4,8},{5,9},{6,10},{7,11},{8,4},{9,5},... | collective-permute-start | bytes 12296 | tf_op jit(solution)/shard_map/ppermute | solution.py:677
  24.9 4.1 %collective-permute-start.12 = (f32[8,128]{1,0:T(8,128)S(1)}, f32[8,128]{1,0:T(8,128)S(1)}, u32[]{:S(2)}, u32[]{:S(2)}) collective-permute-start(f32[8,128]{1,0:T(8,128)S(1)} %pad_maximum_fusion.refs_0_), channel_id=1, source_target_pairs={{0,4},{1,5},{2,6},{3,7},{4,0},{5,1},{6,2},{7,3},{8,12},{9,13},{10,... | collective-permute-start | bytes 12296 | tf_op jit(solution)/shard_map/ppermute | solution.py:677

commit v8 on v7

--- a/solution.py
+++ b/solution.py
@@ -240,7 +240,7 @@
     ]
 
 
-def face_maps(own_maps, nears, fars, maps, strips, levels, kinds=3):
+def face_maps(own_maps, nears, fars, maps, strips, levels, kinds=(0, 1, 2)):
     count, edge = lax.axis_size("lat"), lax.axis_index("lat")
     keep = jnp.where(jnp.logical_and(edge != 0, edge != count - 1), 1.0, 0.0)
 
@@ -250,7 +250,7 @@
     for i, j in enumerate(strips):
         whole = []
         piece = piece_of(j)
-        for a in range(3 - kinds, 3):
+        for a in kinds:
             at = (PIECES[piece + 1] - PIECES[piece]) * STEPS * levels + (3 * (j - PIECES[piece]) + a) * STEPS
             low = fars[piece][at : at + STEPS, :]
             if a == 2:
@@ -424,7 +424,9 @@
 
 
 def kept_row(n, t):
-    return t if n == STEPS - 1 else 4 + 6 * (STEPS - 2 - n) + t + 1
+    if n == STEPS - 1:
+        return t
+    return 4 + t + 1 if n > 0 else 10 + {-1: 0, 0: 1, 3: 2, 4: 3}[t]
 
 
 def add_terms(total, basis, steps, places, shift):
@@ -465,7 +467,7 @@
     strips = own.shape[0]
     levels = own.shape[1] // 4
     group = list(range(strips))
-    face_maps(own_maps, nears, fars, maps, group, levels)
+    face_maps(own_maps, nears, fars, maps, group, levels, kinds=(0, 2))
     coefs = [Coefficients(maps, j, levels) for j in group]
     adjoints = []
     for j in group:
@@ -485,26 +487,31 @@
         rows = list(range(n + 1 - STEPS, 3 + STEPS - n))
         low, high = rows[0], rows[-1]
         for j in group:
-            for t in range(max(low, -1), min(high, 4) + 1):
+            for t in [t for t in adjoints[j] if -1 <= t <= 4]:
                 at = kept_row(n, t) * levels
                 kept[j, at : at + levels, :] = adjoints[j][t]
         outer = [t for t in rows if t < 0 or t > 3]
-        turning = rows if n > 0 else outer
+        made = [t for t in rows if n != 1 or t < 1 or t > 2]
+        turning = made if n > 0 else outer
         turned = [{t: east(field[t]) for t in turning} for field in adjoints]
         to_east = [{t: turn[t] - field[t] for t in turn} for turn, field in zip(turned, adjoints)]
         to_north = [
-            {low - 1: field[low], high: -field[high], **{t: field[t + 1] - field[t] for t in rows[:-1]}}
+            {
+                low - 1: field[low],
+                high: -field[high],
+                **{t: field[t + 1] - field[t] for t in rows[:-1] if t in field and t + 1 in field},
+            }
             for field in adjoints
         ]
         if n > 0:
-            across = [{t: coef.get("east_mix", t) * x[t] for t in rows} for coef, x in zip(coefs, to_east)]
-            turned = [{t: west(x[t]) for t in rows} for x in across]
+            across = [{t: coef.get("east_mix", t) * x[t] for t in made} for coef, x in zip(coefs, to_east)]
+            turned = [{t: west(x[t]) for t in made} for x in across]
             along = [{t: coef.get("north_mix", t) * x[t] for t in x} for coef, x in zip(coefs, to_north)]
             following = []
             for j in group:
                 field, flux = adjoints[j], along[j]
                 new = {low - 1: flux[low - 1], high + 1: -flux[high]}
-                for t in rows:
+                for t in made:
                     still = field[t] + column(field[t], coefs[j].get("column", t)) + (flux[t] - flux[t - 1])
                     new[t] = still + (across[j][t] - turned[j][t])
                 following.append(new)
@@ -529,17 +536,29 @@
     own_share, maps = refs[2 * parts :]
     levels = own.shape[1] // 4
     group = list(range(own.shape[0]))
-    face_maps(own_maps, nears, fars, maps, group, levels, kinds=1)
+    face_maps(own_maps, nears, fars, maps, group, levels, kinds=(0, 2))
     coefs = [Coefficients(maps, j, levels) for j in group]
     east_total = [{} for _ in group]
     north_total = [{} for _ in group]
+
+    def adjoint_of(n, j, rows):
+        return {t: kept[j, kept_row(n, t) * levels : (kept_row(n, t) + 1) * levels, :] for t in rows}
+
+    middle = [adjoint_of(1, j, range(4)) for j in group]
+    across, along = zip(*fluxes(coefs, "mix", gaps(middle, [1, 2])))
+    inner = gathered_in(list(zip(across, along)), [1, 2], middle, coefs)
     for n in range(STEPS):
         last = n == STEPS - 1
+        adjoints = []
         for j in group:
-            rows = range(4) if last else range(-1, 5)
-            adjoint = {t: kept[j, kept_row(n, t) * levels : (kept_row(n, t) + 1) * levels, :] for t in rows}
+            if n == 0:
+                adjoints.append({**adjoint_of(0, j, (-1, 0, 3, 4)), **inner[j]})
+            else:
+                adjoints.append(adjoint_of(n, j, range(4) if last else range(-1, 5)))
+        for j, adjoint in zip(group, adjoints):
             to_east = {t: east(adjoint[t]) - adjoint[t] for t in range(4)}
-            to_north = {t: adjoint[t + 1] - adjoint[t] for t in rows[:-1]}
+            faces = range(3) if last else range(-1, 4)
+            to_north = {t: adjoint[t + 1] - adjoint[t] for t in faces}
             if last:
                 to_north.update({-1: adjoint[0], 3: -adjoint[3]})
             basis = base_rows(n, j, range(-1, 5), own, nears, fars, laters)
@@ -565,11 +584,11 @@
 
 def routes(count):
     bits = count.bit_length() - 1
-    groups = [[1]] if bits % 2 else []
-    for bit in range(bits % 2, bits, 2):
+    groups = []
+    for bit in range(bits - 2, -1, -2):
         one, two = 1 << bit, 2 << bit
-        groups.append([one + two, two, one] if bit == 0 else [two, one + two, one])
-    return groups
+        groups.append([one, one + two, two] if bit > 0 else [3, 2, 1])
+    return groups + ([[1]] if bits % 2 else [])
 
 
 def vmem(count):
@@ -683,14 +702,13 @@
                 out_shape=(
                     jax.ShapeDtypeStruct((rows, lon_count), f32),
                     jax.ShapeDtypeStruct((rows, lon_count), f32),
-                    jax.ShapeDtypeStruct((strips, 16 * levels, LANES), f32),
+                    jax.ShapeDtypeStruct((strips, 14 * levels, LANES), f32),
                 ),
                 in_specs=vmem(4 + len(nears) + 2 * len(sizes)),
                 out_specs=tuple(vmem(3)),
-                scratch_shapes=[pltpu.VMEM((strips, 16 * MAP_FIELDS, LANES), f32)],
+                scratch_shapes=[pltpu.VMEM((strips, 16 * 5, LANES), f32)],
                 compiler_params=params,
             )(own, own_maps, own_classes, weighted[0], *nears, *fars, *laters)
-            *pieces, near_share, far_share = lax.optimization_barrier((*pieces, near_share, far_share))
             near_share, far_share = to_near(near_share), to_far(far_share)
         if i + 1 < len(groups):
             gathered = jnp.concatenate(pieces, axis=0)
@@ -700,7 +718,7 @@
         out_shape=jax.ShapeDtypeStruct((rows, lon_count), f32),
         in_specs=vmem(3 + len(nears) + 2 * len(sizes)),
         out_specs=pl.BlockSpec(memory_space=pltpu.VMEM),
-        scratch_shapes=[pltpu.VMEM((strips, 16 * 3, LANES), f32)],
+        scratch_shapes=[pltpu.VMEM((strips, 16 * 5, LANES), f32)],
         compiler_params=params,
     )(own, own_maps, kept, *nears, *fars, *laters)
     binned, gradient = pl.pallas_call(

time: 29.8 us -> 28.1 us (0.943)
  waiting for transfers between devices: 3.27 us -> 1.28 us
  starting transfers between devices: 14.1 us -> 14.5 us
    ppermute x6, waiting for transfers between devices: 2.9 us -> 0.92 us  [body(): lax.ppermute(gathered, 'lat', [(d, d ^ k) for d in range(count)])]
  transfers between devices with their start and end apart: 13 -> 13, of which waited for: 3 -> 3; matrix products, arithmetic and copies ran while one was open for 0% -> 0% of each run, Pallas kernels for 27% -> 28%
where the time goes in v8:
time: 28.1 us; the launch traced here: 27.9 us
  starting transfers between devices  14.5 us (52%)
  Pallas kernels  11.3 us (40%)
  waiting for transfers between devices  1.28 us (5%)
  between operations  0.73 us (3%)
    ppermute x6, starting transfers between devices, body(): lax.ppermute(gathered, 'lat', [(d, d ^ k) for d in range(count)])  7.38 us
    ppermute x3, starting transfers between devices, to_far(): return lax.ppermute(x, ('members', 'lat'), far_pairs(members, count))  5.99 us
    pallas_call x2, Pallas kernels, body(): pl.pallas_call(functools.partial(forward, piece), name='forward', out_sha...  3.32 us
    pallas_call x1, Pallas kernels, body(): pl.pallas_call(pack_fields, name='pack_fields', out_shape=(jax.ShapeDtype...  1.73 us
    pallas_call x1, Pallas kernels, body(): pl.pallas_call(adjoint_part, name='adjoint_part', out_shape=(jax.ShapeDty...  1.65 us
    pallas_call x1, Pallas kernels, body(): pl.pallas_call(pack_classes, name='pack_classes', out_shape=(jax.ShapeDty...  1.42 us
    pallas_call x1, Pallas kernels, body(): pl.pallas_call(pack_first, name='pack_first', out_shape=far_shapes[0], ou...  1.3 us
    pallas_call x1, Pallas kernels, body(): pl.pallas_call(own_part, name='own_part', out_shape=jax.ShapeDtypeStruct(...  1.28 us
  transfers between devices with their start and end apart: 13, of which 3 were waited for; matrix products, arithmetic and copies ran while one was open for 0% of the time, Pallas kernels for 28%

profile of v8, /device:TPU:0, one launch (start us, length us, event | category | flops | bytes accessed | tf_op | source)
XLA Modules:
  0.0 27.9 jit_solution(16859466058143389948)
XLA Ops:
  0.6 1.3 %pack_first.1 = f32[399,128]{1,0:T(8,128)S(1)} custom-call(f32[16,4,1440]{2,1,0:T(4,128)} %refs_0_.3, f32[4,1440]{1,0:T(4,128)} %refs_1_.3, f32[4,1440]{1,0:T(4,128)} %refs_2_.3, s32[4,1440]{1,0:T(4,128)} %refs_3_.2), custom_call_target="tpu_custom_call" | custom-call | tf_op jit(solution)/shard_map/pack_first/pallas_call | solution.py:628
  1.9 3.0 %collective-permute-start.4 = (f32[399,128]{1,0:T(8,128)S(1)}, f32[399,128]{1,0:T(8,128)S(1)}, u32[]{:S(2)}, u32[]{:S(2)}) collective-permute-start(f32[399,128]{1,0:T(8,128)S(1)} %pack_first.1), channel_id=1, source_target_pairs={{1,2},{2,1},{3,4},{4,3},{5,6},{6,5},{7,8},{8,7},{9,10},{10,9},{11,... | collective-permute-start | bytes 612872 | tf_op jit(solution)/shard_map/ppermute | solution.py:616
  4.9 1.7 %pack_fields.1 = (f32[12,64,128]{2,1,0:T(8,128)S(1)}, f32[12,16,128]{2,1,0:T(8,128)S(1)}, f32[228,128]{1,0:T(8,128)S(1)}, f32[228,128]{1,0:T(8,128)S(1)}, f32[22...) custom-call(f32[16,4,1440]{2,1,0:T(4,128)} %refs_0_.3, f32[4,1440]{1,0:T(4,128)} %refs_1_.3, f32[4,1440]{1,0:T(4,128)} %refs_2_.3, ...), custom_call_target="tpu_custom_call" | custom-call | tf_op jit(solution)/shard_map/pack_fields/pallas_call | solution.py:638
  6.7 0.2 collective-permute-start.1
  6.9 0.4 %collective-permute-start.2 = (f32[228,128]{1,0:T(8,128)S(1)}, f32[228,128]{1,0:T(8,128)S(1)}, u32[]{:S(2)}, u32[]{:S(2)}) collective-permute-start(f32[228,128]{1,0:T(8,128)S(1)} %get-tuple-element.31), channel_id=1, source_target_pairs={{0,1},{1,0},{2,3},{3,2},{4,5},{5,4},{6,7},{7,6},{8,9},{9,8},{10,11... | collective-permute-start | bytes 350216 | tf_op jit(solution)/shard_map/ppermute | solution.py:613
  7.3 0.1 collective-permute-start.3
  7.4 1.5 %collective-permute-start = (f32[285,128]{1,0:T(8,128)S(1)}, f32[285,128]{1,0:T(8,128)S(1)}, u32[]{:S(2)}, u32[]{:S(2)}) collective-permute-start(f32[285,128]{1,0:T(8,128)S(1)} %get-tuple-element.29), channel_id=1, source_target_pairs={{1,2},{2,1},{3,4},{4,3},{5,6},{6,5},{7,8},{8,7},{9,10},{10,9},{11,... | collective-permute-start | bytes 437768 | tf_op jit(solution)/shard_map/ppermute | solution.py:616
  8.9 1.4 %pack_classes.1 = (s32[12,64,128]{2,1,0:T(8,128)S(1)}, f32[8,128]{1,0:T(8,128)S(1)}) custom-call(s32[16,4,1440]{2,1,0:T(4,128)} %refs_0_.4, f32[32,72]{1,0:T(8,128)} %refs_1_.4, s32[4]{0:T(128)} %refs_2_.4), custom_call_target="tpu_custom_call" | custom-call | tf_op jit(solution)/shard_map/pack_classes/pallas_call | solution.py:653
  10.3 0.0 collective-permute-done.1.refs_4_.refs_0_
  10.3 0.0 collective-permute-done.2.refs_5_.refs_1_
  10.3 0.0 collective-permute-done.3.refs_6_.refs_2_
  10.4 0.0 collective-permute-done.4.refs_2_.refs_3_
  10.4 1.8 %forward.2 = (f32[2,144,256]{2,1,0:T(8,128)S(1)}, f32[7,224,128]{2,1,0:T(8,128)S(1)}) custom-call(f32[12,64,128]{2,1,0:T(8,128)S(1)} %get-tuple-element.26.refs_0_.own, f32[12,16,128]{2,1,0:T(8,128)S(1)} %get-tuple-element.27.refs_1_.own_maps, f32[399,128]{1,0:T(8,128)S(1)} %collective-permute-done.4.refs_2_.refs_3_, ...), custom_call_target="tpu_custom_call" | custom-call | flops 2307000064 | bytes 7380000 | tf_op jit(solution)/shard_map/forward/pallas_call | solution.py:676
  12.2 0.4 %collective-permute-done.refs_2_.refs_4_ = f32[285,128]{1,0:T(8,128)S(1)} collective-permute-done((f32[285,128]{1,0:T(8,128)S(1)}, f32[285,128]{1,0:T(8,128)S(1)}, u32[]{:S(2)}, u32[]{:S(2)}) %collective-permute-start) | collective-permute-done | bytes 145952 | tf_op jit(solution)/shard_map/ppermute | solution.py:616
  12.5 1.5 %forward.3 = (f32[2,128]{1,0:T(2,128)S(1)}, f32[5,224,128]{2,1,0:T(8,128)S(1)}, f32[8,128]{1,0:T(8,128)S(1)}) custom-call(f32[12,64,128]{2,1,0:T(8,128)S(1)} %get-tuple-element.26.refs_0_.own, f32[12,16,128]{2,1,0:T(8,128)S(1)} %get-tuple-element.27.refs_1_.own_maps, f32[285,128]{1,0:T(8,128)S(1)} %collective-permute-done.refs_2_.refs_4_, ...), custom_call_target="tpu_custom_call" | custom-call | flops 2307000064 | bytes 7380000 | tf_op jit(solution)/shard_map/forward/pallas_call | solution.py:676
  14.0 3.1 %collective-permute-start.9 = (f32[2,128]{1,0:T(2,128)S(1)}, f32[2,128]{1,0:T(2,128)S(1)}, u32[]{:S(2)}, u32[]{:S(2)}) collective-permute-start(f32[2,128]{1,0:T(2,128)S(1)} %get-tuple-element.41), channel_id=1, source_target_pairs={{0,8},{1,9},{2,10},{3,11},{4,12},{5,13},{6,14},{7,15},{8,0},{9,1},... | collective-permute-start | bytes 3080 | tf_op jit(solution)/shard_map/ppermute | solution.py:696
  17.1 1.3 %collective-permute-start.8 = (f32[2,128]{1,0:T(2,128)S(1)}, f32[2,128]{1,0:T(2,128)S(1)}, u32[]{:S(2)}, u32[]{:S(2)}) collective-permute-start(f32[2,128]{1,0:T(2,128)S(1)} %get-tuple-element.41), channel_id=1, source_target_pairs={{0,12},{1,13},{2,14},{3,15},{4,8},{5,9},{6,10},{7,11},{8,4},{9,5},... | collective-permute-start | bytes 3080 | tf_op jit(solution)/shard_map/ppermute | solution.py:696
  18.5 0.2 collective-permute-start.7
  18.7 1.6 %adjoint_part.1 = (f32[4,1440]{1,0:T(4,128)S(1)}, f32[4,1440]{1,0:T(4,128)S(1)}, f32[12,224,128]{2,1,0:T(8,128)S(1)}) custom-call(f32[12,64,128]{2,1,0:T(8,128)S(1)} %get-tuple-element.26.refs_0_.own, f32[12,16,128]{2,1,0:T(8,128)S(1)} %get-tuple-element.27.refs_1_.own_maps, s32[12,64,128]{2,1,0:T(8,128)S(1)} %get-tuple-element.28.refs_3_.classes, ...), custom_call_target="tpu_custom_call" | custom-call | tf_op jit(solution)/shard_map/adjoint_part/pallas_call | solution.py:699
  20.4 0.4 %collective-permute-start.5 = (f32[4,1440]{1,0:T(4,128)S(1)}, f32[4,1440]{1,0:T(4,128)S(1)}, u32[]{:S(2)}, u32[]{:S(2)}) collective-permute-start(f32[4,1440]{1,0:T(4,128)S(1)} %get-tuple-element.39), channel_id=1, source_target_pairs={{0,1},{1,0},{2,3},{3,2},{4,5},{5,4},{6,7},{7,6},{8,9},{9,8},{10,11... | collective-permute-start | bytes 69128 | tf_op jit(solution)/shard_map/ppermute | solution.py:613
  20.8 1.5 %collective-permute-start.6 = (f32[4,1440]{1,0:T(4,128)S(1)}, f32[4,1440]{1,0:T(4,128)S(1)}, u32[]{:S(2)}, u32[]{:S(2)}) collective-permute-start(f32[4,1440]{1,0:T(4,128)S(1)} %get-tuple-element.40), channel_id=1, source_target_pairs={{1,2},{2,1},{3,4},{4,3},{5,6},{6,5},{7,8},{8,7},{9,10},{10,9},{11,... | collective-permute-start | bytes 69128 | tf_op jit(solution)/shard_map/ppermute | solution.py:616
  22.3 0.0 collective-permute-done.9
  22.3 0.2 collective-permute-done.8
  22.5 1.1 %collective-permute-start.10 = (f32[8,128]{1,0:T(8,128)S(1)}, f32[8,128]{1,0:T(8,128)S(1)}, u32[]{:S(2)}, u32[]{:S(2)}) collective-permute-start(f32[8,128]{1,0:T(8,128)S(1)} %pad_maximum_fusion.refs_0_), channel_id=1, source_target_pairs={{0,3},{1,2},{2,1},{3,0},{4,7},{5,6},{6,5},{7,4},{8,11},{9,10},{10,... | collective-permute-start | bytes 12296 | tf_op jit(solution)/shard_map/ppermute | solution.py:696
  23.6 1.6 %collective-permute-start.11 = (f32[8,128]{1,0:T(8,128)S(1)}, f32[8,128]{1,0:T(8,128)S(1)}, u32[]{:S(2)}, u32[]{:S(2)}) collective-permute-start(f32[8,128]{1,0:T(8,128)S(1)} %pad_maximum_fusion.refs_0_), channel_id=1, source_target_pairs={{0,2},{1,3},{2,0},{3,1},{4,6},{5,7},{6,4},{7,5},{8,10},{9,11},{10,... | collective-permute-start | bytes 12296 | tf_op jit(solution)/shard_map/ppermute | solution.py:696
  25.2 0.0 collective-permute-start.12
  25.2 1.3 %own_part.1.own_share = f32[4,1440]{1,0:T(4,128)S(1)} custom-call(f32[12,64,128]{2,1,0:T(8,128)S(1)} %get-tuple-element.26.refs_0_.own, f32[12,16,128]{2,1,0:T(8,128)S(1)} %get-tuple-element.27.refs_1_.own_maps, f32[12,224,128]{2,1,0:T(8,128)S(1)} %get-tuple-element.38.kept, f32[228,128]{1,0:T(8,128)S(1)} %collective-permute-done.1.refs_4_.refs_0_, ...), custom_call_target="tpu_custom_call" | custom-call | tf_op jit(solution)/shard_map/own_part/pallas_call | solution.py:715
  26.5 0.0 collective-permute-done.10.refs_1_
  26.5 0.7 %collective-permute-done.11.refs_2_ = f32[8,128]{1,0:T(8,128)S(1)} collective-permute-done((f32[8,128]{1,0:T(8,128)S(1)}, f32[8,128]{1,0:T(8,128)S(1)}, u32[]{:S(2)}, u32[]{:S(2)}) %collective-permute-start.11) | collective-permute-done | bytes 4128 | tf_op jit(solution)/shard_map/ppermute | solution.py:696
  27.2 0.0 collective-permute-done.5.near_share
  27.2 0.0 collective-permute-done.6.far_share
  27.2 0.7 %finish.1 = (f32[2,72]{1,0:T(2,128)}, f32[4,1440]{1,0:T(4,128)}) custom-call(f32[4,1440]{1,0:T(4,128)S(1)} %own_part.1.own_share, f32[4,1440]{1,0:T(4,128)S(1)} %collective-permute-done.5.near_share, f32[4,1440]{1,0:T(4,128)S(1)} %collective-permute-done.6.far_share, f32[8,128]{1,0:T(8,128)S(1)} %pad_maximum_fusion.refs_0_, ...), custom_call_target="tpu_custom_call" | custom-call | tf_op jit(solution)/shard_map/finish/pallas_call | solution.py:724
  (3 shorter events, 0.0 us)
Async XLA Ops:
  1.9 8.4 %collective-permute-start.4 = (f32[399,128]{1,0:T(8,128)S(1)}, f32[399,128]{1,0:T(8,128)S(1)}, u32[]{:S(2)}, u32[]{:S(2)}) collective-permute-start(f32[399,128]{1,0:T(8,128)S(1)} %pack_first.1), channel_id=1, source_target_pairs={{1,2},{2,1},{3,4},{4,3},{5,6},{6,5},{7,8},{8,7},{9,10},{10,9},{11,... | collective-permute-start | bytes 612872 | tf_op jit(solution)/shard_map/ppermute | solution.py:616
  6.7 3.6 %collective-permute-start.1 = (f32[228,128]{1,0:T(8,128)S(1)}, f32[228,128]{1,0:T(8,128)S(1)}, u32[]{:S(2)}, u32[]{:S(2)}) collective-permute-start(f32[228,128]{1,0:T(8,128)S(1)} %get-tuple-element.30), channel_id=1, source_target_pairs={{0,1},{1,0},{2,3},{3,2},{4,5},{5,4},{6,7},{7,6},{8,9},{9,8},{10,11... | collective-permute-start | bytes 350216 | tf_op jit(solution)/shard_map/ppermute | solution.py:613
  6.9 3.4 %collective-permute-start.2 = (f32[228,128]{1,0:T(8,128)S(1)}, f32[228,128]{1,0:T(8,128)S(1)}, u32[]{:S(2)}, u32[]{:S(2)}) collective-permute-start(f32[228,128]{1,0:T(8,128)S(1)} %get-tuple-element.31), channel_id=1, source_target_pairs={{0,1},{1,0},{2,3},{3,2},{4,5},{5,4},{6,7},{7,6},{8,9},{9,8},{10,11... | collective-permute-start | bytes 350216 | tf_op jit(solution)/shard_map/ppermute | solution.py:613
  7.3 3.1 %collective-permute-start.3 = (f32[228,128]{1,0:T(8,128)S(1)}, f32[228,128]{1,0:T(8,128)S(1)}, u32[]{:S(2)}, u32[]{:S(2)}) collective-permute-start(f32[228,128]{1,0:T(8,128)S(1)} %get-tuple-element.32), channel_id=1, source_target_pairs={{0,1},{1,0},{2,3},{3,2},{4,5},{5,4},{6,7},{7,6},{8,9},{9,8},{10,11... | collective-permute-start | bytes 350216 | tf_op jit(solution)/shard_map/ppermute | solution.py:613
  7.4 5.1 %collective-permute-start = (f32[285,128]{1,0:T(8,128)S(1)}, f32[285,128]{1,0:T(8,128)S(1)}, u32[]{:S(2)}, u32[]{:S(2)}) collective-permute-start(f32[285,128]{1,0:T(8,128)S(1)} %get-tuple-element.29), channel_id=1, source_target_pairs={{1,2},{2,1},{3,4},{4,3},{5,6},{6,5},{7,8},{8,7},{9,10},{10,9},{11,... | collective-permute-start | bytes 437768 | tf_op jit(solution)/shard_map/ppermute | solution.py:616
  14.0 8.2 %collective-permute-start.9 = (f32[2,128]{1,0:T(2,128)S(1)}, f32[2,128]{1,0:T(2,128)S(1)}, u32[]{:S(2)}, u32[]{:S(2)}) collective-permute-start(f32[2,128]{1,0:T(2,128)S(1)} %get-tuple-element.41), channel_id=1, source_target_pairs={{0,8},{1,9},{2,10},{3,11},{4,12},{5,13},{6,14},{7,15},{8,0},{9,1},... | collective-permute-start | bytes 3080 | tf_op jit(solution)/shard_map/ppermute | solution.py:696
  17.1 5.4 %collective-permute-start.8 = (f32[2,128]{1,0:T(2,128)S(1)}, f32[2,128]{1,0:T(2,128)S(1)}, u32[]{:S(2)}, u32[]{:S(2)}) collective-permute-start(f32[2,128]{1,0:T(2,128)S(1)} %get-tuple-element.41), channel_id=1, source_target_pairs={{0,12},{1,13},{2,14},{3,15},{4,8},{5,9},{6,10},{7,11},{8,4},{9,5},... | collective-permute-start | bytes 3080 | tf_op jit(solution)/shard_map/ppermute | solution.py:696
  18.5 4.0 %collective-permute-start.7 = (f32[2,128]{1,0:T(2,128)S(1)}, f32[2,128]{1,0:T(2,128)S(1)}, u32[]{:S(2)}, u32[]{:S(2)}) collective-permute-start(f32[2,128]{1,0:T(2,128)S(1)} %get-tuple-element.41), channel_id=1, source_target_pairs={{0,4},{1,5},{2,6},{3,7},{4,0},{5,1},{6,2},{7,3},{8,12},{9,13},{10,... | collective-permute-start | bytes 3080 | tf_op jit(solution)/shard_map/ppermute | solution.py:696
  20.4 6.8 %collective-permute-start.5 = (f32[4,1440]{1,0:T(4,128)S(1)}, f32[4,1440]{1,0:T(4,128)S(1)}, u32[]{:S(2)}, u32[]{:S(2)}) collective-permute-start(f32[4,1440]{1,0:T(4,128)S(1)} %get-tuple-element.39), channel_id=1, source_target_pairs={{0,1},{1,0},{2,3},{3,2},{4,5},{5,4},{6,7},{7,6},{8,9},{9,8},{10,11... | collective-permute-start | bytes 69128 | tf_op jit(solution)/shard_map/ppermute | solution.py:613
  20.8 6.4 %collective-permute-start.6 = (f32[4,1440]{1,0:T(4,128)S(1)}, f32[4,1440]{1,0:T(4,128)S(1)}, u32[]{:S(2)}, u32[]{:S(2)}) collective-permute-start(f32[4,1440]{1,0:T(4,128)S(1)} %get-tuple-element.40), channel_id=1, source_target_pairs={{1,2},{2,1},{3,4},{4,3},{5,6},{6,5},{7,8},{8,7},{9,10},{10,9},{11,... | collective-permute-start | bytes 69128 | tf_op jit(solution)/shard_map/ppermute | solution.py:616
  22.5 4.0 %collective-permute-start.10 = (f32[8,128]{1,0:T(8,128)S(1)}, f32[8,128]{1,0:T(8,128)S(1)}, u32[]{:S(2)}, u32[]{:S(2)}) collective-permute-start(f32[8,128]{1,0:T(8,128)S(1)} %pad_maximum_fusion.refs_0_), channel_id=1, source_target_pairs={{0,3},{1,2},{2,1},{3,0},{4,7},{5,6},{6,5},{7,4},{8,11},{9,10},{10,... | collective-permute-start | bytes 12296 | tf_op jit(solution)/shard_map/ppermute | solution.py:696
  23.6 3.6 %collective-permute-start.11 = (f32[8,128]{1,0:T(8,128)S(1)}, f32[8,128]{1,0:T(8,128)S(1)}, u32[]{:S(2)}, u32[]{:S(2)}) collective-permute-start(f32[8,128]{1,0:T(8,128)S(1)} %pad_maximum_fusion.refs_0_), channel_id=1, source_target_pairs={{0,2},{1,3},{2,0},{3,1},{4,6},{5,7},{6,4},{7,5},{8,10},{9,11},{10,... | collective-permute-start | bytes 12296 | tf_op jit(solution)/shard_map/ppermute | solution.py:696
  25.2 2.0 %collective-permute-start.12 = (f32[8,128]{1,0:T(8,128)S(1)}, f32[8,128]{1,0:T(8,128)S(1)}, u32[]{:S(2)}, u32[]{:S(2)}) collective-permute-start(f32[8,128]{1,0:T(8,128)S(1)} %pad_maximum_fusion.refs_0_), channel_id=1, source_target_pairs={{0,1},{1,0},{2,3},{3,2},{4,5},{5,4},{6,7},{7,6},{8,9},{9,8},{10,11... | collective-permute-start | bytes 12296 | tf_op jit(solution)/shard_map/ppermute | solution.py:696

commit v9 on v8

--- a/solution.py
+++ b/solution.py
@@ -17,7 +17,7 @@
 LOW_COUNT = 8
 LOW_SHIFT = 3
 PIECES = (0, 7, 12)
-NEAR_PIECES = (0, 4, 8, 12)
+NEAR_PIECES = (0, 6, 12)
 VMEM_LIMIT = 16 * 1024 * 1024
 
 
@@ -293,7 +293,7 @@
     before = refs.pop(0) if piece > 0 else None
     scales = refs.pop(0) if last else None
     out, later = refs[:2]
-    weighted, maps, grams = refs[2:] if last else (None, refs[2], out)
+    weighted, maps = refs[2:] if last else (None, refs[2])
     levels = own.shape[1] // 4
     group = list(range(PIECES[piece], PIECES[piece + 1]))
     face_maps(own_maps, nears, {piece: far}, maps, group, levels)
@@ -326,6 +326,7 @@
                 for t in rows:
                     at = later_row(n + 1, t) * levels
                     later[u, at : at + levels, :] = fields[u][t]
+    finished = []
     for pair in range(2):
         lefts, rights = [], []
         for u, j in enumerate(group):
@@ -341,9 +342,13 @@
             (((1,), (1,)), ((), ())),
             preferred_element_type=jnp.float32,
         )
-        grams[pair] = gram if before is None else before[pair] + gram
+        gram = gram if before is None else before[pair] + gram
+        if last:
+            finished.append(gram)
+        else:
+            out[pair] = gram
     if last:
-        class_sums(grams, scales, out, weighted, levels)
+        class_sums(finished, scales, out, weighted, levels)
 
 
 def class_sums(grams, scales, sums, weighted, levels):
@@ -354,7 +359,7 @@
     sheets = []
     for pair in range(2):
         for h in range(HIGH_COUNT):
-            sheet = jnp.where(diagonal, grams[pair, h * levels : (h + 1) * levels, :], 0.0)
+            sheet = jnp.where(diagonal, grams[pair][h * levels : (h + 1) * levels, :], 0.0)
             sheets.append(jnp.sum(sheet, axis=0, keepdims=True))
         sheets.append(jnp.zeros((16 - HIGH_COUNT, width), jnp.float32))
     rest = jnp.concatenate(sheets, axis=0)
@@ -684,8 +689,7 @@
             in_specs=vmem(len(given)),
             out_specs=tuple(vmem(3 if last else 2)),
             cost_estimate=cost(2000),
-            scratch_shapes=[pltpu.VMEM((size, 16 * MAP_FIELDS, LANES), f32)]
-            + ([pltpu.VMEM(gram_shape, f32)] if last else []),
+            scratch_shapes=[pltpu.VMEM((size, 16 * MAP_FIELDS, LANES), f32)],
             compiler_params=params,
         )(*given)
         laters.append(later)

time: 28.1 us -> 28.1 us (level)
    ppermute x3, waiting for transfers between devices: 0.36 us -> 0.68 us  [to_far(): return lax.ppermute(x, ('members', 'lat'), far_pairs(members, count))]
    ppermute x4 -> x3, starting transfers between devices: 1.13 us -> 1.42 us  [to_near(): return lax.ppermute(x, 'lat', near_pairs(count))]
    ppermute x3, starting transfers between devices: 5.99 us -> 5.7 us  [to_far(): return lax.ppermute(x, ('members', 'lat'), far_pairs(members, count))]
  transfers between devices with their start and end apart: 13 -> 12, of which waited for: 3 -> 2; matrix products, arithmetic and copies ran while one was open for 0% -> 0% of each run, Pallas kernels for 28% -> 28%
where the time goes in v9:
time: 28.1 us; the launch traced here: 27.8 us
  starting transfers between devices  14.4 us (51%)
  Pallas kernels  11.3 us (40%)
  waiting for transfers between devices  1.35 us (5%)
  between operations  0.73 us (3%)
    ppermute x6, starting transfers between devices, body(): lax.ppermute(gathered, 'lat', [(d, d ^ k) for d in range(count)])  7.33 us
    ppermute x3, starting transfers between devices, to_far(): return lax.ppermute(x, ('members', 'lat'), far_pairs(members, count))  5.7 us
    pallas_call x2, Pallas kernels, body(): pl.pallas_call(functools.partial(forward, piece), name='forward', out_sha...  3.28 us
    pallas_call x1, Pallas kernels, body(): pl.pallas_call(pack_fields, name='pack_fields', out_shape=(jax.ShapeDtype...  1.73 us
    pallas_call x1, Pallas kernels, body(): pl.pallas_call(adjoint_part, name='adjoint_part', out_shape=(jax.ShapeDty...  1.63 us
    ppermute x3, starting transfers between devices, to_near(): return lax.ppermute(x, 'lat', near_pairs(count))  1.42 us
    pallas_call x1, Pallas kernels, body(): pl.pallas_call(pack_classes, name='pack_classes', out_shape=(jax.ShapeDty...  1.42 us
    pallas_call x1, Pallas kernels, body(): pl.pallas_call(pack_first, name='pack_first', out_shape=far_shapes[0], ou...  1.3 us
  transfers between devices with their start and end apart: 12, of which 2 were waited for; matrix products, arithmetic and copies ran while one was open for 0% of the time, Pallas kernels for 28%

profile of v9, /device:TPU:0, one launch (start us, length us, event | category | flops | bytes accessed | tf_op | source)
XLA Modules:
  0.0 27.8 jit_solution(14675889769842839630)
XLA Ops:
  0.6 1.3 %pack_first.1 = f32[399,128]{1,0:T(8,128)S(1)} custom-call(f32[16,4,1440]{2,1,0:T(4,128)} %refs_0_.3, f32[4,1440]{1,0:T(4,128)} %refs_1_.3, f32[4,1440]{1,0:T(4,128)} %refs_2_.3, s32[4,1440]{1,0:T(4,128)} %refs_3_.2), custom_call_target="tpu_custom_call" | custom-call | tf_op jit(solution)/shard_map/pack_first/pallas_call | solution.py:633
  1.9 3.0 %collective-permute-start.3 = (f32[399,128]{1,0:T(8,128)S(1)}, f32[399,128]{1,0:T(8,128)S(1)}, u32[]{:S(2)}, u32[]{:S(2)}) collective-permute-start(f32[399,128]{1,0:T(8,128)S(1)} %pack_first.1), channel_id=1, source_target_pairs={{1,2},{2,1},{3,4},{4,3},{5,6},{6,5},{7,8},{8,7},{9,10},{10,9},{11,... | collective-permute-start | bytes 612872 | tf_op jit(solution)/shard_map/ppermute | solution.py:621
  4.9 1.7 %pack_fields.1 = (f32[12,64,128]{2,1,0:T(8,128)S(1)}, f32[12,16,128]{2,1,0:T(8,128)S(1)}, f32[342,128]{1,0:T(8,128)S(1)}, f32[342,128]{1,0:T(8,128)S(1)}, f32[285,128]{1,0:T(8,128)S(1)}) custom-call(f32[16,4,1440]{2,1,0:T(4,128)} %refs_0_.3, f32[4,1440]{1,0:T(4,128)} %refs_1_.3, f32[4,1440]{1,0:T(4,128)} %refs_2_.3, s32[4,1440]{1,0:T(4,128)} %refs_3_.2), custom_call_target="tpu_custom_call" | custom-call | tf_op jit(solution)/shard_map/pack_fields/pallas_call | solution.py:643
  6.7 0.2 collective-permute-start.1
  6.9 0.4 %collective-permute-start.2 = (f32[342,128]{1,0:T(8,128)S(1)}, f32[342,128]{1,0:T(8,128)S(1)}, u32[]{:S(2)}, u32[]{:S(2)}) collective-permute-start(f32[342,128]{1,0:T(8,128)S(1)} %get-tuple-element.30), channel_id=1, source_target_pairs={{0,1},{1,0},{2,3},{3,2},{4,5},{5,4},{6,7},{7,6},{8,9},{9,8},{10,11... | collective-permute-start | bytes 525320 | tf_op jit(solution)/shard_map/ppermute | solution.py:618
  7.3 1.2 %collective-permute-start = (f32[285,128]{1,0:T(8,128)S(1)}, f32[285,128]{1,0:T(8,128)S(1)}, u32[]{:S(2)}, u32[]{:S(2)}) collective-permute-start(f32[285,128]{1,0:T(8,128)S(1)} %get-tuple-element.28), channel_id=1, source_target_pairs={{1,2},{2,1},{3,4},{4,3},{5,6},{6,5},{7,8},{8,7},{9,10},{10,9},{11,... | collective-permute-start | bytes 437768 | tf_op jit(solution)/shard_map/ppermute | solution.py:621
  8.5 1.4 %pack_classes.1 = (s32[12,64,128]{2,1,0:T(8,128)S(1)}, f32[8,128]{1,0:T(8,128)S(1)}) custom-call(s32[16,4,1440]{2,1,0:T(4,128)} %refs_0_.4, f32[32,72]{1,0:T(8,128)} %refs_1_.4, s32[4]{0:T(128)} %refs_2_.4), custom_call_target="tpu_custom_call" | custom-call | tf_op jit(solution)/shard_map/pack_classes/pallas_call | solution.py:658
  9.9 0.0 collective-permute-done.1.refs_4_.refs_0_
  9.9 0.0 collective-permute-done.2.refs_5_.refs_1_
  9.9 0.0 collective-permute-done.3.refs_2_
  9.9 1.8 %forward.2 = (f32[2,144,256]{2,1,0:T(8,128)S(1)}, f32[7,224,128]{2,1,0:T(8,128)S(1)}) custom-call(f32[12,64,128]{2,1,0:T(8,128)S(1)} %get-tuple-element.25.refs_0_.own, f32[12,16,128]{2,1,0:T(8,128)S(1)} %get-tuple-element.26.refs_1_.own_maps, f32[399,128]{1,0:T(8,128)S(1)} %collective-permute-done.3.refs_2_, ...), custom_call_target="tpu_custom_call" | custom-call | flops 2307000064 | bytes 7380000 | tf_op jit(solution)/shard_map/forward/pallas_call | solution.py:681
  11.7 0.7 %collective-permute-done.refs_2_.refs_3_ = f32[285,128]{1,0:T(8,128)S(1)} collective-permute-done((f32[285,128]{1,0:T(8,128)S(1)}, f32[285,128]{1,0:T(8,128)S(1)}, u32[]{:S(2)}, u32[]{:S(2)}) %collective-permute-start) | collective-permute-done | bytes 145952 | tf_op jit(solution)/shard_map/ppermute | solution.py:621
  12.4 1.5 %forward.3 = (f32[2,128]{1,0:T(2,128)S(1)}, f32[5,224,128]{2,1,0:T(8,128)S(1)}, f32[8,128]{1,0:T(8,128)S(1)}) custom-call(f32[12,64,128]{2,1,0:T(8,128)S(1)} %get-tuple-element.25.refs_0_.own, f32[12,16,128]{2,1,0:T(8,128)S(1)} %get-tuple-element.26.refs_1_.own_maps, f32[285,128]{1,0:T(8,128)S(1)} %collective-permute-done.refs_2_.refs_3_, ...), custom_call_target="tpu_custom_call" | custom-call | flops 2307000064 | bytes 7380000 | tf_op jit(solution)/shard_map/forward/pallas_call | solution.py:681
  13.9 2.8 %collective-permute-start.8 = (f32[2,128]{1,0:T(2,128)S(1)}, f32[2,128]{1,0:T(2,128)S(1)}, u32[]{:S(2)}, u32[]{:S(2)}) collective-permute-start(f32[2,128]{1,0:T(2,128)S(1)} %get-tuple-element.39), channel_id=1, source_target_pairs={{0,8},{1,9},{2,10},{3,11},{4,12},{5,13},{6,14},{7,15},{8,0},{9,1},... | collective-permute-start | bytes 3080 | tf_op jit(solution)/shard_map/ppermute | solution.py:700
  16.7 1.3 %collective-permute-start.7 = (f32[2,128]{1,0:T(2,128)S(1)}, f32[2,128]{1,0:T(2,128)S(1)}, u32[]{:S(2)}, u32[]{:S(2)}) collective-permute-start(f32[2,128]{1,0:T(2,128)S(1)} %get-tuple-element.39), channel_id=1, source_target_pairs={{0,12},{1,13},{2,14},{3,15},{4,8},{5,9},{6,10},{7,11},{8,4},{9,5},... | collective-permute-start | bytes 3080 | tf_op jit(solution)/shard_map/ppermute | solution.py:700
  18.0 0.2 collective-permute-start.6
  18.3 1.6 %adjoint_part.1 = (f32[4,1440]{1,0:T(4,128)S(1)}, f32[4,1440]{1,0:T(4,128)S(1)}, f32[12,224,128]{2,1,0:T(8,128)S(1)}) custom-call(f32[12,64,128]{2,1,0:T(8,128)S(1)} %get-tuple-element.25.refs_0_.own, f32[12,16,128]{2,1,0:T(8,128)S(1)} %get-tuple-element.26.refs_1_.own_maps, s32[12,64,128]{2,1,0:T(8,128)S(1)} %get-tuple-element.27.refs_3_.classes, ...), custom_call_target="tpu_custom_call" | custom-call | tf_op jit(solution)/shard_map/adjoint_part/pallas_call | solution.py:703
  19.9 0.8 %collective-permute-start.4 = (f32[4,1440]{1,0:T(4,128)S(1)}, f32[4,1440]{1,0:T(4,128)S(1)}, u32[]{:S(2)}, u32[]{:S(2)}) collective-permute-start(f32[4,1440]{1,0:T(4,128)S(1)} %get-tuple-element.37), channel_id=1, source_target_pairs={{0,1},{1,0},{2,3},{3,2},{4,5},{5,4},{6,7},{7,6},{8,9},{9,8},{10,11... | collective-permute-start | bytes 69128 | tf_op jit(solution)/shard_map/ppermute | solution.py:618
  20.7 1.5 %collective-permute-start.5 = (f32[4,1440]{1,0:T(4,128)S(1)}, f32[4,1440]{1,0:T(4,128)S(1)}, u32[]{:S(2)}, u32[]{:S(2)}) collective-permute-start(f32[4,1440]{1,0:T(4,128)S(1)} %get-tuple-element.38), channel_id=1, source_target_pairs={{1,2},{2,1},{3,4},{4,3},{5,6},{6,5},{7,8},{8,7},{9,10},{10,9},{11,... | collective-permute-start | bytes 69128 | tf_op jit(solution)/shard_map/ppermute | solution.py:621
  22.2 0.0 collective-permute-done.8
  22.2 0.0 collective-permute-done.7
  22.2 0.0 collective-permute-done.6
  22.3 1.3 %collective-permute-start.9 = (f32[8,128]{1,0:T(8,128)S(1)}, f32[8,128]{1,0:T(8,128)S(1)}, u32[]{:S(2)}, u32[]{:S(2)}) collective-permute-start(f32[8,128]{1,0:T(8,128)S(1)} %pad_maximum_fusion.refs_0_), channel_id=1, source_target_pairs={{0,3},{1,2},{2,1},{3,0},{4,7},{5,6},{6,5},{7,4},{8,11},{9,10},{10,... | collective-permute-start | bytes 12296 | tf_op jit(solution)/shard_map/ppermute | solution.py:700
  23.6 1.6 %collective-permute-start.10 = (f32[8,128]{1,0:T(8,128)S(1)}, f32[8,128]{1,0:T(8,128)S(1)}, u32[]{:S(2)}, u32[]{:S(2)}) collective-permute-start(f32[8,128]{1,0:T(8,128)S(1)} %pad_maximum_fusion.refs_0_), channel_id=1, source_target_pairs={{0,2},{1,3},{2,0},{3,1},{4,6},{5,7},{6,4},{7,5},{8,10},{9,11},{10,... | collective-permute-start | bytes 12296 | tf_op jit(solution)/shard_map/ppermute | solution.py:700
  25.2 0.0 collective-permute-start.11
  25.2 1.3 %own_part.1.own_share = f32[4,1440]{1,0:T(4,128)S(1)} custom-call(f32[12,64,128]{2,1,0:T(8,128)S(1)} %get-tuple-element.25.refs_0_.own, f32[12,16,128]{2,1,0:T(8,128)S(1)} %get-tuple-element.26.refs_1_.own_maps, f32[12,224,128]{2,1,0:T(8,128)S(1)} %get-tuple-element.36.kept, f32[342,128]{1,0:T(8,128)S(1)} %collective-permute-done.1.refs_4_.refs_0_, ...), custom_call_target="tpu_custom_call" | custom-call | tf_op jit(solution)/shard_map/own_part/pallas_call | solution.py:719
  26.5 0.0 collective-permute-done.9.refs_1_
  26.5 0.7 %collective-permute-done.10.refs_2_ = f32[8,128]{1,0:T(8,128)S(1)} collective-permute-done((f32[8,128]{1,0:T(8,128)S(1)}, f32[8,128]{1,0:T(8,128)S(1)}, u32[]{:S(2)}, u32[]{:S(2)}) %collective-permute-start.10) | collective-permute-done | bytes 4128 | tf_op jit(solution)/shard_map/ppermute | solution.py:700
  27.2 0.0 collective-permute-done.11.refs_3_
  27.2 0.0 collective-permute-done.4.near_share
  27.2 0.0 collective-permute-done.5.far_share
  27.2 0.6 %finish.1 = (f32[2,72]{1,0:T(2,128)}, f32[4,1440]{1,0:T(4,128)}) custom-call(f32[4,1440]{1,0:T(4,128)S(1)} %own_part.1.own_share, f32[4,1440]{1,0:T(4,128)S(1)} %collective-permute-done.4.near_share, f32[4,1440]{1,0:T(4,128)S(1)} %collective-permute-done.5.far_share, f32[8,128]{1,0:T(8,128)S(1)} %pad_maximum_fusion.refs_0_, ...), custom_call_target="tpu_custom_call" | custom-call | tf_op jit(solution)/shard_map/finish/pallas_call | solution.py:728
  (1 shorter events, 0.0 us)
Async XLA Ops:
  1.9 8.0 %collective-permute-start.3 = (f32[399,128]{1,0:T(8,128)S(1)}, f32[399,128]{1,0:T(8,128)S(1)}, u32[]{:S(2)}, u32[]{:S(2)}) collective-permute-start(f32[399,128]{1,0:T(8,128)S(1)} %pack_first.1), channel_id=1, source_target_pairs={{1,2},{2,1},{3,4},{4,3},{5,6},{6,5},{7,8},{8,7},{9,10},{10,9},{11,... | collective-permute-start | bytes 612872 | tf_op jit(solution)/shard_map/ppermute | solution.py:621
  6.7 3.2 %collective-permute-start.1 = (f32[342,128]{1,0:T(8,128)S(1)}, f32[342,128]{1,0:T(8,128)S(1)}, u32[]{:S(2)}, u32[]{:S(2)}) collective-permute-start(f32[342,128]{1,0:T(8,128)S(1)} %get-tuple-element.29), channel_id=1, source_target_pairs={{0,1},{1,0},{2,3},{3,2},{4,5},{5,4},{6,7},{7,6},{8,9},{9,8},{10,11... | collective-permute-start | bytes 525320 | tf_op jit(solution)/shard_map/ppermute | solution.py:618
  6.9 3.0 %collective-permute-start.2 = (f32[342,128]{1,0:T(8,128)S(1)}, f32[342,128]{1,0:T(8,128)S(1)}, u32[]{:S(2)}, u32[]{:S(2)}) collective-permute-start(f32[342,128]{1,0:T(8,128)S(1)} %get-tuple-element.30), channel_id=1, source_target_pairs={{0,1},{1,0},{2,3},{3,2},{4,5},{5,4},{6,7},{7,6},{8,9},{9,8},{10,11... | collective-permute-start | bytes 525320 | tf_op jit(solution)/shard_map/ppermute | solution.py:618
  7.3 5.1 %collective-permute-start = (f32[285,128]{1,0:T(8,128)S(1)}, f32[285,128]{1,0:T(8,128)S(1)}, u32[]{:S(2)}, u32[]{:S(2)}) collective-permute-start(f32[285,128]{1,0:T(8,128)S(1)} %get-tuple-element.28), channel_id=1, source_target_pairs={{1,2},{2,1},{3,4},{4,3},{5,6},{6,5},{7,8},{8,7},{9,10},{10,9},{11,... | collective-permute-start | bytes 437768 | tf_op jit(solution)/shard_map/ppermute | solution.py:621
  13.9 8.4 %collective-permute-start.8 = (f32[2,128]{1,0:T(2,128)S(1)}, f32[2,128]{1,0:T(2,128)S(1)}, u32[]{:S(2)}, u32[]{:S(2)}) collective-permute-start(f32[2,128]{1,0:T(2,128)S(1)} %get-tuple-element.39), channel_id=1, source_target_pairs={{0,8},{1,9},{2,10},{3,11},{4,12},{5,13},{6,14},{7,15},{8,0},{9,1},... | collective-permute-start | bytes 3080 | tf_op jit(solution)/shard_map/ppermute | solution.py:700
  16.7 5.6 %collective-permute-start.7 = (f32[2,128]{1,0:T(2,128)S(1)}, f32[2,128]{1,0:T(2,128)S(1)}, u32[]{:S(2)}, u32[]{:S(2)}) collective-permute-start(f32[2,128]{1,0:T(2,128)S(1)} %get-tuple-element.39), channel_id=1, source_target_pairs={{0,12},{1,13},{2,14},{3,15},{4,8},{5,9},{6,10},{7,11},{8,4},{9,5},... | collective-permute-start | bytes 3080 | tf_op jit(solution)/shard_map/ppermute | solution.py:700
  18.0 4.2 %collective-permute-start.6 = (f32[2,128]{1,0:T(2,128)S(1)}, f32[2,128]{1,0:T(2,128)S(1)}, u32[]{:S(2)}, u32[]{:S(2)}) collective-permute-start(f32[2,128]{1,0:T(2,128)S(1)} %get-tuple-element.39), channel_id=1, source_target_pairs={{0,4},{1,5},{2,6},{3,7},{4,0},{5,1},{6,2},{7,3},{8,12},{9,13},{10,... | collective-permute-start | bytes 3080 | tf_op jit(solution)/shard_map/ppermute | solution.py:700
  19.9 7.3 %collective-permute-start.4 = (f32[4,1440]{1,0:T(4,128)S(1)}, f32[4,1440]{1,0:T(4,128)S(1)}, u32[]{:S(2)}, u32[]{:S(2)}) collective-permute-start(f32[4,1440]{1,0:T(4,128)S(1)} %get-tuple-element.37), channel_id=1, source_target_pairs={{0,1},{1,0},{2,3},{3,2},{4,5},{5,4},{6,7},{7,6},{8,9},{9,8},{10,11... | collective-permute-start | bytes 69128 | tf_op jit(solution)/shard_map/ppermute | solution.py:618
  20.7 6.4 %collective-permute-start.5 = (f32[4,1440]{1,0:T(4,128)S(1)}, f32[4,1440]{1,0:T(4,128)S(1)}, u32[]{:S(2)}, u32[]{:S(2)}) collective-permute-start(f32[4,1440]{1,0:T(4,128)S(1)} %get-tuple-element.38), channel_id=1, source_target_pairs={{1,2},{2,1},{3,4},{4,3},{5,6},{6,5},{7,8},{8,7},{9,10},{10,9},{11,... | collective-permute-start | bytes 69128 | tf_op jit(solution)/shard_map/ppermute | solution.py:621
  22.3 4.2 %collective-permute-start.9 = (f32[8,128]{1,0:T(8,128)S(1)}, f32[8,128]{1,0:T(8,128)S(1)}, u32[]{:S(2)}, u32[]{:S(2)}) collective-permute-start(f32[8,128]{1,0:T(8,128)S(1)} %pad_maximum_fusion.refs_0_), channel_id=1, source_target_pairs={{0,3},{1,2},{2,1},{3,0},{4,7},{5,6},{6,5},{7,4},{8,11},{9,10},{10,... | collective-permute-start | bytes 12296 | tf_op jit(solution)/shard_map/ppermute | solution.py:700
  23.6 3.6 %collective-permute-start.10 = (f32[8,128]{1,0:T(8,128)S(1)}, f32[8,128]{1,0:T(8,128)S(1)}, u32[]{:S(2)}, u32[]{:S(2)}) collective-permute-start(f32[8,128]{1,0:T(8,128)S(1)} %pad_maximum_fusion.refs_0_), channel_id=1, source_target_pairs={{0,2},{1,3},{2,0},{3,1},{4,6},{5,7},{6,4},{7,5},{8,10},{9,11},{10,... | collective-permute-start | bytes 12296 | tf_op jit(solution)/shard_map/ppermute | solution.py:700
  25.2 2.0 %collective-permute-start.11 = (f32[8,128]{1,0:T(8,128)S(1)}, f32[8,128]{1,0:T(8,128)S(1)}, u32[]{:S(2)}, u32[]{:S(2)}) collective-permute-start(f32[8,128]{1,0:T(8,128)S(1)} %pad_maximum_fusion.refs_0_), channel_id=1, source_target_pairs={{0,1},{1,0},{2,3},{3,2},{4,5},{5,4},{6,7},{7,6},{8,9},{9,8},{10,11... | collective-permute-start | bytes 12296 | tf_op jit(solution)/shard_map/ppermute | solution.py:700

commit v10 on v9

--- a/solution.py
+++ b/solution.py
@@ -592,7 +592,7 @@
     groups = []
     for bit in range(bits - 2, -1, -2):
         one, two = 1 << bit, 2 << bit
-        groups.append([one, one + two, two] if bit > 0 else [3, 2, 1])
+        groups.append([one, two, one + two] if bit > 0 else [3, 2, 1])
     return groups + ([[1]] if bits % 2 else [])
 
 

time: 28.1 us -> 27.9 us (level)
  no operation moved by 1% of the time
where the time goes in v10:
time: 27.9 us; the launch traced here: 27.8 us
  starting transfers between devices  14.3 us (51%)
  Pallas kernels  11.3 us (41%)
  waiting for transfers between devices  1.44 us (5%)
  between operations  0.73 us (3%)
    ppermute x6, starting transfers between devices, body(): lax.ppermute(gathered, 'lat', [(d, d ^ k) for d in range(count)])  7.18 us
    ppermute x3, starting transfers between devices, to_far(): return lax.ppermute(x, ('members', 'lat'), far_pairs(members, count))  5.7 us
    pallas_call x2, Pallas kernels, body(): pl.pallas_call(functools.partial(forward, piece), name='forward', out_sha...  3.28 us
    pallas_call x1, Pallas kernels, body(): pl.pallas_call(pack_fields, name='pack_fields', out_shape=(jax.ShapeDtype...  1.73 us
    pallas_call x1, Pallas kernels, body(): pl.pallas_call(adjoint_part, name='adjoint_part', out_shape=(jax.ShapeDty...  1.63 us
    ppermute x3, starting transfers between devices, to_near(): return lax.ppermute(x, 'lat', near_pairs(count))  1.42 us
    pallas_call x1, Pallas kernels, body(): pl.pallas_call(pack_classes, name='pack_classes', out_shape=(jax.ShapeDty...  1.42 us
    pallas_call x1, Pallas kernels, body(): pl.pallas_call(pack_first, name='pack_first', out_shape=far_shapes[0], ou...  1.3 us
  transfers between devices with their start and end apart: 12, of which 2 were waited for; matrix products, arithmetic and copies ran while one was open for 0% of the time, Pallas kernels for 28%

profile of v10, /device:TPU:0, one launch (start us, length us, event | category | flops | bytes accessed | tf_op | source)
XLA Modules:
  0.0 27.8 jit_solution(9415730327085830436)
XLA Ops:
  0.6 1.3 %pack_first.1 = f32[399,128]{1,0:T(8,128)S(1)} custom-call(f32[16,4,1440]{2,1,0:T(4,128)} %refs_0_.3, f32[4,1440]{1,0:T(4,128)} %refs_1_.3, f32[4,1440]{1,0:T(4,128)} %refs_2_.3, s32[4,1440]{1,0:T(4,128)} %refs_3_.2), custom_call_target="tpu_custom_call" | custom-call | tf_op jit(solution)/shard_map/pack_first/pallas_call | solution.py:633
  1.9 3.0 %collective-permute-start.3 = (f32[399,128]{1,0:T(8,128)S(1)}, f32[399,128]{1,0:T(8,128)S(1)}, u32[]{:S(2)}, u32[]{:S(2)}) collective-permute-start(f32[399,128]{1,0:T(8,128)S(1)} %pack_first.1), channel_id=1, source_target_pairs={{1,2},{2,1},{3,4},{4,3},{5,6},{6,5},{7,8},{8,7},{9,10},{10,9},{11,... | collective-permute-start | bytes 612872 | tf_op jit(solution)/shard_map/ppermute | solution.py:621
  4.9 1.7 %pack_fields.1 = (f32[12,64,128]{2,1,0:T(8,128)S(1)}, f32[12,16,128]{2,1,0:T(8,128)S(1)}, f32[342,128]{1,0:T(8,128)S(1)}, f32[342,128]{1,0:T(8,128)S(1)}, f32[285,128]{1,0:T(8,128)S(1)}) custom-call(f32[16,4,1440]{2,1,0:T(4,128)} %refs_0_.3, f32[4,1440]{1,0:T(4,128)} %refs_1_.3, f32[4,1440]{1,0:T(4,128)} %refs_2_.3, s32[4,1440]{1,0:T(4,128)} %refs_3_.2), custom_call_target="tpu_custom_call" | custom-call | tf_op jit(solution)/shard_map/pack_fields/pallas_call | solution.py:643
  6.7 0.2 collective-permute-start.1
  6.9 0.4 %collective-permute-start.2 = (f32[342,128]{1,0:T(8,128)S(1)}, f32[342,128]{1,0:T(8,128)S(1)}, u32[]{:S(2)}, u32[]{:S(2)}) collective-permute-start(f32[342,128]{1,0:T(8,128)S(1)} %get-tuple-element.30), channel_id=1, source_target_pairs={{0,1},{1,0},{2,3},{3,2},{4,5},{5,4},{6,7},{7,6},{8,9},{9,8},{10,11... | collective-permute-start | bytes 525320 | tf_op jit(solution)/shard_map/ppermute | solution.py:618
  7.3 1.2 %collective-permute-start = (f32[285,128]{1,0:T(8,128)S(1)}, f32[285,128]{1,0:T(8,128)S(1)}, u32[]{:S(2)}, u32[]{:S(2)}) collective-permute-start(f32[285,128]{1,0:T(8,128)S(1)} %get-tuple-element.28), channel_id=1, source_target_pairs={{1,2},{2,1},{3,4},{4,3},{5,6},{6,5},{7,8},{8,7},{9,10},{10,9},{11,... | collective-permute-start | bytes 437768 | tf_op jit(solution)/shard_map/ppermute | solution.py:621
  8.5 1.4 %pack_classes.1 = (s32[12,64,128]{2,1,0:T(8,128)S(1)}, f32[8,128]{1,0:T(8,128)S(1)}) custom-call(s32[16,4,1440]{2,1,0:T(4,128)} %refs_0_.4, f32[32,72]{1,0:T(8,128)} %refs_1_.4, s32[4]{0:T(128)} %refs_2_.4), custom_call_target="tpu_custom_call" | custom-call | tf_op jit(solution)/shard_map/pack_classes/pallas_call | solution.py:658
  9.9 0.0 collective-permute-done.1.refs_4_.refs_0_
  9.9 0.0 collective-permute-done.2.refs_5_.refs_1_
  9.9 0.0 collective-permute-done.3.refs_2_
  9.9 1.8 %forward.2 = (f32[2,144,256]{2,1,0:T(8,128)S(1)}, f32[7,224,128]{2,1,0:T(8,128)S(1)}) custom-call(f32[12,64,128]{2,1,0:T(8,128)S(1)} %get-tuple-element.25.refs_0_.own, f32[12,16,128]{2,1,0:T(8,128)S(1)} %get-tuple-element.26.refs_1_.own_maps, f32[399,128]{1,0:T(8,128)S(1)} %collective-permute-done.3.refs_2_, ...), custom_call_target="tpu_custom_call" | custom-call | flops 2307000064 | bytes 7380000 | tf_op jit(solution)/shard_map/forward/pallas_call | solution.py:681
  11.7 0.7 %collective-permute-done.refs_2_.refs_3_ = f32[285,128]{1,0:T(8,128)S(1)} collective-permute-done((f32[285,128]{1,0:T(8,128)S(1)}, f32[285,128]{1,0:T(8,128)S(1)}, u32[]{:S(2)}, u32[]{:S(2)}) %collective-permute-start) | collective-permute-done | bytes 145952 | tf_op jit(solution)/shard_map/ppermute | solution.py:621
  12.4 1.5 %forward.3 = (f32[2,128]{1,0:T(2,128)S(1)}, f32[5,224,128]{2,1,0:T(8,128)S(1)}, f32[8,128]{1,0:T(8,128)S(1)}) custom-call(f32[12,64,128]{2,1,0:T(8,128)S(1)} %get-tuple-element.25.refs_0_.own, f32[12,16,128]{2,1,0:T(8,128)S(1)} %get-tuple-element.26.refs_1_.own_maps, f32[285,128]{1,0:T(8,128)S(1)} %collective-permute-done.refs_2_.refs_3_, ...), custom_call_target="tpu_custom_call" | custom-call | flops 2307000064 | bytes 7380000 | tf_op jit(solution)/shard_map/forward/pallas_call | solution.py:681
  13.9 3.8 %collective-permute-start.8 = (f32[2,128]{1,0:T(2,128)S(1)}, f32[2,128]{1,0:T(2,128)S(1)}, u32[]{:S(2)}, u32[]{:S(2)}) collective-permute-start(f32[2,128]{1,0:T(2,128)S(1)} %get-tuple-element.39), channel_id=1, source_target_pairs={{0,12},{1,13},{2,14},{3,15},{4,8},{5,9},{6,10},{7,11},{8,4},{9,5},... | collective-permute-start | bytes 3080 | tf_op jit(solution)/shard_map/ppermute | solution.py:700
  17.7 0.0 collective-permute-start.7
  17.7 0.6 %collective-permute-start.6 = (f32[2,128]{1,0:T(2,128)S(1)}, f32[2,128]{1,0:T(2,128)S(1)}, u32[]{:S(2)}, u32[]{:S(2)}) collective-permute-start(f32[2,128]{1,0:T(2,128)S(1)} %get-tuple-element.39), channel_id=1, source_target_pairs={{0,4},{1,5},{2,6},{3,7},{4,0},{5,1},{6,2},{7,3},{8,12},{9,13},{10,... | collective-permute-start | bytes 3080 | tf_op jit(solution)/shard_map/ppermute | solution.py:700
  18.3 1.6 %adjoint_part.1 = (f32[4,1440]{1,0:T(4,128)S(1)}, f32[4,1440]{1,0:T(4,128)S(1)}, f32[12,224,128]{2,1,0:T(8,128)S(1)}) custom-call(f32[12,64,128]{2,1,0:T(8,128)S(1)} %get-tuple-element.25.refs_0_.own, f32[12,16,128]{2,1,0:T(8,128)S(1)} %get-tuple-element.26.refs_1_.own_maps, s32[12,64,128]{2,1,0:T(8,128)S(1)} %get-tuple-element.27.refs_3_.classes, ...), custom_call_target="tpu_custom_call" | custom-call | tf_op jit(solution)/shard_map/adjoint_part/pallas_call | solution.py:703
  20.0 0.8 %collective-permute-start.4 = (f32[4,1440]{1,0:T(4,128)S(1)}, f32[4,1440]{1,0:T(4,128)S(1)}, u32[]{:S(2)}, u32[]{:S(2)}) collective-permute-start(f32[4,1440]{1,0:T(4,128)S(1)} %get-tuple-element.37), channel_id=1, source_target_pairs={{0,1},{1,0},{2,3},{3,2},{4,5},{5,4},{6,7},{7,6},{8,9},{9,8},{10,11... | collective-permute-start | bytes 69128 | tf_op jit(solution)/shard_map/ppermute | solution.py:618
  20.8 1.5 %collective-permute-start.5 = (f32[4,1440]{1,0:T(4,128)S(1)}, f32[4,1440]{1,0:T(4,128)S(1)}, u32[]{:S(2)}, u32[]{:S(2)}) collective-permute-start(f32[4,1440]{1,0:T(4,128)S(1)} %get-tuple-element.38), channel_id=1, source_target_pairs={{1,2},{2,1},{3,4},{4,3},{5,6},{6,5},{7,8},{8,7},{9,10},{10,9},{11,... | collective-permute-start | bytes 69128 | tf_op jit(solution)/shard_map/ppermute | solution.py:621
  22.3 0.0 collective-permute-done.8
  22.3 0.0 collective-permute-done.7
  22.3 0.0 collective-permute-done.6
  22.3 1.1 %collective-permute-start.9 = (f32[8,128]{1,0:T(8,128)S(1)}, f32[8,128]{1,0:T(8,128)S(1)}, u32[]{:S(2)}, u32[]{:S(2)}) collective-permute-start(f32[8,128]{1,0:T(8,128)S(1)} %pad_maximum_fusion.refs_0_), channel_id=1, source_target_pairs={{0,3},{1,2},{2,1},{3,0},{4,7},{5,6},{6,5},{7,4},{8,11},{9,10},{10,... | collective-permute-start | bytes 12296 | tf_op jit(solution)/shard_map/ppermute | solution.py:700
  23.5 1.6 %collective-permute-start.10 = (f32[8,128]{1,0:T(8,128)S(1)}, f32[8,128]{1,0:T(8,128)S(1)}, u32[]{:S(2)}, u32[]{:S(2)}) collective-permute-start(f32[8,128]{1,0:T(8,128)S(1)} %pad_maximum_fusion.refs_0_), channel_id=1, source_target_pairs={{0,2},{1,3},{2,0},{3,1},{4,6},{5,7},{6,4},{7,5},{8,10},{9,11},{10,... | collective-permute-start | bytes 12296 | tf_op jit(solution)/shard_map/ppermute | solution.py:700
  25.1 0.0 collective-permute-start.11
  25.1 1.3 %own_part.1.own_share = f32[4,1440]{1,0:T(4,128)S(1)} custom-call(f32[12,64,128]{2,1,0:T(8,128)S(1)} %get-tuple-element.25.refs_0_.own, f32[12,16,128]{2,1,0:T(8,128)S(1)} %get-tuple-element.26.refs_1_.own_maps, f32[12,224,128]{2,1,0:T(8,128)S(1)} %get-tuple-element.36.kept, f32[342,128]{1,0:T(8,128)S(1)} %collective-permute-done.1.refs_4_.refs_0_, ...), custom_call_target="tpu_custom_call" | custom-call | tf_op jit(solution)/shard_map/own_part/pallas_call | solution.py:719
  26.4 0.0 collective-permute-done.9.refs_1_
  26.4 0.7 %collective-permute-done.10.refs_2_ = f32[8,128]{1,0:T(8,128)S(1)} collective-permute-done((f32[8,128]{1,0:T(8,128)S(1)}, f32[8,128]{1,0:T(8,128)S(1)}, u32[]{:S(2)}, u32[]{:S(2)}) %collective-permute-start.10) | collective-permute-done | bytes 4128 | tf_op jit(solution)/shard_map/ppermute | solution.py:700
  27.1 0.0 collective-permute-done.11.refs_3_
  27.1 0.0 collective-permute-done.4.near_share
  27.1 0.0 collective-permute-done.5.far_share
  27.1 0.6 %finish.1 = (f32[2,72]{1,0:T(2,128)}, f32[4,1440]{1,0:T(4,128)}) custom-call(f32[4,1440]{1,0:T(4,128)S(1)} %own_part.1.own_share, f32[4,1440]{1,0:T(4,128)S(1)} %collective-permute-done.4.near_share, f32[4,1440]{1,0:T(4,128)S(1)} %collective-permute-done.5.far_share, f32[8,128]{1,0:T(8,128)S(1)} %pad_maximum_fusion.refs_0_, ...), custom_call_target="tpu_custom_call" | custom-call | tf_op jit(solution)/shard_map/finish/pallas_call | solution.py:728
  (1 shorter events, 0.0 us)
Async XLA Ops:
  1.9 8.0 %collective-permute-start.3 = (f32[399,128]{1,0:T(8,128)S(1)}, f32[399,128]{1,0:T(8,128)S(1)}, u32[]{:S(2)}, u32[]{:S(2)}) collective-permute-start(f32[399,128]{1,0:T(8,128)S(1)} %pack_first.1), channel_id=1, source_target_pairs={{1,2},{2,1},{3,4},{4,3},{5,6},{6,5},{7,8},{8,7},{9,10},{10,9},{11,... | collective-permute-start | bytes 612872 | tf_op jit(solution)/shard_map/ppermute | solution.py:621
  6.7 3.2 %collective-permute-start.1 = (f32[342,128]{1,0:T(8,128)S(1)}, f32[342,128]{1,0:T(8,128)S(1)}, u32[]{:S(2)}, u32[]{:S(2)}) collective-permute-start(f32[342,128]{1,0:T(8,128)S(1)} %get-tuple-element.29), channel_id=1, source_target_pairs={{0,1},{1,0},{2,3},{3,2},{4,5},{5,4},{6,7},{7,6},{8,9},{9,8},{10,11... | collective-permute-start | bytes 525320 | tf_op jit(solution)/shard_map/ppermute | solution.py:618
  6.9 3.0 %collective-permute-start.2 = (f32[342,128]{1,0:T(8,128)S(1)}, f32[342,128]{1,0:T(8,128)S(1)}, u32[]{:S(2)}, u32[]{:S(2)}) collective-permute-start(f32[342,128]{1,0:T(8,128)S(1)} %get-tuple-element.30), channel_id=1, source_target_pairs={{0,1},{1,0},{2,3},{3,2},{4,5},{5,4},{6,7},{7,6},{8,9},{9,8},{10,11... | collective-permute-start | bytes 525320 | tf_op jit(solution)/shard_map/ppermute | solution.py:618
  7.3 5.1 %collective-permute-start = (f32[285,128]{1,0:T(8,128)S(1)}, f32[285,128]{1,0:T(8,128)S(1)}, u32[]{:S(2)}, u32[]{:S(2)}) collective-permute-start(f32[285,128]{1,0:T(8,128)S(1)} %get-tuple-element.28), channel_id=1, source_target_pairs={{1,2},{2,1},{3,4},{4,3},{5,6},{6,5},{7,8},{8,7},{9,10},{10,9},{11,... | collective-permute-start | bytes 437768 | tf_op jit(solution)/shard_map/ppermute | solution.py:621
  13.9 8.4 %collective-permute-start.8 = (f32[2,128]{1,0:T(2,128)S(1)}, f32[2,128]{1,0:T(2,128)S(1)}, u32[]{:S(2)}, u32[]{:S(2)}) collective-permute-start(f32[2,128]{1,0:T(2,128)S(1)} %get-tuple-element.39), channel_id=1, source_target_pairs={{0,12},{1,13},{2,14},{3,15},{4,8},{5,9},{6,10},{7,11},{8,4},{9,5},... | collective-permute-start | bytes 3080 | tf_op jit(solution)/shard_map/ppermute | solution.py:700
  17.7 4.6 %collective-permute-start.7 = (f32[2,128]{1,0:T(2,128)S(1)}, f32[2,128]{1,0:T(2,128)S(1)}, u32[]{:S(2)}, u32[]{:S(2)}) collective-permute-start(f32[2,128]{1,0:T(2,128)S(1)} %get-tuple-element.39), channel_id=1, source_target_pairs={{0,8},{1,9},{2,10},{3,11},{4,12},{5,13},{6,14},{7,15},{8,0},{9,1},... | collective-permute-start | bytes 3080 | tf_op jit(solution)/shard_map/ppermute | solution.py:700
  17.7 4.6 %collective-permute-start.6 = (f32[2,128]{1,0:T(2,128)S(1)}, f32[2,128]{1,0:T(2,128)S(1)}, u32[]{:S(2)}, u32[]{:S(2)}) collective-permute-start(f32[2,128]{1,0:T(2,128)S(1)} %get-tuple-element.39), channel_id=1, source_target_pairs={{0,4},{1,5},{2,6},{3,7},{4,0},{5,1},{6,2},{7,3},{8,12},{9,13},{10,... | collective-permute-start | bytes 3080 | tf_op jit(solution)/shard_map/ppermute | solution.py:700
  20.0 7.1 %collective-permute-start.4 = (f32[4,1440]{1,0:T(4,128)S(1)}, f32[4,1440]{1,0:T(4,128)S(1)}, u32[]{:S(2)}, u32[]{:S(2)}) collective-permute-start(f32[4,1440]{1,0:T(4,128)S(1)} %get-tuple-element.37), channel_id=1, source_target_pairs={{0,1},{1,0},{2,3},{3,2},{4,5},{5,4},{6,7},{7,6},{8,9},{9,8},{10,11... | collective-permute-start | bytes 69128 | tf_op jit(solution)/shard_map/ppermute | solution.py:618
  20.8 6.3 %collective-permute-start.5 = (f32[4,1440]{1,0:T(4,128)S(1)}, f32[4,1440]{1,0:T(4,128)S(1)}, u32[]{:S(2)}, u32[]{:S(2)}) collective-permute-start(f32[4,1440]{1,0:T(4,128)S(1)} %get-tuple-element.38), channel_id=1, source_target_pairs={{1,2},{2,1},{3,4},{4,3},{5,6},{6,5},{7,8},{8,7},{9,10},{10,9},{11,... | collective-permute-start | bytes 69128 | tf_op jit(solution)/shard_map/ppermute | solution.py:621
  22.3 4.0 %collective-permute-start.9 = (f32[8,128]{1,0:T(8,128)S(1)}, f32[8,128]{1,0:T(8,128)S(1)}, u32[]{:S(2)}, u32[]{:S(2)}) collective-permute-start(f32[8,128]{1,0:T(8,128)S(1)} %pad_maximum_fusion.refs_0_), channel_id=1, source_target_pairs={{0,3},{1,2},{2,1},{3,0},{4,7},{5,6},{6,5},{7,4},{8,11},{9,10},{10,... | collective-permute-start | bytes 12296 | tf_op jit(solution)/shard_map/ppermute | solution.py:700
  23.5 3.6 %collective-permute-start.10 = (f32[8,128]{1,0:T(8,128)S(1)}, f32[8,128]{1,0:T(8,128)S(1)}, u32[]{:S(2)}, u32[]{:S(2)}) collective-permute-start(f32[8,128]{1,0:T(8,128)S(1)} %pad_maximum_fusion.refs_0_), channel_id=1, source_target_pairs={{0,2},{1,3},{2,0},{3,1},{4,6},{5,7},{6,4},{7,5},{8,10},{9,11},{10,... | collective-permute-start | bytes 12296 | tf_op jit(solution)/shard_map/ppermute | solution.py:700
  25.1 2.0 %collective-permute-start.11 = (f32[8,128]{1,0:T(8,128)S(1)}, f32[8,128]{1,0:T(8,128)S(1)}, u32[]{:S(2)}, u32[]{:S(2)}) collective-permute-start(f32[8,128]{1,0:T(8,128)S(1)} %pad_maximum_fusion.refs_0_), channel_id=1, source_target_pairs={{0,1},{1,0},{2,3},{3,2},{4,5},{5,4},{6,7},{7,6},{8,9},{9,8},{10,11... | collective-permute-start | bytes 12296 | tf_op jit(solution)/shard_map/ppermute | solution.py:700
